TPU v7x, 512 devices: a whole 4x4x16 slice. The times are simulated.
512 devices in a mesh: row: 32 (over y, x, z_hi), col: 16 (over z_lo, core).
Axes of the slice: x: 4, y: 4, z: 16 (z_hi: 2, z_lo: 8; z = z_hi * 8 + z_lo), core: 2. Of those that a mesh axis runs over, the one named last changes fastest.
Arguments:
- object_slices: float32 [2, 2, 4096, 2048], P(None, None, 'row', 'col'), may hold values from -4 to 4
- probe_wave: bfloat16 [2, 256, 256], replicated, may hold values from -4 to 4
- propagator_phase: bfloat16 [256, 256], replicated, may hold values from -3.140625 to 3.140625
- intensity: bfloat16 [32, 16, 2, 256, 256], P('row', 'col'), may hold values from 0.099609375 to 3
- centres: int32 [32, 16, 2, 2], P('row', 'col'), may hold values from 0 to 4095, as said below
- batch_order: int32 [32, 16, 2], P('row', 'col'), may hold values from -1 to 510, as said below
Outputs:
- object_gradient: float32 [2, 2, 4096, 2048], P(None, None, 'row', 'col')
- probe_gradient: float32 [2, 256, 256], P(None, 'row', 'col')
Inputs may be any that keep to these rules, and one draw needn't show every extreme that they name: `centres`: slot c of tile (g, h) holds (row, column) pixel coordinates in the whole object that lie in that tile: rows g * 128 to (g + 1) * 128 - 1, columns h * 128 to (h + 1) * 128 - 1; empty slots hold a point of their tile too. `batch_order`: -1 marks an empty slot; the live slots of a tile come first and are numbered 0, 1, 2, ... in batch order, tile after tile in row-major order of tiles; some tile has all 2 slots live and some tile has none.
All inputs are finite; a program needn't handle non-finite values.
Results may differ from a plain program's by a relative error of at most 0.0003.
Values sent between devices are 32-bit elements; how exact they have to be, the bound alone decides.
No kernel may reach another device: no remote copies, remote signals or barrier semaphores. Data moves between devices by JAX's collectives and lax.ppermute only.
A program may use at most 64 MiB of HBM per device.

v0:
```python
import math

import jax
import jax.numpy as jnp
from jax import lax
from jax.sharding import PartitionSpec as P

PRECISE = lax.Precision.HIGHEST


def with_halo(value, sides, width):
    for axis, dim in sides:
        devices, length = (lax.axis_size(axis), value.shape[dim])
        up = [(i, (i + 1) % devices) for i in range(devices - 1)]
        down = [(j, i) for i, j in up]
        last = lax.slice_in_dim(value, length - width, length, axis=dim)
        leading = lax.slice_in_dim(value, 0, width, axis=dim)
        before = lax.ppermute(last, axis, up)
        after = lax.ppermute(leading, axis, down)
        value = jnp.concatenate([before, value, after], axis=dim)
    return value


def product(left, right):
    return (left[0] * right[0] - left[1] * right[1], left[0] * right[1] + left[1] * right[0])


def conjugate(values):
    return (values[0], -values[1])


def block_table(width, orient):
    first_index = jnp.arange(width, dtype=jnp.int32)[:, None]
    second_index = jnp.arange(width, dtype=jnp.int32)[None, :]
    angles = (first_index * second_index % width).astype(jnp.float32) * (2.0 * math.pi / width)
    factor = 1.0 / math.sqrt(width)
    cosine = jnp.cos(angles) * factor
    sine = orient * jnp.sin(angles) * factor
    real_out = jnp.stack([cosine, -sine])
    imag_out = jnp.stack([sine, cosine])
    return jnp.stack([real_out, imag_out], axis=2)


def transform(values, orient):
    width = values[0].shape[1]
    table = block_table(width, orient)
    stacked = jnp.stack([values[0], values[1]], axis=1)
    once = jnp.einsum("bcaw,cadk->bdkw", stacked, table, precision=PRECISE)
    twice = jnp.einsum("bckw,cwdj->bdkj", once, table, precision=PRECISE)
    return (twice[:, 0], twice[:, 1])


def fold_joint(gradient, half_win):
    received = with_halo(gradient, (("row", 2), ("col", 3)), half_win)
    middle = gradient[:, :, half_win:-half_win, half_win:-half_win]
    inner_rows, inner_cols = (middle.shape[2], middle.shape[3])
    border = 2 * half_win
    middle = middle.at[:, :, :half_win, :].add(
        received[:, :, :half_win, border : border + inner_cols]
    )
    middle = middle.at[:, :, -half_win:, :].add(
        received[:, :, -half_win:, border : border + inner_cols]
    )
    middle = middle.at[:, :, :, :half_win].add(
        received[:, :, border : border + inner_rows, :half_win]
    )
    middle = middle.at[:, :, :, -half_win:].add(
        received[:, :, border : border + inner_rows, -half_win:]
    )
    middle = middle.at[:, :, :half_win, :half_win].add(received[:, :, :half_win, :half_win])
    middle = middle.at[:, :, :half_win, -half_win:].add(received[:, :, :half_win, -half_win:])
    middle = middle.at[:, :, -half_win:, :half_win].add(received[:, :, -half_win:, :half_win])
    middle = middle.at[:, :, -half_win:, -half_win:].add(received[:, :, -half_win:, -half_win:])
    return middle


def per_device(object_slices, probe_wave, propagator_phase, intensity, centres, batch_order):
    slices = object_slices.shape[0]
    tile_rows = object_slices.shape[2]
    tile_cols = object_slices.shape[3]
    width = probe_wave.shape[1]
    half_win = width // 2
    slot_count = centres.shape[2]
    extended = with_halo(object_slices, (("row", 2), ("col", 3)), half_win)
    start_rows = centres[0, 0, :, 0] - lax.axis_index("row") * tile_rows
    start_cols = centres[0, 0, :, 1] - lax.axis_index("col") * tile_cols
    weights = (batch_order[0, 0] >= 0).astype(jnp.float32)[:, None, None]
    zero_index = jnp.zeros((), jnp.int32)

    def cut_window(row_start, col_start):
        return lax.dynamic_slice(
            extended, (zero_index, zero_index, row_start, col_start), (slices, 2, width, width)
        )

    windows = jax.vmap(cut_window)(start_rows, start_cols)
    field_shape = (slot_count, width, width)
    wave_field = (
        jnp.broadcast_to(probe_wave[0].astype(jnp.float32), field_shape),
        jnp.broadcast_to(probe_wave[1].astype(jnp.float32), field_shape),
    )
    angles = propagator_phase.astype(jnp.float32)
    propagator = (jnp.cos(angles)[None], jnp.sin(angles)[None])
    entering = []
    for slice_index in range(slices):
        entering.append(wave_field)
        layer = (windows[:, slice_index, 0], windows[:, slice_index, 1])
        spectrum = transform(product(wave_field, layer), -1.0)
        if slice_index + 1 < slices:
            wave_field = transform(product(spectrum, propagator), 1.0)
    measured = intensity[0, 0].astype(jnp.float32)
    misfit = weights * (spectrum[0] * spectrum[0] + spectrum[1] * spectrum[1] - measured)
    adjoint = transform((misfit * spectrum[0], misfit * spectrum[1]), 1.0)
    object_terms = [None] * slices
    for slice_index in reversed(range(slices)):
        layer = (windows[:, slice_index, 0], windows[:, slice_index, 1])
        object_terms[slice_index] = product(conjugate(entering[slice_index]), adjoint)
        upstream = product(conjugate(layer), adjoint)
        if slice_index > 0:
            adjoint = transform(product(transform(upstream, -1.0), conjugate(propagator)), 1.0)
    stacked = jnp.stack([jnp.stack(term_pair, axis=1) for term_pair in object_terms], axis=1)
    accumulated = jnp.zeros(extended.shape, jnp.float32)
    for slot_index in range(slot_count):
        anchor = (zero_index, zero_index, start_rows[slot_index], start_cols[slot_index])
        current = lax.dynamic_slice(accumulated, anchor, stacked.shape[1:])
        accumulated = lax.dynamic_update_slice(accumulated, current + stacked[slot_index], anchor)
    object_gradient = fold_joint(accumulated, half_win)
    row_count = lax.axis_size("row")
    col_count = lax.axis_size("col")
    block_rows = width // row_count
    block_cols = width // col_count
    probe_term = jnp.stack([jnp.sum(upstream[0], axis=0), jnp.sum(upstream[1], axis=0)])
    probe_term = probe_term.reshape(2, row_count, block_rows, col_count, block_cols)
    probe_term = probe_term.transpose(0, 1, 3, 2, 4).reshape(
        2, row_count * col_count, block_rows * block_cols
    )
    probe_share = lax.psum_scatter(probe_term, ("row", "col"), scatter_dimension=1, tiled=True)
    probe_gradient = probe_share.reshape(2, block_rows, block_cols)
    return (object_gradient, probe_gradient)


def solution(mesh):
    placed = (
        P(None, None, "row", "col"),
        P(),
        P(),
        P("row", "col", None, None, None),
        P("row", "col", None, None),
        P("row", "col", None),
    )
    return jax.shard_map(
        per_device,
        mesh=mesh,
        in_specs=placed,
        out_specs=(P(None, None, "row", "col"), P(None, "row", "col")),
        check_vma=False,
    )
```

profile of v0, /device:TPU:1, one launch (start us, length us, event | category | flops | bytes accessed | tf_op | source)
XLA Modules:
  0.0 788.5 jit_solution(7473621586727764595)
XLA Ops:
  7.2 16.4 %collective-permute-start = (f32[2,2,128,128]{3,2,1,0:T(8,128)}, f32[2,2,128,128]{3,2,1,0:T(8,128)S(1)}, u32[]{:S(2)}, u32[]{:S(2)}) collective-permute-start(f32[2,2,128,128]{3,2,1,0:T(8,128)} %param.38), channel_id=1, source_target_pairs={{0,16},{16,32},{32,48},{48,64},{64,80},{80,96},{96,112},{112,128},... | collective-permute-start | bytes 786440 | tf_op jit(solution)/shard_map/ppermute | solution.py:18
  43.4 10.8 %collective-permute-done.1 = f32[2,2,128,128]{3,2,1,0:T(8,128)S(1)} collective-permute-done((f32[2,2,128,128]{3,2,1,0:T(8,128)}, f32[2,2,128,128]{3,2,1,0:T(8,128)S(1)}, u32[]{:S(2)}, u32[]{:S(2)}) %collective-permute-start.1) | collective-permute-done | bytes 262176 | tf_op jit(solution)/shard_map/ppermute | solution.py:19
  54.2 18.9 %collective-permute-start.2 = (f32[2,2,384,128]{3,2,1,0:T(8,128)S(1)}, f32[2,2,384,128]{3,2,1,0:T(8,128)S(1)}, u32[]{:S(2)}, u32[]{:S(2)}) collective-permute-start(f32[2,2,384,128]{3,2,1,0:T(8,128)S(1)} %constant_dynamic-update-slice_fusion), channel_id=1, source_target_pairs={{0,1},{1,2},{2,3},{3,4},{4,5},{5,6},{6,7},{7,8},{8,9},{9,10},{10,1... | collective-permute-start | bytes 2359304 | tf_op jit(solution)/shard_map/ppermute | solution.py:18
  73.1 1.9 collective-permute-start.3
  77.3 4.8 collective-permute-done.2
  82.0 4.4 collective-permute-done.3
  88.0 9.6 %while.17 = (s32[]{:T(128)}, f32[2,2,384,384]{3,2,1,0:T(8,128)}, s32[2,4]{1,0:T(2,128)S(1)}, f32[2,2,2,256,256]{4,3,0,2,1:T(8,128)}, s32[]{:T(128)}) while((s32[]{:T(128)}, f32[2,2,384,384]{3,2,1,0:T(8,128)}, s32[2,4]{1,0:T(2,128)S(1)}, f32[2,2,2,256,256]{4,3,0,2,1:T(8,128)}, s32[]{:T(128)}) %tuple.109), condition=%wide.while_cond.8, body=%wide.while_body.8.sunk | while | flops 2 | bytes 2098801 | solution.py:91
  88.7 4.0 bitcast_dynamic-update-slice_fusion.2
  93.3 4.1 bitcast_dynamic-update-slice_fusion.2
  100.8 1.9 convolution_bitcast_fusion.10
  102.8 1.9 convolution_bitcast_fusion.9
  104.7 1.9 convolution_bitcast_fusion.8
  110.6 2.1 convolution_bitcast_fusion.5
  112.7 1.9 convolution_bitcast_fusion.4
  116.7 1.9 convolution_bitcast_fusion.2
  118.7 1.9 convolution_bitcast_fusion.1
  120.6 1.9 convolution_bitcast_fusion
  125.3 14.9 %dynamic_update_slice.6 = f32[2,2,384,384]{3,2,1,0:T(8,128)S(1)} dynamic-update-slice(f32[2,2,384,384]{3,2,1,0:T(8,128)S(1)} %broadcast_in_dim.8, f32[2,2,256,256]{3,2,1,0:T(8,128)} %fusion.1, s32[]{:T(128)} %constant.298.clone.1, s32[]{:T(128)} %constant.298.clone.1, s32[]{:T(128)S(6)} %select_n.91, s32[]{:T(128)S(6)} %select_n.92) | dynamic-update-slice | bytes 2097156 | tf_op jit(solution)/shard_map/dynamic_update_slice | solution.py:125
  140.3 2.4 fusion.3
  142.6 14.5 %dynamic_update_slice.7 = f32[2,2,384,384]{3,2,1,0:T(8,128)S(1)} dynamic-update-slice(f32[2,2,384,384]{3,2,1,0:T(8,128)S(1)} %dynamic_update_slice.6, f32[2,2,256,256]{3,2,1,0:T(8,128)} %fusion.3, s32[]{:T(128)} %constant.298.clone.1, s32[]{:T(128)} %constant.298.clone.1, s32[]{:T(128)S(6)} %select_n.93, s32[]{:T(128)S(6)} %select_n.94) | dynamic-update-slice | bytes 2097156 | tf_op jit(solution)/shard_map/dynamic_update_slice | solution.py:125
  157.2 11.0 %collective-permute-start.4 = (f32[2,2,128,384]{3,2,1,0:T(8,128)S(1)}, f32[2,2,128,384]{3,2,1,0:T(8,128)S(1)}, u32[]{:S(2)}, u32[]{:S(2)}) collective-permute-start(f32[2,2,128,384]{3,2,1,0:T(8,128)S(1)} %get-tuple-element.194), channel_id=1, source_target_pairs={{0,16},{16,32},{32,48},{48,64},{64,80},{80,96},{96,112},{112,128},... | collective-permute-start | bytes 2359304 | tf_op jit(solution)/shard_map/ppermute | solution.py:18
  169.8 12.6 %collective-permute-done.4 = f32[2,2,128,384]{3,2,1,0:T(8,128)S(1)} collective-permute-done((f32[2,2,128,384]{3,2,1,0:T(8,128)S(1)}, f32[2,2,128,384]{3,2,1,0:T(8,128)S(1)}, u32[]{:S(2)}, u32[]{:S(2)}) %collective-permute-start.4) | collective-permute-done | bytes 786464 | tf_op jit(solution)/shard_map/ppermute | solution.py:18
  182.4 62.5 %collective-permute-done.5 = f32[2,2,128,384]{3,2,1,0:T(8,128)S(1)} collective-permute-done((f32[2,2,128,384]{3,2,1,0:T(8,128)S(1)}, f32[2,2,128,384]{3,2,1,0:T(8,128)S(1)}, u32[]{:S(2)}, u32[]{:S(2)}) %collective-permute-start.5) | collective-permute-done | bytes 786464 | tf_op jit(solution)/shard_map/ppermute | solution.py:19
  246.7 58.5 %collective-permute-start.6 = (f32[2,2,640,128]{3,2,1,0:T(8,128)}, f32[2,2,640,128]{3,2,1,0:T(8,128)}, u32[]{:S(2)}, u32[]{:S(2)}) collective-permute-start(f32[2,2,640,128]{3,2,1,0:T(8,128)} %get-tuple-element.186), channel_id=1, source_target_pairs={{0,1},{1,2},{2,3},{3,4},{4,5},{5,6},{6,7},{7,8},{8,9},{9,10},{10,1... | collective-permute-start | bytes 3932168 | tf_op jit(solution)/shard_map/ppermute | solution.py:18
  305.2 1.9 collective-permute-start.7
  308.0 2.8 stack.69
  310.8 2.0 stack.70
  312.8 2.6 maximum_bitcast_fusion
  315.3 3.7 copy.99
  319.0 4.3 reshape.626
  323.3 454.3 %all-reduce.3.cloned.1.call-done = f32[2,512,128]{2,0,1:T(2,128)} async-done(((f32[2,512,128]{2,0,1:T(2,128)}), f32[2,512,128]{2,0,1:T(2,128)}) %all-reduce.3.cloned.1.call-update) | async-done | bytes 524304
  779.0 2.3 slice_add_fusion
  (78 shorter events, 35.3 us)
Async XLA Ops:
  7.2 33.3 %copy-start.9 = (bf16[1,1,2,256,256]{4,3,2,1,0:T(8,128)(2,1)S(1)}, bf16[1,1,2,256,256]{4,3,2,1,0:T(8,128)(2,1)}, u32[]{:S(2)}) copy-start(bf16[1,1,2,256,256]{4,3,2,1,0:T(8,128)(2,1)} %param.41) | copy-start | bytes 786436
  7.2 770.5 %all-reduce.3.cloned.1.call-start = ((), (), s32[]{:S(2)}) async-start(), calls=%async_computation | async-start | bytes 1048576
  7.2 36.1 %collective-permute-start = (f32[2,2,128,128]{3,2,1,0:T(8,128)}, f32[2,2,128,128]{3,2,1,0:T(8,128)S(1)}, u32[]{:S(2)}, u32[]{:S(2)}) collective-permute-start(f32[2,2,128,128]{3,2,1,0:T(8,128)} %param.38), channel_id=1, source_target_pairs={{0,16},{16,32},{32,48},{48,64},{64,80},{80,96},{96,112},{112,128},... | collective-permute-start | bytes 786440 | tf_op jit(solution)/shard_map/ppermute | solution.py:18
  23.6 30.5 %collective-permute-start.1 = (f32[2,2,128,128]{3,2,1,0:T(8,128)}, f32[2,2,128,128]{3,2,1,0:T(8,128)S(1)}, u32[]{:S(2)}, u32[]{:S(2)}) collective-permute-start(f32[2,2,128,128]{3,2,1,0:T(8,128)} %param.38), channel_id=1, source_target_pairs={{16,0},{32,16},{48,32},{64,48},{80,64},{96,80},{112,96},{128,112},... | collective-permute-start | bytes 786440 | tf_op jit(solution)/shard_map/ppermute | solution.py:19
  26.7 16.6 %copy-start.10 = (f32[2,2,128,128]{3,2,1,0:T(8,128)S(1)}, f32[2,2,128,128]{3,2,1,0:T(8,128)}, u32[]{:S(2)}) copy-start(f32[2,2,128,128]{3,2,1,0:T(8,128)} %param.38) | copy-start | bytes 786436
  43.4 33.1 %copy-start.8 = (bf16[2,256,256]{2,1,0:T(8,128)(2,1)S(1)}, bf16[2,256,256]{2,1,0:T(8,128)(2,1)}, u32[]{:S(2)}) copy-start(bf16[2,256,256]{2,1,0:T(8,128)(2,1)} %param.39) | copy-start | bytes 786436
  54.2 27.8 %collective-permute-start.2 = (f32[2,2,384,128]{3,2,1,0:T(8,128)S(1)}, f32[2,2,384,128]{3,2,1,0:T(8,128)S(1)}, u32[]{:S(2)}, u32[]{:S(2)}) collective-permute-start(f32[2,2,384,128]{3,2,1,0:T(8,128)S(1)} %constant_dynamic-update-slice_fusion), channel_id=1, source_target_pairs={{0,1},{1,2},{2,3},{3,4},{4,5},{5,6},{6,7},{7,8},{8,9},{9,10},{10,1... | collective-permute-start | bytes 2359304 | tf_op jit(solution)/shard_map/ppermute | solution.py:18
  73.1 13.3 %collective-permute-start.3 = (f32[2,2,384,128]{3,2,1,0:T(8,128)S(1)}, f32[2,2,384,128]{3,2,1,0:T(8,128)S(1)}, u32[]{:S(2)}, u32[]{:S(2)}) collective-permute-start(f32[2,2,384,128]{3,2,1,0:T(8,128)S(1)} %constant_dynamic-update-slice_fusion), channel_id=1, source_target_pairs={{1,0},{2,1},{3,2},{4,3},{5,4},{6,5},{7,6},{8,7},{9,8},{10,9},{11,1... | collective-permute-start | bytes 2359304 | tf_op jit(solution)/shard_map/ppermute | solution.py:19
  100.8 1.9 copy-start.7
  104.6 1.9 copy-start.3
  120.6 2.0 copy-start.6
  122.5 1.0 copy-start.1
  123.8 1.4 copy-start
  157.2 25.2 %collective-permute-start.4 = (f32[2,2,128,384]{3,2,1,0:T(8,128)S(1)}, f32[2,2,128,384]{3,2,1,0:T(8,128)S(1)}, u32[]{:S(2)}, u32[]{:S(2)}) collective-permute-start(f32[2,2,128,384]{3,2,1,0:T(8,128)S(1)} %get-tuple-element.194), channel_id=1, source_target_pairs={{0,16},{16,32},{32,48},{48,64},{64,80},{80,96},{96,112},{112,128},... | collective-permute-start | bytes 2359304 | tf_op jit(solution)/shard_map/ppermute | solution.py:18
  168.2 138.8 %copy-start.2 = (f32[2,2,256,256]{3,2,0,1:T(8,128)S(1)}, f32[2,2,256,256]{3,2,0,1:T(8,128)}, u32[]{:S(2)}) copy-start(f32[2,2,256,256]{3,2,0,1:T(8,128)} %copy-done.1) | copy-start | bytes 3145732
  168.3 138.8 %copy-start.4 = (f32[2,2,2,256,256]{4,3,0,2,1:T(8,128)S(1)}, f32[2,2,2,256,256]{4,3,0,2,1:T(8,128)}, u32[]{:S(2)}) copy-start(f32[2,2,2,256,256]{4,3,0,2,1:T(8,128)} %get-tuple-element.169) | copy-start | bytes 6291460
  168.3 76.6 %collective-permute-start.5 = (f32[2,2,128,384]{3,2,1,0:T(8,128)S(1)}, f32[2,2,128,384]{3,2,1,0:T(8,128)S(1)}, u32[]{:S(2)}, u32[]{:S(2)}) collective-permute-start(f32[2,2,128,384]{3,2,1,0:T(8,128)S(1)} %get-tuple-element.195), channel_id=1, source_target_pairs={{16,0},{32,16},{48,32},{64,48},{80,64},{96,80},{112,96},{128,112},... | collective-permute-start | bytes 2359304 | tf_op jit(solution)/shard_map/ppermute | solution.py:19
  244.9 1.8 copy-start.5
  246.7 532.3 %collective-permute-start.6 = (f32[2,2,640,128]{3,2,1,0:T(8,128)}, f32[2,2,640,128]{3,2,1,0:T(8,128)}, u32[]{:S(2)}, u32[]{:S(2)}) collective-permute-start(f32[2,2,640,128]{3,2,1,0:T(8,128)} %get-tuple-element.186), channel_id=1, source_target_pairs={{0,1},{1,2},{2,3},{3,4},{4,5},{5,6},{6,7},{7,8},{8,9},{9,10},{10,1... | collective-permute-start | bytes 3932168 | tf_op jit(solution)/shard_map/ppermute | solution.py:18
  305.2 473.8 %collective-permute-start.7 = (f32[2,2,640,128]{3,2,1,0:T(8,128)}, f32[2,2,640,128]{3,2,1,0:T(8,128)}, u32[]{:S(2)}, u32[]{:S(2)}) collective-permute-start(f32[2,2,640,128]{3,2,1,0:T(8,128)} %get-tuple-element.187), channel_id=1, source_target_pairs={{1,0},{2,1},{3,2},{4,3},{5,4},{6,5},{7,6},{8,7},{9,8},{10,9},{11,1... | collective-permute-start | bytes 3932168 | tf_op jit(solution)/shard_map/ppermute | solution.py:19
Sparse Core Ops, SparseCore 0:
  323.4 454.1 all-reduce.2
where the time goes:
time: 795 us; the launch traced here: 789 us
  waiting for transfers between devices  549 us (69%)
  starting transfers between devices  112 us (14%)
  local copies, waits for them, and re-layouts  56.3 us (7%)
  other arithmetic  26.2 us (3%)
  matrix products  22.5 us (3%)
  between operations  22.5 us (3%)
    unnamed x2, waiting for transfers between devices  454 us
    ppermute x4, starting transfers between devices, with_halo(): before = lax.ppermute(last, axis, up)  105 us
    ppermute x4, waiting for transfers between devices, with_halo(): after = lax.ppermute(leading, axis, down)  77.7 us
    dynamic_update_slice x2, local copies, waits for them, and re-layouts, per_device(): lax.dynamic_update_slice(accumulated, current + stacked[slot_index], anchor)  29.4 us
    ppermute x4, waiting for transfers between devices, with_halo(): before = lax.ppermute(last, axis, up)  17.3 us
  transfers between devices with their start and end apart: 9, of which 6 were waited for; matrix products, arithmetic and copies ran while one was open for 4% of the time, Pallas kernels for 0%

commit v1 on v0

v1 whole, which is shorter than its diff:
```python
import math

import jax
import jax.numpy as jnp
import numpy as np
from jax import lax
from jax.experimental import pallas as pl
from jax.experimental.pallas import tpu as pltpu
from jax.sharding import PartitionSpec as P

WIN = 256
HALF = 128
F32 = jnp.float32
BF16 = jnp.bfloat16


def frequency_order():
    return np.concatenate([np.arange(0, WIN, 2), np.arange(1, WIN, 2)])


def order_matrix():
    matrix = np.zeros((WIN, WIN), np.float32)
    matrix[np.arange(WIN), frequency_order()] = 1.0
    return jnp.asarray(matrix, BF16)


def half_tables():
    spots = np.arange(HALF)
    tables = []
    for parity in range(2):
        angles = 2.0 * math.pi * (np.outer(spots, 2 * spots + parity) % WIN) / WIN
        cosine, sine = (np.cos(angles) / 16.0, np.sin(angles) / 16.0)
        block = np.block([[cosine, -sine], [sine, cosine]])
        tables += [block, block.T]
    exact = np.stack(tables).astype(np.float32)
    high = exact.astype(jnp.bfloat16)
    low = (exact - high.astype(np.float32)).astype(jnp.bfloat16)
    return jnp.asarray(np.stack([high, low], axis=1))


def split(value):
    high = value.astype(BF16)
    return high, (value - high.astype(F32)).astype(BF16)


def dot(left, right):
    return jnp.dot(left, right, preferred_element_type=F32)


def right_mul(value, table_ref, index):
    high, low = split(value)
    table = table_ref[index, 0]
    return dot(high, table) + (dot(low, table) + dot(high, table_ref[index, 1]))


def left_mul(table_ref, index, value):
    high, low = split(value)
    table = table_ref[index, 0]
    return dot(table, high) + (dot(table, low) + dot(table_ref[index, 1], high))


def join(first, second, axis):
    return jnp.concatenate([first, second], axis=axis)


def halves(value, axis):
    if axis == 0:
        return value[:HALF], value[HALF:]
    return value[:, :HALF], value[:, HALF:]


def forward_axis(field, tables, axis):
    (re0, re1), (im0, im1) = (halves(field[0], axis), halves(field[1], axis))
    even = join(re0 + re1, im0 + im1, axis)
    odd = join(re0 - re1, im0 - im1, axis)
    if axis == 1:
        even, odd = (right_mul(even, tables, 0), right_mul(odd, tables, 2))
    else:
        even, odd = (left_mul(tables, 1, even), left_mul(tables, 3, odd))
    (re0, im0), (re1, im1) = (halves(even, axis), halves(odd, axis))
    return (join(re0, re1, axis), join(im0, im1, axis))


def inverse_axis(field, tables, axis):
    (re0, re1), (im0, im1) = (halves(field[0], axis), halves(field[1], axis))
    even = join(re0, im0, axis)
    odd = join(re1, im1, axis)
    if axis == 1:
        even, odd = (right_mul(even, tables, 1), right_mul(odd, tables, 3))
    else:
        even, odd = (left_mul(tables, 0, even), left_mul(tables, 2, odd))
    (re0, im0), (re1, im1) = (halves(even, axis), halves(odd, axis))
    return (join(re0 + re1, re0 - re1, axis), join(im0 + im1, im0 - im1, axis))


def forward(field, tables):
    return forward_axis(forward_axis(field, tables, 1), tables, 0)


def inverse(field, tables):
    return inverse_axis(inverse_axis(field, tables, 0), tables, 1)


def times(left, right):
    return (left[0] * right[0] - left[1] * right[1], left[0] * right[1] + left[1] * right[0])


def conj_times(left, right):
    return (left[0] * right[0] + left[1] * right[1], left[0] * right[1] - left[1] * right[0])


def cut_lanes(strip, shift):
    turned = [pltpu.roll(strip[:, k * HALF:(k + 1) * HALF], (HALF - shift) & (HALF - 1), 1) for k in range(3)]
    kept = lax.broadcasted_iota(jnp.int32, turned[0].shape, 1) < HALF - shift
    return jnp.concatenate([jnp.where(kept, turned[k], turned[k + 1]) for k in range(2)], axis=1)


def put_lanes(value, shift):
    turned = [pltpu.roll(value[:, k * HALF:(k + 1) * HALF], shift, 1) for k in range(2)]
    kept = lax.broadcasted_iota(jnp.int32, turned[0].shape, 1) >= shift
    return jnp.concatenate(
        [jnp.where(kept, turned[0], 0.0), jnp.where(kept, turned[1], turned[0]), jnp.where(kept, 0.0, turned[1])],
        axis=1,
    )


def cut_rows(strip, shift):
    groups = pltpu.roll(strip.reshape(WIN // 8 + 1, 8, strip.shape[1]), (8 - shift) & 7, 1)
    kept = lax.broadcasted_iota(jnp.int32, (WIN // 8, 8, strip.shape[1]), 1) < 8 - shift
    return jnp.where(kept, groups[:-1], groups[1:]).reshape(WIN, strip.shape[1])


def put_rows(value, shift):
    groups = pltpu.roll(value.reshape(WIN // 8, 8, value.shape[1]), shift, 1)
    none = jnp.zeros((1, 8, value.shape[1]), F32)
    kept = lax.broadcasted_iota(jnp.int32, (WIN // 8 + 1, 8, value.shape[1]), 1) >= shift
    here = jnp.concatenate([groups, none], axis=0)
    before = jnp.concatenate([none, groups], axis=0)
    return jnp.where(kept, here, before).reshape(WIN + 8, value.shape[1])


def work_kernel(place, weight, own, own_l, own_r, near, near_l, near_r, far, far_l, far_r,
                probe, propagator, intensity, tables, out_own, out_own_l, out_own_r, out_near,
                out_near_l, out_near_r, out_far, out_far_l, out_far_r, out_probe, extended, total):
    near_top = pl.multiple_of(place[4], HALF)
    far_top = pl.multiple_of(place[5], HALF)
    groups_in = ((far_top, (far_l, far, far_r)), (near_top, (near_l, near, near_r)), (HALF, (own_l, own, own_r)))
    for top, trio in groups_in:
        for k in range(3):
            for layer in range(2):
                for part in range(2):
                    extended[2 * layer + part, pl.ds(top, HALF), k * HALF:(k + 1) * HALF] = trio[k][layer, part]
    total[...] = jnp.zeros(total.shape, F32)
    wave = (probe[0].astype(F32), probe[1].astype(F32))
    spread = (propagator[0], propagator[1])
    for slot in range(2):
        row, col = (place[2 * slot], place[2 * slot + 1])

        low = row % 8
        base = pl.multiple_of(row - low, 8)

        def window(index):
            strip = extended[index, pl.ds(base, WIN + 8), :]
            return cut_rows(cut_lanes(strip, col), low)

        layer0 = (window(0), window(1))
        spectrum = forward(times(wave, layer0), tables)
        entering = inverse(times(spectrum, spread), tables)
        layer1 = (window(2), window(3))
        spectrum = forward(times(entering, layer1), tables)
        power = spectrum[0] * spectrum[0] + spectrum[1] * spectrum[1]
        misfit = weight[slot] * (power - intensity[slot])
        adjoint = inverse((misfit * spectrum[0], misfit * spectrum[1]), tables)
        term1 = conj_times(entering, adjoint)
        spectrum = forward(conj_times(layer1, adjoint), tables)
        adjoint = inverse(conj_times(spread, spectrum), tables)
        term0 = conj_times(wave, adjoint)
        upstream = conj_times(layer0, adjoint)
        for part in range(2):
            if slot == 0:
                out_probe[part] = upstream[part]
            else:
                out_probe[part] += upstream[part]

        def add_window(index, value):
            total[index, pl.ds(base, WIN + 8), :] += put_lanes(put_rows(value, low), col)

        for layer, term in ((0, term0), (1, term1)):
            for part in range(2):
                add_window(2 * layer + part, term[part])
    groups_out = ((far_top, (out_far_l, out_far, out_far_r)), (near_top, (out_near_l, out_near, out_near_r)), (HALF, (out_own_l, out_own, out_own_r)))
    for top, trio in groups_out:
        for k in range(3):
            for layer in range(2):
                for part in range(2):
                    trio[k][layer, part] = total[2 * layer + part, pl.ds(top, HALF), k * HALF:(k + 1) * HALF]


def work(place, weight, tiles, probe, propagator, intensity, tables):
    vmem = pl.BlockSpec(memory_space=pltpu.VMEM)
    smem = pl.BlockSpec(memory_space=pltpu.SMEM)
    tile = jax.ShapeDtypeStruct((2, 2, HALF, HALF), F32)
    return pl.pallas_call(
        work_kernel,
        out_shape=[tile] * 9 + [jax.ShapeDtypeStruct((2, WIN, WIN), F32)],
        in_specs=[smem, smem] + [vmem] * 13,
        out_specs=[vmem] * 10,
        scratch_shapes=[pltpu.VMEM((4, 3 * HALF, 3 * HALF), F32)] * 2,
        compiler_params=pltpu.CompilerParams(vmem_limit_bytes=48 * 1024 * 1024),
        cost_estimate=pl.CostEstimate(flops=10_000_000_000, bytes_accessed=8_000_000, transcendentals=0),
    )(place, weight, *tiles, probe, propagator, intensity, tables)


def pairs_up(count):
    return [(i, i + 1) for i in range(count - 1)]


def flipped(pairs):
    return [(j, i) for i, j in pairs]


def sides(value):
    ups = pairs_up(lax.axis_size("col"))
    return lax.ppermute(value, "col", ups), lax.ppermute(value, "col", flipped(ups))


def across(axis, bit):
    return [(i, i ^ bit) for i in range(lax.axis_size(axis))]


def probe_block(term):
    row, col = (lax.axis_index("row"), lax.axis_index("col"))
    rows, cols = (lax.axis_size("row"), lax.axis_size("col"))
    bit = rows // 2
    while bit >= 1:
        size = term.shape[1] // 2
        upper = (row // bit) % 2
        first, second = (term[:, :size], term[:, size:])
        kept = jnp.where(upper == 1, second, first)
        sent = jnp.where(upper == 1, first, second)
        term = kept + lax.ppermute(sent, "row", across("row", bit))
        bit //= 2
    bit = 1
    while bit < cols:
        term = term + lax.ppermute(term, "col", across("col", bit))
        bit *= 2
    width = WIN // cols
    return lax.dynamic_slice(term, (0, 0, col * width), (2, term.shape[1], width))


def per_device(object_slices, probe_wave, propagator_phase, intensity, centres, batch_order):
    rows = lax.axis_size("row")
    row, col = (lax.axis_index("row"), lax.axis_index("col"))
    hops = [(i, i + 2) for i in range(0, rows - 2, 2)] + [(i + 2, i) for i in range(1, rows - 2, 2)]
    swap = across("row", 1)
    near = lax.ppermute(object_slices, "row", swap)
    own_l, own_r = sides(object_slices)
    far = lax.ppermute(near, "row", hops)
    near_l, near_r = sides(near)
    far_l, far_r = sides(far)
    tiles = (object_slices, own_l, own_r, near, near_l, near_r, far, far_l, far_r)

    order = order_matrix()
    angles = dot(dot(order, propagator_phase).astype(BF16), order.T)
    propagator = jnp.stack([jnp.cos(angles), jnp.sin(angles)])
    middle = jnp.einsum("ab,sbc->sac", order, intensity[0, 0], preferred_element_type=F32).astype(BF16)
    measured = jnp.einsum("sac,dc->sad", middle, order, preferred_element_type=F32)
    upper = row % 2
    place = jnp.concatenate([
        (centres[0, 0] - jnp.stack([row * HALF, col * HALF])).reshape(4),
        jnp.stack([2 * HALF * (1 - upper), 2 * HALF * upper]),
    ]).astype(jnp.int32)
    weight = (batch_order[0, 0] >= 0).astype(F32)
    outs = work(place, weight, tiles, probe_wave, propagator, measured, half_tables())
    own, own_l, own_r, near, near_l, near_r, far, far_l, far_r, probe_term = outs

    ups = pairs_up(lax.axis_size("col"))

    def fold(middle, left, right):
        return middle + lax.ppermute(left, "col", flipped(ups)) + lax.ppermute(right, "col", ups)

    far = fold(far, far_l, far_r)
    near = fold(near, near_l, near_r) + lax.ppermute(far, "row", flipped(hops))
    own = fold(own, own_l, own_r) + lax.ppermute(near, "row", swap)
    return own, probe_block(probe_term)


def solution(mesh):
    placed = (
        P(None, None, "row", "col"),
        P(),
        P(),
        P("row", "col", None, None, None),
        P("row", "col", None, None),
        P("row", "col", None),
    )
    return jax.shard_map(
        per_device,
        mesh=mesh,
        in_specs=placed,
        out_specs=(P(None, None, "row", "col"), P(None, "row", "col")),
        check_vma=False,
    )
```

time: 795 us -> 190 us (0.24)
  waiting for transfers between devices: 549 us -> 42.3 us
  local copies, waits for them, and re-layouts: 56.3 us -> 13.5 us
  other arithmetic: 26.2 us -> 1.96 us
  between operations: 22.5 us -> 1.27 us
  matrix products: 22.5 us -> 3.36 us
  Pallas kernels: 0 us -> 11.1 us
    unnamed x2 -> x0, waiting for transfers between devices: 454 us -> none
    ppermute x8 -> x25, waiting for transfers between devices: 95 us -> 42.3 us  [the longest x4 28.4 us: probe_block(): term = term + lax.ppermute(term, 'col', across('col', bit))]
    dynamic_update_slice x2 -> x0, local copies, waits for them, and re-layouts: 29.4 us -> none  [per_device(): lax.dynamic_update_slice(accumulated, current + stacked[slot_index], anchor)]
    dot_general x12 -> x2, matrix products: 22.5 us -> 3.36 us  [the longest x1 2.2 us: dot(): return jnp.dot(left, right, preferred_element_type=F32)]
    unnamed x26 -> x56, local copies, waits for them, and re-layouts: 1.82 us -> 13.3 us
    pallas_call x0 -> x1, Pallas kernels: none -> 11.1 us  [work(): pl.pallas_call(work_kernel, out_shape=[tile] * 9 + [jax.ShapeDtypeStruct(...]
    gather x6 -> x0, local copies, waits for them, and re-layouts: 9.42 us -> none
    reshape x3 -> x0, local copies, waits for them, and re-layouts: 8.63 us -> none  [the longest x2 7.95 us: per_device(): probe_term.transpose(0, 1, 3, 2, 4)]
  transfers between devices with their start and end apart: 9 -> 25, of which waited for: 6 -> 8; matrix products, arithmetic and copies ran while one was open for 4% -> 2% of each run, Pallas kernels for 0% -> 0%
where the time goes in v1:
time: 190 us; the launch traced here: 186 us
  starting transfers between devices  113 us (59%)
  waiting for transfers between devices  42.3 us (22%)
  local copies, waits for them, and re-layouts  13.5 us (7%)
  Pallas kernels  11.1 us (6%)
  matrix products  3.36 us (2%)
  other arithmetic  1.96 us (1%)
    ppermute x5, starting transfers between devices, probe_block(): term = kept + lax.ppermute(sent, 'row', across('row', bit))  29 us
    ppermute x4, waiting for transfers between devices, probe_block(): term = term + lax.ppermute(term, 'col', across('col', bit))  28.4 us
    ppermute x3, starting transfers between devices, sides(): lax.ppermute(value, 'col', ups)  25.9 us
    ppermute x1, starting transfers between devices, per_device(): near = lax.ppermute(object_slices, 'row', swap)  16.4 us
    unnamed x56, local copies, waits for them, and re-layouts  13.3 us
    ppermute x4, starting transfers between devices, probe_block(): term = term + lax.ppermute(term, 'col', across('col', bit))  11.2 us
    pallas_call x1, Pallas kernels, work(): pl.pallas_call(work_kernel, out_shape=[tile] * 9 + [jax.ShapeDtypeStruct(...  11.1 us
    ppermute x5, waiting for transfers between devices, probe_block(): term = kept + lax.ppermute(sent, 'row', across('row', bit))  10.9 us
  transfers between devices with their start and end apart: 25, of which 8 were waited for; matrix products, arithmetic and copies ran while one was open for 2% of the time, Pallas kernels for 0%

profile of v1, /device:TPU:1, one launch (start us, length us, event | category | flops | bytes accessed | tf_op | source)
XLA Modules:
  0.0 186.0 jit_solution(18207482675176638430)
XLA Ops:
  0.6 16.4 %collective-permute-start.2 = (f32[2,2,128,128]{3,2,1,0:T(8,128)}, f32[2,2,128,128]{3,2,1,0:T(8,128)S(1)}, u32[]{:S(2)}, u32[]{:S(2)}) collective-permute-start(f32[2,2,128,128]{3,2,1,0:T(8,128)} %own.1), channel_id=1, source_target_pairs={{0,16},{16,0},{32,48},{48,32},{64,80},{80,64},{96,112},{112,96},{1... | collective-permute-start | bytes 786440 | tf_op jit(solution)/shard_map/ppermute | solution.py:256
  17.1 2.9 %collective-permute-start.1 = (f32[2,2,128,128]{3,2,1,0:T(8,128)}, f32[2,2,128,128]{3,2,1,0:T(8,128)S(1)}, u32[]{:S(2)}, u32[]{:S(2)}) collective-permute-start(f32[2,2,128,128]{3,2,1,0:T(8,128)} %own.1), channel_id=1, source_target_pairs={{1,0},{2,1},{3,2},{4,3},{5,4},{6,5},{7,6},{8,7},{9,8},{10,9},{11,1... | collective-permute-start | bytes 786440 | tf_op jit(solution)/shard_map/ppermute | solution.py:224
  19.9 2.7 %collective-permute-start = (f32[2,2,128,128]{3,2,1,0:T(8,128)}, f32[2,2,128,128]{3,2,1,0:T(8,128)S(1)}, u32[]{:S(2)}, u32[]{:S(2)}) collective-permute-start(f32[2,2,128,128]{3,2,1,0:T(8,128)} %own.1), channel_id=1, source_target_pairs={{0,1},{1,2},{2,3},{3,4},{4,5},{5,6},{6,7},{7,8},{8,9},{9,10},{10,1... | collective-permute-start | bytes 786440 | tf_op jit(solution)/shard_map/ppermute | solution.py:224
  22.6 2.2 %cosine_bitcast_fusion = (f32[1,256,256]{2,1,0:T(8,128)S(1)}, f32[1,256,256]{2,1,0:T(8,128)S(1)}) fusion(bf16[256,256]{1,0:T(8,128)(2,1)} %constant.104.clone, bf16[256,256]{1,0:T(8,128)(2,1)} %param.10), kind=kOutput, calls=%fused_computation.12 | convolution fusion | flops 67174400 | bytes 786432 | tf_op jit(solution)/shard_map/dot_general | solution.py:47
  24.9 3.1 %collective-permute-start.5 = (f32[2,2,128,128]{3,2,1,0:T(8,128)S(1)}, f32[2,2,128,128]{3,2,1,0:T(8,128)S(1)}, u32[]{:S(2)}, u32[]{:S(2)}) collective-permute-start(f32[2,2,128,128]{3,2,1,0:T(8,128)S(1)} %collective-permute-done.2.near), channel_id=1, source_target_pairs={{0,32},{32,64},{64,96},{96,128},{128,160},{160,192},{192,224},{224... | collective-permute-start | bytes 786440 | tf_op jit(solution)/shard_map/ppermute | solution.py:258
  29.7 2.1 %collective-permute-start.4 = (f32[2,2,128,128]{3,2,1,0:T(8,128)S(1)}, f32[2,2,128,128]{3,2,1,0:T(8,128)S(1)}, u32[]{:S(2)}, u32[]{:S(2)}) collective-permute-start(f32[2,2,128,128]{3,2,1,0:T(8,128)S(1)} %collective-permute-done.2.near), channel_id=1, source_target_pairs={{1,0},{2,1},{3,2},{4,3},{5,4},{6,5},{7,6},{8,7},{9,8},{10,9},{11,1... | collective-permute-start | bytes 786440 | tf_op jit(solution)/shard_map/ppermute | solution.py:224
  31.7 19.6 %collective-permute-start.3 = (f32[2,2,128,128]{3,2,1,0:T(8,128)S(1)}, f32[2,2,128,128]{3,2,1,0:T(8,128)S(1)}, u32[]{:S(2)}, u32[]{:S(2)}) collective-permute-start(f32[2,2,128,128]{3,2,1,0:T(8,128)S(1)} %collective-permute-done.2.near), channel_id=1, source_target_pairs={{0,1},{1,2},{2,3},{3,4},{4,5},{5,6},{6,7},{7,8},{8,9},{9,10},{10,1... | collective-permute-start | bytes 786440 | tf_op jit(solution)/shard_map/ppermute | solution.py:224
  51.3 1.9 %collective-permute-start.7 = (f32[2,2,128,128]{3,2,1,0:T(8,128)S(1)}, f32[2,2,128,128]{3,2,1,0:T(8,128)S(1)}, u32[]{:S(2)}, u32[]{:S(2)}) collective-permute-start(f32[2,2,128,128]{3,2,1,0:T(8,128)S(1)} %collective-permute-done.5.far), channel_id=1, source_target_pairs={{1,0},{2,1},{3,2},{4,3},{5,4},{6,5},{7,6},{8,7},{9,8},{10,9},{11,1... | collective-permute-start | bytes 786440 | tf_op jit(solution)/shard_map/ppermute | solution.py:224
  53.3 3.6 %collective-permute-start.6 = (f32[2,2,128,128]{3,2,1,0:T(8,128)S(1)}, f32[2,2,128,128]{3,2,1,0:T(8,128)S(1)}, u32[]{:S(2)}, u32[]{:S(2)}) collective-permute-start(f32[2,2,128,128]{3,2,1,0:T(8,128)S(1)} %collective-permute-done.5.far), channel_id=1, source_target_pairs={{0,1},{1,2},{2,3},{3,4},{4,5},{5,6},{6,7},{7,8},{8,9},{9,10},{10,1... | collective-permute-start | bytes 786440 | tf_op jit(solution)/shard_map/ppermute | solution.py:224
  69.4 11.1 %shard_map.95 = (f32[2,2,128,128]{3,2,1,0:T(8,128)S(1)}, f32[2,2,128,128]{3,2,1,0:T(8,128)S(1)}, f32[2,2,128,128]{3,2,1,0:T(8,128)S(1)}, f32[2,2,128,128]{3,2,1,...) custom-call(s32[6]{0:T(128)S(1)} %pad_add_fusion.1.place, ...), custom_call_target="tpu_custom_call" | custom-call | flops 10000000000 | bytes 8000000 | tf_op jit(solution)/shard_map/pallas_call | solution.py:203
  81.3 5.5 %collective-permute-start.16 = (f32[2,128,256]{2,1,0:T(8,128)S(1)}, f32[2,128,256]{2,1,0:T(8,128)S(1)}, u32[]{:S(2)}, u32[]{:S(2)}) collective-permute-start(f32[2,128,256]{2,1,0:T(8,128)S(1)} %slice_select_fusion), channel_id=1, source_target_pairs={{0,256},{16,272},{32,288},{48,304},{64,320},{80,336},{96,352},{112... | collective-permute-start | bytes 786440 | tf_op jit(solution)/shard_map/ppermute | solution.py:241
  86.8 5.2 %collective-permute-done.16 = f32[2,128,256]{2,1,0:T(8,128)S(1)} collective-permute-done((f32[2,128,256]{2,1,0:T(8,128)S(1)}, f32[2,128,256]{2,1,0:T(8,128)S(1)}, u32[]{:S(2)}, u32[]{:S(2)}) %collective-permute-start.16) | collective-permute-done | bytes 262176 | tf_op jit(solution)/shard_map/ppermute | solution.py:241
  92.1 3.2 %collective-permute-start.17 = (f32[2,64,256]{2,1,0:T(8,128)S(1)}, f32[2,64,256]{2,1,0:T(8,128)S(1)}, u32[]{:S(2)}, u32[]{:S(2)}) collective-permute-start(f32[2,64,256]{2,1,0:T(8,128)S(1)} %slice_select_fusion.1), channel_id=1, source_target_pairs={{0,128},{16,144},{32,160},{48,176},{64,192},{80,208},{96,224},{112... | collective-permute-start | bytes 393224 | tf_op jit(solution)/shard_map/ppermute | solution.py:241
  95.4 3.6 %collective-permute-done.17 = f32[2,64,256]{2,1,0:T(8,128)S(1)} collective-permute-done((f32[2,64,256]{2,1,0:T(8,128)S(1)}, f32[2,64,256]{2,1,0:T(8,128)S(1)}, u32[]{:S(2)}, u32[]{:S(2)}) %collective-permute-start.17) | collective-permute-done | bytes 131104 | tf_op jit(solution)/shard_map/ppermute | solution.py:241
  99.0 4.5 %collective-permute-start.18 = (f32[2,32,256]{2,1,0:T(8,128)S(1)}, f32[2,32,256]{2,1,0:T(8,128)S(1)}, u32[]{:S(2)}, u32[]{:S(2)}) collective-permute-start(f32[2,32,256]{2,1,0:T(8,128)S(1)} %slice_select_fusion.2), channel_id=1, source_target_pairs={{0,64},{16,80},{32,96},{48,112},{64,0},{80,16},{96,32},{112,48},{1... | collective-permute-start | bytes 196616 | tf_op jit(solution)/shard_map/ppermute | solution.py:241
  103.6 2.9 %collective-permute-start.8 = (f32[2,2,128,128]{3,2,1,0:T(8,128)S(1)}, f32[2,2,128,128]{3,2,1,0:T(8,128)S(1)}, u32[]{:S(2)}, u32[]{:S(2)}) collective-permute-start(f32[2,2,128,128]{3,2,1,0:T(8,128)S(1)} %get-tuple-element.13), channel_id=1, source_target_pairs={{1,0},{2,1},{3,2},{4,3},{5,4},{6,5},{7,6},{8,7},{9,8},{10,9},{11,1... | collective-permute-start | bytes 786440 | tf_op jit(solution)/shard_map/ppermute | solution.py:280
  106.5 2.6 %collective-permute-start.9 = (f32[2,2,128,128]{3,2,1,0:T(8,128)S(1)}, f32[2,2,128,128]{3,2,1,0:T(8,128)S(1)}, u32[]{:S(2)}, u32[]{:S(2)}) collective-permute-start(f32[2,2,128,128]{3,2,1,0:T(8,128)S(1)} %get-tuple-element.14), channel_id=1, source_target_pairs={{0,1},{1,2},{2,3},{3,4},{4,5},{5,6},{6,7},{7,8},{8,9},{9,10},{10,1... | collective-permute-start | bytes 786440 | tf_op jit(solution)/shard_map/ppermute | solution.py:280
  109.2 1.9 %collective-permute-start.10 = (f32[2,2,128,128]{3,2,1,0:T(8,128)S(1)}, f32[2,2,128,128]{3,2,1,0:T(8,128)S(1)}, u32[]{:S(2)}, u32[]{:S(2)}) collective-permute-start(f32[2,2,128,128]{3,2,1,0:T(8,128)S(1)} %copy-done.4), channel_id=1, source_target_pairs={{1,0},{2,1},{3,2},{4,3},{5,4},{6,5},{7,6},{8,7},{9,8},{10,9},{11,1... | collective-permute-start | bytes 786440 | tf_op jit(solution)/shard_map/ppermute | solution.py:280
  111.1 1.9 %collective-permute-start.12 = (f32[2,2,128,128]{3,2,1,0:T(8,128)S(1)}, f32[2,2,128,128]{3,2,1,0:T(8,128)S(1)}, u32[]{:S(2)}, u32[]{:S(2)}) collective-permute-start(f32[2,2,128,128]{3,2,1,0:T(8,128)S(1)} %copy-done.8), channel_id=1, source_target_pairs={{1,0},{2,1},{3,2},{4,3},{5,4},{6,5},{7,6},{8,7},{9,8},{10,9},{11,1... | collective-permute-start | bytes 786440 | tf_op jit(solution)/shard_map/ppermute | solution.py:280
  113.1 3.6 %collective-permute-start.13 = (f32[2,2,128,128]{3,2,1,0:T(8,128)S(1)}, f32[2,2,128,128]{3,2,1,0:T(8,128)S(1)}, u32[]{:S(2)}, u32[]{:S(2)}) collective-permute-start(f32[2,2,128,128]{3,2,1,0:T(8,128)S(1)} %copy-done.6), channel_id=1, source_target_pairs={{0,1},{1,2},{2,3},{3,4},{4,5},{5,6},{6,7},{7,8},{8,9},{9,10},{10,1... | collective-permute-start | bytes 786440 | tf_op jit(solution)/shard_map/ppermute | solution.py:280
  116.8 2.9 %collective-permute-done.12 = f32[2,2,128,128]{3,2,1,0:T(8,128)S(1)} collective-permute-done((f32[2,2,128,128]{3,2,1,0:T(8,128)S(1)}, f32[2,2,128,128]{3,2,1,0:T(8,128)S(1)}, u32[]{:S(2)}, u32[]{:S(2)}) %collective-permute-start.12) | collective-permute-done | bytes 262176 | tf_op jit(solution)/shard_map/ppermute | solution.py:280
  119.7 1.9 %collective-permute-start.11 = (f32[2,2,128,128]{3,2,1,0:T(8,128)S(1)}, f32[2,2,128,128]{3,2,1,0:T(8,128)S(1)}, u32[]{:S(2)}, u32[]{:S(2)}) collective-permute-start(f32[2,2,128,128]{3,2,1,0:T(8,128)S(1)} %get-tuple-element.17), channel_id=1, source_target_pairs={{0,1},{1,2},{2,3},{3,4},{4,5},{5,6},{6,7},{7,8},{8,9},{9,10},{10,1... | collective-permute-start | bytes 786440 | tf_op jit(solution)/shard_map/ppermute | solution.py:280
  121.6 2.5 %collective-permute-start.19 = (f32[2,16,256]{2,1,0:T(8,128)S(1)}, f32[2,16,256]{2,1,0:T(8,128)S(1)}, u32[]{:S(2)}, u32[]{:S(2)}) collective-permute-start(f32[2,16,256]{2,1,0:T(8,128)S(1)} %slice_select_fusion.3), channel_id=1, source_target_pairs={{0,32},{16,48},{32,0},{48,16},{64,96},{80,112},{96,64},{112,80},{1... | collective-permute-start | bytes 98312 | tf_op jit(solution)/shard_map/ppermute | solution.py:241
  124.2 2.1 %collective-permute-done.19 = f32[2,16,256]{2,1,0:T(8,128)S(1)} collective-permute-done((f32[2,16,256]{2,1,0:T(8,128)S(1)}, f32[2,16,256]{2,1,0:T(8,128)S(1)}, u32[]{:S(2)}, u32[]{:S(2)}) %collective-permute-start.19) | collective-permute-done | bytes 32800 | tf_op jit(solution)/shard_map/ppermute | solution.py:241
  127.6 13.3 %collective-permute-start.20 = (f32[2,8,256]{2,1,0:T(8,128)S(1)}, f32[2,8,256]{2,1,0:T(8,128)S(1)}, u32[]{:S(2)}, u32[]{:S(2)}) collective-permute-start(f32[2,8,256]{2,1,0:T(8,128)S(1)} %slice_select_fusion.4), channel_id=1, source_target_pairs={{0,16},{16,0},{32,48},{48,32},{64,80},{80,64},{96,112},{112,96},{1... | collective-permute-start | bytes 49160 | tf_op jit(solution)/shard_map/ppermute | solution.py:241
  141.0 3.8 %collective-permute-start.15 = (f32[2,2,128,128]{3,2,1,0:T(8,128)S(1)}, f32[2,2,128,128]{3,2,1,0:T(8,128)S(1)}, u32[]{:S(2)}, u32[]{:S(2)}) collective-permute-start(f32[2,2,128,128]{3,2,1,0:T(8,128)S(1)} %add_add_fusion.1), channel_id=1, source_target_pairs={{0,16},{16,0},{32,48},{48,32},{64,80},{80,64},{96,112},{112,96},{1... | collective-permute-start | bytes 786440 | tf_op jit(solution)/shard_map/ppermute | solution.py:284
  144.9 4.8 %collective-permute-start.21 = (f32[2,8,256]{2,1,0:T(8,128)S(1)}, f32[2,8,256]{2,1,0:T(8,128)S(1)}, u32[]{:S(2)}, u32[]{:S(2)}) collective-permute-start(f32[2,8,256]{2,1,0:T(8,128)S(1)} %select_add_fusion.4), channel_id=1, source_target_pairs={{0,1},{1,0},{2,3},{3,2},{4,5},{5,4},{6,7},{7,6},{8,9},{9,8},{10,11... | collective-permute-start | bytes 49160 | tf_op jit(solution)/shard_map/ppermute | solution.py:245
  150.5 2.6 %collective-permute-start.22 = (f32[2,8,256]{2,1,0:T(8,128)S(1)}, f32[2,8,256]{2,1,0:T(8,128)S(1)}, u32[]{:S(2)}, u32[]{:S(2)}) collective-permute-start(f32[2,8,256]{2,1,0:T(8,128)S(1)} %add.94), channel_id=1, source_target_pairs={{0,2},{1,3},{2,0},{3,1},{4,6},{5,7},{6,4},{7,5},{8,10},{9,11},{10,... | collective-permute-start | bytes 49160 | tf_op jit(solution)/shard_map/ppermute | solution.py:245
  153.1 15.1 %collective-permute-done.22 = f32[2,8,256]{2,1,0:T(8,128)S(1)} collective-permute-done((f32[2,8,256]{2,1,0:T(8,128)S(1)}, f32[2,8,256]{2,1,0:T(8,128)S(1)}, u32[]{:S(2)}, u32[]{:S(2)}) %collective-permute-start.22) | collective-permute-done | bytes 16416 | tf_op jit(solution)/shard_map/ppermute | solution.py:245
  168.2 1.9 %collective-permute-start.23 = (f32[2,8,256]{2,1,0:T(8,128)S(1)}, f32[2,8,256]{2,1,0:T(8,128)S(1)}, u32[]{:S(2)}, u32[]{:S(2)}) collective-permute-start(f32[2,8,256]{2,1,0:T(8,128)S(1)} %add.95), channel_id=1, source_target_pairs={{0,4},{1,5},{2,6},{3,7},{4,0},{5,1},{6,2},{7,3},{8,12},{9,13},{10,... | collective-permute-start | bytes 49160 | tf_op jit(solution)/shard_map/ppermute | solution.py:245
  170.1 5.7 %collective-permute-done.23 = f32[2,8,256]{2,1,0:T(8,128)S(1)} collective-permute-done((f32[2,8,256]{2,1,0:T(8,128)S(1)}, f32[2,8,256]{2,1,0:T(8,128)S(1)}, u32[]{:S(2)}, u32[]{:S(2)}) %collective-permute-start.23) | collective-permute-done | bytes 16416 | tf_op jit(solution)/shard_map/ppermute | solution.py:245
  177.8 6.8 %collective-permute-done.24 = f32[2,8,256]{2,1,0:T(8,128)S(1)} collective-permute-done((f32[2,8,256]{2,1,0:T(8,128)S(1)}, f32[2,8,256]{2,1,0:T(8,128)S(1)}, u32[]{:S(2)}, u32[]{:S(2)}) %collective-permute-start.24) | collective-permute-done | bytes 16416 | tf_op jit(solution)/shard_map/ppermute | solution.py:245
  (102 shorter events, 20.6 us)
Async XLA Ops:
  0.6 56.4 %copy-start = (bf16[1,1,2,256,256]{4,3,2,1,0:T(8,128)(2,1)S(1)}, bf16[1,1,2,256,256]{4,3,2,1,0:T(8,128)(2,1)}, u32[]{:S(2)}) copy-start(bf16[1,1,2,256,256]{4,3,2,1,0:T(8,128)(2,1)} %param.11) | copy-start | bytes 786436
  0.6 24.3 %collective-permute-start.2 = (f32[2,2,128,128]{3,2,1,0:T(8,128)}, f32[2,2,128,128]{3,2,1,0:T(8,128)S(1)}, u32[]{:S(2)}, u32[]{:S(2)}) collective-permute-start(f32[2,2,128,128]{3,2,1,0:T(8,128)} %own.1), channel_id=1, source_target_pairs={{0,16},{16,0},{32,48},{48,32},{64,80},{80,64},{96,112},{112,96},{1... | collective-permute-start | bytes 786440 | tf_op jit(solution)/shard_map/ppermute | solution.py:256
  17.1 36.2 %collective-permute-start.1 = (f32[2,2,128,128]{3,2,1,0:T(8,128)}, f32[2,2,128,128]{3,2,1,0:T(8,128)S(1)}, u32[]{:S(2)}, u32[]{:S(2)}) collective-permute-start(f32[2,2,128,128]{3,2,1,0:T(8,128)} %own.1), channel_id=1, source_target_pairs={{1,0},{2,1},{3,2},{4,3},{5,4},{6,5},{7,6},{8,7},{9,8},{10,9},{11,1... | collective-permute-start | bytes 786440 | tf_op jit(solution)/shard_map/ppermute | solution.py:224
  19.9 38.3 %collective-permute-start = (f32[2,2,128,128]{3,2,1,0:T(8,128)}, f32[2,2,128,128]{3,2,1,0:T(8,128)S(1)}, u32[]{:S(2)}, u32[]{:S(2)}) collective-permute-start(f32[2,2,128,128]{3,2,1,0:T(8,128)} %own.1), channel_id=1, source_target_pairs={{0,1},{1,2},{2,3},{3,4},{4,5},{5,6},{6,7},{7,8},{8,9},{9,10},{10,1... | collective-permute-start | bytes 786440 | tf_op jit(solution)/shard_map/ppermute | solution.py:224
  24.9 32.2 %copy-start.25 = (bf16[256,256,1]{1,0,2:T(8,128)(2,1)S(1)}, bf16[256,256,1]{1,0,2:T(8,128)(2,1)}, u32[]{:S(2)}) copy-start(bf16[256,256,1]{1,0,2:T(8,128)(2,1)} %constant.109) | copy-start | bytes 393220
  24.9 33.3 %copy-start.9 = (f32[2,2,128,128]{3,2,1,0:T(8,128)}, f32[2,2,128,128]{3,2,1,0:T(8,128)S(1)}, u32[]{:S(2)}) copy-start(f32[2,2,128,128]{3,2,1,0:T(8,128)S(1)} %collective-permute-done.2.near) | copy-start | bytes 786436
  24.9 26.4 %collective-permute-start.5 = (f32[2,2,128,128]{3,2,1,0:T(8,128)S(1)}, f32[2,2,128,128]{3,2,1,0:T(8,128)S(1)}, u32[]{:S(2)}, u32[]{:S(2)}) collective-permute-start(f32[2,2,128,128]{3,2,1,0:T(8,128)S(1)} %collective-permute-done.2.near), channel_id=1, source_target_pairs={{0,32},{32,64},{64,96},{96,128},{128,160},{160,192},{192,224},{224... | collective-permute-start | bytes 786440 | tf_op jit(solution)/shard_map/ppermute | solution.py:258
  29.7 29.3 %collective-permute-start.4 = (f32[2,2,128,128]{3,2,1,0:T(8,128)S(1)}, f32[2,2,128,128]{3,2,1,0:T(8,128)S(1)}, u32[]{:S(2)}, u32[]{:S(2)}) collective-permute-start(f32[2,2,128,128]{3,2,1,0:T(8,128)S(1)} %collective-permute-done.2.near), channel_id=1, source_target_pairs={{1,0},{2,1},{3,2},{4,3},{5,4},{6,5},{7,6},{8,7},{9,8},{10,9},{11,1... | collective-permute-start | bytes 786440 | tf_op jit(solution)/shard_map/ppermute | solution.py:224
  31.7 27.9 %collective-permute-start.3 = (f32[2,2,128,128]{3,2,1,0:T(8,128)S(1)}, f32[2,2,128,128]{3,2,1,0:T(8,128)S(1)}, u32[]{:S(2)}, u32[]{:S(2)}) collective-permute-start(f32[2,2,128,128]{3,2,1,0:T(8,128)S(1)} %collective-permute-done.2.near), channel_id=1, source_target_pairs={{0,1},{1,2},{2,3},{3,4},{4,5},{5,6},{6,7},{7,8},{8,9},{9,10},{10,1... | collective-permute-start | bytes 786440 | tf_op jit(solution)/shard_map/ppermute | solution.py:224
  51.3 6.9 %copy-start.15 = (f32[2,2,128,128]{3,2,1,0:T(8,128)}, f32[2,2,128,128]{3,2,1,0:T(8,128)S(1)}, u32[]{:S(2)}) copy-start(f32[2,2,128,128]{3,2,1,0:T(8,128)S(1)} %collective-permute-done.5.far) | copy-start | bytes 786436
  51.3 9.0 %collective-permute-start.7 = (f32[2,2,128,128]{3,2,1,0:T(8,128)S(1)}, f32[2,2,128,128]{3,2,1,0:T(8,128)S(1)}, u32[]{:S(2)}, u32[]{:S(2)}) collective-permute-start(f32[2,2,128,128]{3,2,1,0:T(8,128)S(1)} %collective-permute-done.5.far), channel_id=1, source_target_pairs={{1,0},{2,1},{3,2},{4,3},{5,4},{6,5},{7,6},{8,7},{9,8},{10,9},{11,1... | collective-permute-start | bytes 786440 | tf_op jit(solution)/shard_map/ppermute | solution.py:224
  53.3 7.8 %collective-permute-start.6 = (f32[2,2,128,128]{3,2,1,0:T(8,128)S(1)}, f32[2,2,128,128]{3,2,1,0:T(8,128)S(1)}, u32[]{:S(2)}, u32[]{:S(2)}) collective-permute-start(f32[2,2,128,128]{3,2,1,0:T(8,128)S(1)} %collective-permute-done.5.far), channel_id=1, source_target_pairs={{0,1},{1,2},{2,3},{3,4},{4,5},{5,6},{6,7},{7,8},{8,9},{9,10},{10,1... | collective-permute-start | bytes 786440 | tf_op jit(solution)/shard_map/ppermute | solution.py:224
  81.3 10.7 %collective-permute-start.16 = (f32[2,128,256]{2,1,0:T(8,128)S(1)}, f32[2,128,256]{2,1,0:T(8,128)S(1)}, u32[]{:S(2)}, u32[]{:S(2)}) collective-permute-start(f32[2,128,256]{2,1,0:T(8,128)S(1)} %slice_select_fusion), channel_id=1, source_target_pairs={{0,256},{16,272},{32,288},{48,304},{64,320},{80,336},{96,352},{112... | collective-permute-start | bytes 786440 | tf_op jit(solution)/shard_map/ppermute | solution.py:241
  92.1 6.9 %collective-permute-start.17 = (f32[2,64,256]{2,1,0:T(8,128)S(1)}, f32[2,64,256]{2,1,0:T(8,128)S(1)}, u32[]{:S(2)}, u32[]{:S(2)}) collective-permute-start(f32[2,64,256]{2,1,0:T(8,128)S(1)} %slice_select_fusion.1), channel_id=1, source_target_pairs={{0,128},{16,144},{32,160},{48,176},{64,192},{80,208},{96,224},{112... | collective-permute-start | bytes 393224 | tf_op jit(solution)/shard_map/ppermute | solution.py:241
  95.3 15.8 %copy-start.8 = (f32[2,2,128,128]{3,2,1,0:T(8,128)S(1)}, f32[2,2,128,128]{3,2,1,0:T(8,128)}, u32[]{:S(2)}) copy-start(f32[2,2,128,128]{3,2,1,0:T(8,128)} %copy-done.7) | copy-start | bytes 786436
  95.3 13.8 %copy-start.4 = (f32[2,2,128,128]{3,2,1,0:T(8,128)S(1)}, f32[2,2,128,128]{3,2,1,0:T(8,128)}, u32[]{:S(2)}) copy-start(f32[2,2,128,128]{3,2,1,0:T(8,128)} %copy-done.3) | copy-start | bytes 786436
  95.4 17.7 %copy-start.6 = (f32[2,2,128,128]{3,2,1,0:T(8,128)S(1)}, f32[2,2,128,128]{3,2,1,0:T(8,128)}, u32[]{:S(2)}) copy-start(f32[2,2,128,128]{3,2,1,0:T(8,128)} %copy-done.5) | copy-start | bytes 786436
  99.0 14.0 %collective-permute-start.18 = (f32[2,32,256]{2,1,0:T(8,128)S(1)}, f32[2,32,256]{2,1,0:T(8,128)S(1)}, u32[]{:S(2)}, u32[]{:S(2)}) collective-permute-start(f32[2,32,256]{2,1,0:T(8,128)S(1)} %slice_select_fusion.2), channel_id=1, source_target_pairs={{0,64},{16,80},{32,96},{48,112},{64,0},{80,16},{96,32},{112,48},{1... | collective-permute-start | bytes 196616 | tf_op jit(solution)/shard_map/ppermute | solution.py:241
  103.6 81.6 %collective-permute-start.8 = (f32[2,2,128,128]{3,2,1,0:T(8,128)S(1)}, f32[2,2,128,128]{3,2,1,0:T(8,128)S(1)}, u32[]{:S(2)}, u32[]{:S(2)}) collective-permute-start(f32[2,2,128,128]{3,2,1,0:T(8,128)S(1)} %get-tuple-element.13), channel_id=1, source_target_pairs={{1,0},{2,1},{3,2},{4,3},{5,4},{6,5},{7,6},{8,7},{9,8},{10,9},{11,1... | collective-permute-start | bytes 786440 | tf_op jit(solution)/shard_map/ppermute | solution.py:280
  106.5 78.7 %collective-permute-start.9 = (f32[2,2,128,128]{3,2,1,0:T(8,128)S(1)}, f32[2,2,128,128]{3,2,1,0:T(8,128)S(1)}, u32[]{:S(2)}, u32[]{:S(2)}) collective-permute-start(f32[2,2,128,128]{3,2,1,0:T(8,128)S(1)} %get-tuple-element.14), channel_id=1, source_target_pairs={{0,1},{1,2},{2,3},{3,4},{4,5},{5,6},{6,7},{7,8},{8,9},{9,10},{10,1... | collective-permute-start | bytes 786440 | tf_op jit(solution)/shard_map/ppermute | solution.py:280
  109.2 18.4 %collective-permute-start.10 = (f32[2,2,128,128]{3,2,1,0:T(8,128)S(1)}, f32[2,2,128,128]{3,2,1,0:T(8,128)S(1)}, u32[]{:S(2)}, u32[]{:S(2)}) collective-permute-start(f32[2,2,128,128]{3,2,1,0:T(8,128)S(1)} %copy-done.4), channel_id=1, source_target_pairs={{1,0},{2,1},{3,2},{4,3},{5,4},{6,5},{7,6},{8,7},{9,8},{10,9},{11,1... | collective-permute-start | bytes 786440 | tf_op jit(solution)/shard_map/ppermute | solution.py:280
  111.1 8.6 %collective-permute-start.12 = (f32[2,2,128,128]{3,2,1,0:T(8,128)S(1)}, f32[2,2,128,128]{3,2,1,0:T(8,128)S(1)}, u32[]{:S(2)}, u32[]{:S(2)}) collective-permute-start(f32[2,2,128,128]{3,2,1,0:T(8,128)S(1)} %copy-done.8), channel_id=1, source_target_pairs={{1,0},{2,1},{3,2},{4,3},{5,4},{6,5},{7,6},{8,7},{9,8},{10,9},{11,1... | collective-permute-start | bytes 786440 | tf_op jit(solution)/shard_map/ppermute | solution.py:280
  113.1 8.5 %collective-permute-start.13 = (f32[2,2,128,128]{3,2,1,0:T(8,128)S(1)}, f32[2,2,128,128]{3,2,1,0:T(8,128)S(1)}, u32[]{:S(2)}, u32[]{:S(2)}) collective-permute-start(f32[2,2,128,128]{3,2,1,0:T(8,128)S(1)} %copy-done.6), channel_id=1, source_target_pairs={{0,1},{1,2},{2,3},{3,4},{4,5},{5,6},{6,7},{7,8},{8,9},{9,10},{10,1... | collective-permute-start | bytes 786440 | tf_op jit(solution)/shard_map/ppermute | solution.py:280
  119.7 21.2 %collective-permute-start.11 = (f32[2,2,128,128]{3,2,1,0:T(8,128)S(1)}, f32[2,2,128,128]{3,2,1,0:T(8,128)S(1)}, u32[]{:S(2)}, u32[]{:S(2)}) collective-permute-start(f32[2,2,128,128]{3,2,1,0:T(8,128)S(1)} %get-tuple-element.17), channel_id=1, source_target_pairs={{0,1},{1,2},{2,3},{3,4},{4,5},{5,6},{6,7},{7,8},{8,9},{9,10},{10,1... | collective-permute-start | bytes 786440 | tf_op jit(solution)/shard_map/ppermute | solution.py:280
  121.6 4.7 %collective-permute-start.19 = (f32[2,16,256]{2,1,0:T(8,128)S(1)}, f32[2,16,256]{2,1,0:T(8,128)S(1)}, u32[]{:S(2)}, u32[]{:S(2)}) collective-permute-start(f32[2,16,256]{2,1,0:T(8,128)S(1)} %slice_select_fusion.3), channel_id=1, source_target_pairs={{0,32},{16,48},{32,0},{48,16},{64,96},{80,112},{96,64},{112,80},{1... | collective-permute-start | bytes 98312 | tf_op jit(solution)/shard_map/ppermute | solution.py:241
  126.3 14.7 %collective-permute-start.14 = (f32[2,2,128,128]{3,2,1,0:T(8,128)S(1)}, f32[2,2,128,128]{3,2,1,0:T(8,128)S(1)}, u32[]{:S(2)}, u32[]{:S(2)}) collective-permute-start(f32[2,2,128,128]{3,2,1,0:T(8,128)S(1)} %add_add_fusion), channel_id=1, source_target_pairs={{32,0},{64,32},{96,64},{128,96},{160,128},{192,160},{224,192},{256... | collective-permute-start | bytes 786440 | tf_op jit(solution)/shard_map/ppermute | solution.py:283
  127.6 17.3 %collective-permute-start.20 = (f32[2,8,256]{2,1,0:T(8,128)S(1)}, f32[2,8,256]{2,1,0:T(8,128)S(1)}, u32[]{:S(2)}, u32[]{:S(2)}) collective-permute-start(f32[2,8,256]{2,1,0:T(8,128)S(1)} %slice_select_fusion.4), channel_id=1, source_target_pairs={{0,16},{16,0},{32,48},{48,32},{64,80},{80,64},{96,112},{112,96},{1... | collective-permute-start | bytes 49160 | tf_op jit(solution)/shard_map/ppermute | solution.py:241
  141.0 44.2 %collective-permute-start.15 = (f32[2,2,128,128]{3,2,1,0:T(8,128)S(1)}, f32[2,2,128,128]{3,2,1,0:T(8,128)S(1)}, u32[]{:S(2)}, u32[]{:S(2)}) collective-permute-start(f32[2,2,128,128]{3,2,1,0:T(8,128)S(1)} %add_add_fusion.1), channel_id=1, source_target_pairs={{0,16},{16,0},{32,48},{48,32},{64,80},{80,64},{96,112},{112,96},{1... | collective-permute-start | bytes 786440 | tf_op jit(solution)/shard_map/ppermute | solution.py:284
  144.9 5.6 %collective-permute-start.21 = (f32[2,8,256]{2,1,0:T(8,128)S(1)}, f32[2,8,256]{2,1,0:T(8,128)S(1)}, u32[]{:S(2)}, u32[]{:S(2)}) collective-permute-start(f32[2,8,256]{2,1,0:T(8,128)S(1)} %select_add_fusion.4), channel_id=1, source_target_pairs={{0,1},{1,0},{2,3},{3,2},{4,5},{5,4},{6,7},{7,6},{8,9},{9,8},{10,11... | collective-permute-start | bytes 49160 | tf_op jit(solution)/shard_map/ppermute | solution.py:245
  150.5 17.7 %collective-permute-start.22 = (f32[2,8,256]{2,1,0:T(8,128)S(1)}, f32[2,8,256]{2,1,0:T(8,128)S(1)}, u32[]{:S(2)}, u32[]{:S(2)}) collective-permute-start(f32[2,8,256]{2,1,0:T(8,128)S(1)} %add.94), channel_id=1, source_target_pairs={{0,2},{1,3},{2,0},{3,1},{4,6},{5,7},{6,4},{7,5},{8,10},{9,11},{10,... | collective-permute-start | bytes 49160 | tf_op jit(solution)/shard_map/ppermute | solution.py:245
  168.2 7.6 %collective-permute-start.23 = (f32[2,8,256]{2,1,0:T(8,128)S(1)}, f32[2,8,256]{2,1,0:T(8,128)S(1)}, u32[]{:S(2)}, u32[]{:S(2)}) collective-permute-start(f32[2,8,256]{2,1,0:T(8,128)S(1)} %add.95), channel_id=1, source_target_pairs={{0,4},{1,5},{2,6},{3,7},{4,0},{5,1},{6,2},{7,3},{8,12},{9,13},{10,... | collective-permute-start | bytes 49160 | tf_op jit(solution)/shard_map/ppermute | solution.py:245
  175.9 8.7 %collective-permute-start.24 = (f32[2,8,256]{2,1,0:T(8,128)S(1)}, f32[2,8,256]{2,1,0:T(8,128)S(1)}, u32[]{:S(2)}, u32[]{:S(2)}) collective-permute-start(f32[2,8,256]{2,1,0:T(8,128)S(1)} %add.96), channel_id=1, source_target_pairs={{0,8},{1,9},{2,10},{3,11},{4,12},{5,13},{6,14},{7,15},{8,0},{9,1},... | collective-permute-start | bytes 49160 | tf_op jit(solution)/shard_map/ppermute | solution.py:245
  (21 other events, 29.2 us)

commit v2 on v1

--- a/solution.py
+++ b/solution.py
@@ -139,34 +139,41 @@
     return jnp.where(kept, here, before).reshape(WIN + 8, value.shape[1])
 
 
-def work_kernel(place, weight, own, own_l, own_r, near, near_l, near_r, far, far_l, far_r,
-                probe, propagator, intensity, tables, out_own, out_own_l, out_own_r, out_near,
-                out_near_l, out_near_r, out_far, out_far_l, out_far_r, out_probe, extended, total):
-    near_top = pl.multiple_of(place[4], HALF)
-    far_top = pl.multiple_of(place[5], HALF)
-    groups_in = ((far_top, (far_l, far, far_r)), (near_top, (near_l, near, near_r)), (HALF, (own_l, own, own_r)))
-    for top, trio in groups_in:
+def work_kernel(place, weight, own, near, far, left, right, probe, propagator, intensity, tables,
+                out_own, out_near, out_far, out_left, out_right, out_probe, extended, total, arrived, left_sem):
+    tops = (HALF, pl.multiple_of(place[4], HALF), pl.multiple_of(place[5], HALF))
+
+    def pieces(field, middle, before, after):
         for k in range(3):
-            for layer in range(2):
-                for part in range(2):
-                    extended[2 * layer + part, pl.ds(top, HALF), k * HALF:(k + 1) * HALF] = trio[k][layer, part]
+            rows = pl.ds(tops[k], HALF)
+            yield middle[k], field.at[:, :, rows, HALF:2 * HALF]
+            yield before.at[k], field.at[:, :, rows, 0:HALF]
+            yield after.at[k], field.at[:, :, rows, 2 * HALF:3 * HALF]
+
+    loads = [
+        pltpu.make_async_copy(source, target, arrived.at[n])
+        for n, (source, target) in enumerate(pieces(extended, (own, near, far), left, right))
+    ]
+    for load in loads:
+        load.start()
     total[...] = jnp.zeros(total.shape, F32)
     wave = (probe[0].astype(F32), probe[1].astype(F32))
     spread = (propagator[0], propagator[1])
+    for load in loads:
+        load.wait()
     for slot in range(2):
         row, col = (place[2 * slot], place[2 * slot + 1])
-
         low = row % 8
         base = pl.multiple_of(row - low, 8)
 
-        def window(index):
-            strip = extended[index, pl.ds(base, WIN + 8), :]
+        def window(layer, part):
+            strip = extended[layer, part, pl.ds(base, WIN + 8), :]
             return cut_rows(cut_lanes(strip, col), low)
 
-        layer0 = (window(0), window(1))
+        layer0 = (window(0, 0), window(0, 1))
         spectrum = forward(times(wave, layer0), tables)
         entering = inverse(times(spectrum, spread), tables)
-        layer1 = (window(2), window(3))
+        layer1 = (window(1, 0), window(1, 1))
         spectrum = forward(times(entering, layer1), tables)
         power = spectrum[0] * spectrum[0] + spectrum[1] * spectrum[1]
         misfit = weight[slot] * (power - intensity[slot])
@@ -176,36 +183,40 @@
         adjoint = inverse(conj_times(spread, spectrum), tables)
         term0 = conj_times(wave, adjoint)
         upstream = conj_times(layer0, adjoint)
+        blocks = out_probe.shape[0]
         for part in range(2):
+            shared = upstream[part].reshape(blocks, WIN // blocks, WIN)
             if slot == 0:
-                out_probe[part] = upstream[part]
+                out_probe[:, part] = shared
             else:
-                out_probe[part] += upstream[part]
-
-        def add_window(index, value):
-            total[index, pl.ds(base, WIN + 8), :] += put_lanes(put_rows(value, low), col)
+                out_probe[:, part] += shared
 
         for layer, term in ((0, term0), (1, term1)):
             for part in range(2):
-                add_window(2 * layer + part, term[part])
-    groups_out = ((far_top, (out_far_l, out_far, out_far_r)), (near_top, (out_near_l, out_near, out_near_r)), (HALF, (out_own_l, out_own, out_own_r)))
-    for top, trio in groups_out:
-        for k in range(3):
-            for layer in range(2):
-                for part in range(2):
-                    trio[k][layer, part] = total[2 * layer + part, pl.ds(top, HALF), k * HALF:(k + 1) * HALF]
-
-
-def work(place, weight, tiles, probe, propagator, intensity, tables):
+                total[layer, part, pl.ds(base, WIN + 8), :] += put_lanes(put_rows(term[part], low), col)
+    stores = [
+        pltpu.make_async_copy(source, target, left_sem.at[n])
+        for n, (target, source) in enumerate(pieces(total, (out_own, out_near, out_far), out_left, out_right))
+    ]
+    for store in stores:
+        store.start()
+    for store in stores:
+        store.wait()
+
+
+def work(place, weight, tiles, probe, propagator, intensity, tables, blocks):
     vmem = pl.BlockSpec(memory_space=pltpu.VMEM)
     smem = pl.BlockSpec(memory_space=pltpu.SMEM)
+    anywhere = pl.BlockSpec(memory_space=pl.ANY)
     tile = jax.ShapeDtypeStruct((2, 2, HALF, HALF), F32)
+    triple = jax.ShapeDtypeStruct((3, 2, 2, HALF, HALF), F32)
+    term = jax.ShapeDtypeStruct((blocks, 2, WIN // blocks, WIN), F32)
     return pl.pallas_call(
         work_kernel,
-        out_shape=[tile] * 9 + [jax.ShapeDtypeStruct((2, WIN, WIN), F32)],
-        in_specs=[smem, smem] + [vmem] * 13,
-        out_specs=[vmem] * 10,
-        scratch_shapes=[pltpu.VMEM((4, 3 * HALF, 3 * HALF), F32)] * 2,
+        out_shape=[tile] * 3 + [triple] * 2 + [term],
+        in_specs=[smem, smem] + [anywhere] * 5 + [vmem] * 4,
+        out_specs=[anywhere] * 5 + [vmem],
+        scratch_shapes=[pltpu.VMEM((2, 2, 3 * HALF, 3 * HALF), F32)] * 2 + [pltpu.SemaphoreType.DMA((9,))] * 2,
         compiler_params=pltpu.CompilerParams(vmem_limit_bytes=48 * 1024 * 1024),
         cost_estimate=pl.CostEstimate(flops=10_000_000_000, bytes_accessed=8_000_000, transcendentals=0),
     )(place, weight, *tiles, probe, propagator, intensity, tables)
@@ -219,46 +230,36 @@
     return [(j, i) for i, j in pairs]
 
 
-def sides(value):
-    ups = pairs_up(lax.axis_size("col"))
-    return lax.ppermute(value, "col", ups), lax.ppermute(value, "col", flipped(ups))
-
-
-def across(axis, bit):
-    return [(i, i ^ bit) for i in range(lax.axis_size(axis))]
-
-
-def probe_block(term):
-    row, col = (lax.axis_index("row"), lax.axis_index("col"))
+def probe_rows(term):
+    rows = lax.axis_size("row")
+    groups = [[2 * k + half for k in range(rows // 2)] for half in range(2)]
+    return lax.all_to_all(term, "row", 0, 0, tiled=True, axis_index_groups=groups)
+
+
+def probe_block(spread):
     rows, cols = (lax.axis_size("row"), lax.axis_size("col"))
-    bit = rows // 2
-    while bit >= 1:
-        size = term.shape[1] // 2
-        upper = (row // bit) % 2
-        first, second = (term[:, :size], term[:, size:])
-        kept = jnp.where(upper == 1, second, first)
-        sent = jnp.where(upper == 1, first, second)
-        term = kept + lax.ppermute(sent, "row", across("row", bit))
-        bit //= 2
-    bit = 1
-    while bit < cols:
-        term = term + lax.ppermute(term, "col", across("col", bit))
-        bit *= 2
-    width = WIN // cols
-    return lax.dynamic_slice(term, (0, 0, col * width), (2, term.shape[1], width))
+    pair = jnp.sum(spread, axis=0)
+    size = pair.shape[1] // 2
+    upper = lax.axis_index("row") % 2 == 1
+    first, second = (pair[:, :size], pair[:, size:])
+    swap = [(i, i ^ 1) for i in range(rows)]
+    mine = jnp.where(upper, second, first) + lax.ppermute(jnp.where(upper, first, second), "row", swap)
+    mine = mine.reshape(2, size, cols, WIN // cols).transpose(2, 0, 1, 3)
+    return jnp.sum(lax.all_to_all(mine, "col", 0, 0, tiled=True), axis=0)
 
 
 def per_device(object_slices, probe_wave, propagator_phase, intensity, centres, batch_order):
     rows = lax.axis_size("row")
     row, col = (lax.axis_index("row"), lax.axis_index("col"))
     hops = [(i, i + 2) for i in range(0, rows - 2, 2)] + [(i + 2, i) for i in range(1, rows - 2, 2)]
-    swap = across("row", 1)
+    swap = [(i, i ^ 1) for i in range(rows)]
+    ups = pairs_up(lax.axis_size("col"))
     near = lax.ppermute(object_slices, "row", swap)
-    own_l, own_r = sides(object_slices)
     far = lax.ppermute(near, "row", hops)
-    near_l, near_r = sides(near)
-    far_l, far_r = sides(far)
-    tiles = (object_slices, own_l, own_r, near, near_l, near_r, far, far_l, far_r)
+    stack = jnp.stack([object_slices, near, far])
+    left = lax.ppermute(stack, "col", ups)
+    right = lax.ppermute(stack, "col", flipped(ups))
+    tiles = (object_slices, near, far, left, right)
 
     order = order_matrix()
     angles = dot(dot(order, propagator_phase).astype(BF16), order.T)
@@ -271,18 +272,16 @@
         jnp.stack([2 * HALF * (1 - upper), 2 * HALF * upper]),
     ]).astype(jnp.int32)
     weight = (batch_order[0, 0] >= 0).astype(F32)
-    outs = work(place, weight, tiles, probe_wave, propagator, measured, half_tables())
-    own, own_l, own_r, near, near_l, near_r, far, far_l, far_r, probe_term = outs
-
-    ups = pairs_up(lax.axis_size("col"))
-
-    def fold(middle, left, right):
-        return middle + lax.ppermute(left, "col", flipped(ups)) + lax.ppermute(right, "col", ups)
-
-    far = fold(far, far_l, far_r)
-    near = fold(near, near_l, near_r) + lax.ppermute(far, "row", flipped(hops))
-    own = fold(own, own_l, own_r) + lax.ppermute(near, "row", swap)
-    return own, probe_block(probe_term)
+    outs = work(place, weight, tiles, probe_wave, propagator, measured, half_tables(), rows // 2)
+    own, near, far, left, right, probe_term = outs
+    from_right = lax.ppermute(left, "col", flipped(ups))
+    from_left = lax.ppermute(right, "col", ups)
+    spread = probe_rows(probe_term)
+    from_left, from_right, spread = lax.optimization_barrier((from_left, from_right, spread))
+    far = far + from_left[2] + from_right[2]
+    near = near + from_left[1] + from_right[1] + lax.ppermute(far, "row", flipped(hops))
+    own = own + from_left[0] + from_right[0] + lax.ppermute(near, "row", swap)
+    return own, probe_block(spread)
 
 
 def solution(mesh):

time: 190 us -> 157 us (0.83); the launches traced: 186 us -> 156 us
  blocking collectives: 0 us -> 45.8 us
  starting transfers between devices: 113 us -> 69.4 us
  waiting for transfers between devices: 42.3 us -> 17.9 us
  local copies, waits for them, and re-layouts: 13.5 us -> 3.44 us
  other arithmetic: 1.96 us -> 5.04 us
    all_to_all x0 -> x2, blocking collectives: none -> 45.8 us  [the longest x1 26.1 us: probe_block(): return jnp.sum(lax.all_to_all(mine, 'col', 0, 0, tiled=True), axis=0)]
    ppermute x23 -> x7, starting transfers between devices: 93 us -> 49.3 us  [the longest x1 21.8 us: per_device(): left = lax.ppermute(stack, 'col', ups)]
    ppermute x23 -> x7, waiting for transfers between devices: 42.3 us -> 9.17 us  [the longest x1 4.76 us: per_device(): left = lax.ppermute(stack, 'col', ups)]
    unnamed x56 -> x18, local copies, waits for them, and re-layouts: 13.3 us -> 2.62 us
    ppermute x1, waiting for transfers between devices: 0.01 us -> 5.58 us  [per_device(): near = lax.ppermute(object_slices, 'row', swap)]
    ppermute x1, waiting for transfers between devices: 0.01 us -> 3.18 us  [per_device(): far = lax.ppermute(near, 'row', hops)]
    another operation x0 -> x1, other arithmetic: none -> 1.92 us  [per_device(): stack = jnp.stack([object_slices, near, far])]
  transfers between devices with their start and end apart: 25 -> 9, of which waited for: 8 -> 4; matrix products, arithmetic and copies ran while one was open for 2% -> 3% of each run, Pallas kernels for 0% -> 0%
where the time goes in v2:
time: 157 us; the launch traced here: 156 us
  starting transfers between devices  69.4 us (44%)
  blocking collectives  45.8 us (29%)
  waiting for transfers between devices  17.9 us (11%)
  Pallas kernels  11.9 us (8%)
  other arithmetic  5.04 us (3%)
  local copies, waits for them, and re-layouts  3.44 us (2%)
    all_to_all x1, blocking collectives, probe_block(): return jnp.sum(lax.all_to_all(mine, 'col', 0, 0, tiled=True), axis=0)  26.1 us
    ppermute x1, starting transfers between devices, per_device(): left = lax.ppermute(stack, 'col', ups)  21.8 us
    all_to_all x1, blocking collectives, probe_rows(): lax.all_to_all(term, 'row', 0, 0, tiled=True, axis_index_groups=groups)  19.8 us
    ppermute x1, starting transfers between devices, per_device(): near = lax.ppermute(object_slices, 'row', swap)  16.4 us
    ppermute x1, starting transfers between devices, probe_block(): lax.ppermute(jnp.where(upper, first, second), 'row', swap)  14.5 us
    pallas_call x1, Pallas kernels, work(): pl.pallas_call(work_kernel, out_shape=[tile] * 3 + [triple] * 2 + [term],...  11.9 us
    ppermute x1, waiting for transfers between devices, per_device(): near = lax.ppermute(object_slices, 'row', swap)  5.58 us
    ppermute x1, starting transfers between devices, per_device(): own = own + from_left[0] + from_right[0] + lax.ppermute(near, 'row', swap)  5.35 us
  transfers between devices with their start and end apart: 9, of which 4 were waited for; matrix products, arithmetic and copies ran while one was open for 3% of the time, Pallas kernels for 0%

profile of v2, /device:TPU:1, one launch (start us, length us, event | category | flops | bytes accessed | tf_op | source)
XLA Modules:
  0.0 156.0 jit_solution(11855213032458519650)
XLA Ops:
  0.6 16.4 %collective-permute-start = (f32[2,2,128,128]{3,2,1,0:T(8,128)}, f32[2,2,128,128]{3,2,1,0:T(8,128)S(1)}, u32[]{:S(2)}, u32[]{:S(2)}) collective-permute-start(f32[2,2,128,128]{3,2,1,0:T(8,128)} %own.1), channel_id=1, source_target_pairs={{0,16},{16,0},{32,48},{48,32},{64,80},{80,64},{96,112},{112,96},{1... | collective-permute-start | bytes 786440 | tf_op jit(solution)/shard_map/ppermute | solution.py:257
  17.1 5.6 %collective-permute-done.near = f32[2,2,128,128]{3,2,1,0:T(8,128)S(1)} collective-permute-done((f32[2,2,128,128]{3,2,1,0:T(8,128)}, f32[2,2,128,128]{3,2,1,0:T(8,128)S(1)}, u32[]{:S(2)}, u32[]{:S(2)}) %collective-permute-start) | collective-permute-done | bytes 262176 | tf_op jit(solution)/shard_map/ppermute | solution.py:257
  22.6 3.8 %collective-permute-start.1 = (f32[2,2,128,128]{3,2,1,0:T(8,128)S(1)}, f32[2,2,128,128]{3,2,1,0:T(8,128)S(1)}, u32[]{:S(2)}, u32[]{:S(2)}) collective-permute-start(f32[2,2,128,128]{3,2,1,0:T(8,128)S(1)} %collective-permute-done.near), channel_id=1, source_target_pairs={{0,32},{32,64},{64,96},{96,128},{128,160},{160,192},{192,224},{224... | collective-permute-start | bytes 786440 | tf_op jit(solution)/shard_map/ppermute | solution.py:258
  26.5 0.1 sub.15
  26.6 0.6 copy-done.6
  27.3 3.2 %collective-permute-done.1.far = f32[2,2,128,128]{3,2,1,0:T(8,128)S(1)} collective-permute-done((f32[2,2,128,128]{3,2,1,0:T(8,128)S(1)}, f32[2,2,128,128]{3,2,1,0:T(8,128)S(1)}, u32[]{:S(2)}, u32[]{:S(2)}) %collective-permute-start.1) | collective-permute-done | bytes 262176 | tf_op jit(solution)/shard_map/ppermute | solution.py:258
  30.5 1.9 %pad_maximum_fusion = f32[3,2,2,128,128]{4,3,2,1,0:T(8,128)} fusion(f32[1,2,2,128,128]{4,3,2,1,0:T(8,128)S(1)} %bitcast.52, f32[1,2,2,128,128]{4,3,2,1,0:T(8,128)S(1)} %bitcast.51, f32[1,2,2,128,128]{4,3,2,1,0:T(8,128)} %bitcast.50), kind=kLoop, calls=%fused_computation.5 | loop fusion | flops 393216 | bytes 1572864 | tf_op jit(solution)/shard_map/stack | solution.py:259
  32.4 21.8 %collective-permute-start.2 = (f32[3,2,2,128,128]{4,3,2,1,0:T(8,128)}, f32[3,2,2,128,128]{4,3,2,1,0:T(8,128)S(1)}, u32[]{:S(2)}, u32[]{:S(2)}) collective-permute-start(f32[3,2,2,128,128]{4,3,2,1,0:T(8,128)} %pad_maximum_fusion), channel_id=1, source_target_pairs={{0,1},{1,2},{2,3},{3,4},{4,5},{5,6},{6,7},{7,8},{8,9},{9,10},{10,1... | collective-permute-start | bytes 2359304 | tf_op jit(solution)/shard_map/ppermute | solution.py:260
  54.2 1.9 %collective-permute-start.3 = (f32[3,2,2,128,128]{4,3,2,1,0:T(8,128)}, f32[3,2,2,128,128]{4,3,2,1,0:T(8,128)}, u32[]{:S(2)}, u32[]{:S(2)}) collective-permute-start(f32[3,2,2,128,128]{4,3,2,1,0:T(8,128)} %pad_maximum_fusion), channel_id=1, source_target_pairs={{1,0},{2,1},{3,2},{4,3},{5,4},{6,5},{7,6},{8,7},{9,8},{10,9},{11,1... | collective-permute-start | bytes 2359304 | tf_op jit(solution)/shard_map/ppermute | solution.py:261
  56.2 1.2 cosine_bitcast_fusion
  57.5 0.6 copy-done.7
  58.1 0.3 copy-done.4
  58.3 0.4 fusion.1.intensity
  58.7 4.8 %collective-permute-done.2.left = f32[3,2,2,128,128]{4,3,2,1,0:T(8,128)S(1)} collective-permute-done((f32[3,2,2,128,128]{4,3,2,1,0:T(8,128)}, f32[3,2,2,128,128]{4,3,2,1,0:T(8,128)S(1)}, u32[]{:S(2)}, u32[]{:S(2)}) %collective-permute-start.2) | collective-permute-done | bytes 786464 | tf_op jit(solution)/shard_map/ppermute | solution.py:260
  63.5 4.4 %collective-permute-done.3.right = f32[3,2,2,128,128]{4,3,2,1,0:T(8,128)} collective-permute-done((f32[3,2,2,128,128]{4,3,2,1,0:T(8,128)}, f32[3,2,2,128,128]{4,3,2,1,0:T(8,128)}, u32[]{:S(2)}, u32[]{:S(2)}) %collective-permute-start.3) | collective-permute-done | bytes 786464 | tf_op jit(solution)/shard_map/ppermute | solution.py:261
  67.9 0.9 copy-done.2
  68.8 11.9 %shard_map.95 = (f32[2,2,128,128]{3,2,1,0:T(8,128)S(1)}, f32[2,2,128,128]{3,2,1,0:T(8,128)S(1)}, f32[2,2,128,128]{3,2,1,0:T(8,128)S(1)}, f32[3,2,2,128,128]{4,3,...) custom-call(s32[6]{0:T(128)S(1)} %pad_add_fusion.1.place, f32[2]{0:T(128)S(1)} %fusion.7.weight, ...), custom_call_target="tpu_custom_call" | custom-call | flops 10000000000 | bytes 8000000 | tf_op jit(solution)/shard_map/pallas_call | solution.py:214
  80.8 1.9 %collective-permute-start.4 = (f32[3,2,2,128,128]{4,3,2,1,0:T(8,128)S(1)}, f32[3,2,2,128,128]{4,3,2,1,0:T(8,128)S(1)}, u32[]{:S(2)}, u32[]{:S(2)}) collective-permute-start(f32[3,2,2,128,128]{4,3,2,1,0:T(8,128)S(1)} %get-tuple-element.12), channel_id=1, source_target_pairs={{0,1},{1,2},{2,3},{3,4},{4,5},{5,6},{6,7},{7,8},{8,9},{9,10},{10,1... | collective-permute-start | bytes 2359304 | tf_op jit(solution)/shard_map/ppermute | solution.py:278
  82.7 2.5 %collective-permute-start.5 = (f32[3,2,2,128,128]{4,3,2,1,0:T(8,128)S(1)}, f32[3,2,2,128,128]{4,3,2,1,0:T(8,128)S(1)}, u32[]{:S(2)}, u32[]{:S(2)}) collective-permute-start(f32[3,2,2,128,128]{4,3,2,1,0:T(8,128)S(1)} %get-tuple-element.13), channel_id=1, source_target_pairs={{1,0},{2,1},{3,2},{4,3},{5,4},{6,5},{7,6},{8,7},{9,8},{10,9},{11,1... | collective-permute-start | bytes 2359304 | tf_op jit(solution)/shard_map/ppermute | solution.py:277
  85.2 19.8 %all_to_all.10 = f32[16,2,16,256]{3,2,1,0:T(8,128)S(1)} all-to-all(f32[16,2,16,256]{3,2,1,0:T(8,128)S(1)} %get-tuple-element.14), channel_id=1, replica_groups={{0,32,64,96,128,160,192,224,256,288,320,352,384,416,448,480},{16,48,80,..., dimensions={0} | all-to-all | bytes 1048576 | tf_op jit(solution)/shard_map/all_to_all | solution.py:236
  104.9 0.8 bitcast_add_fusion
  105.7 1.3 collective-permute-start.6
  107.0 14.5 %collective-permute-start.8 = (f32[2,8,256]{2,1,0:T(8,128)S(1)}, f32[2,8,256]{2,1,0:T(8,128)S(1)}, u32[]{:S(2)}, u32[]{:S(2)}) collective-permute-start(f32[2,8,256]{2,1,0:T(8,128)S(1)} %slice_select_fusion), channel_id=1, source_target_pairs={{0,16},{16,0},{32,48},{48,32},{64,80},{80,64},{96,112},{112,96},{1... | collective-permute-start | bytes 49160 | tf_op jit(solution)/shard_map/ppermute | solution.py:246
  121.6 5.3 %collective-permute-start.7 = (f32[2,2,128,128]{3,2,1,0:T(8,128)S(1)}, f32[2,2,128,128]{3,2,1,0:T(8,128)S(1)}, u32[]{:S(2)}, u32[]{:S(2)}) collective-permute-start(f32[2,2,128,128]{3,2,1,0:T(8,128)S(1)} %fusion.3), channel_id=1, source_target_pairs={{0,16},{16,0},{32,48},{48,32},{64,80},{80,64},{96,112},{112,96},{1... | collective-permute-start | bytes 786440 | tf_op jit(solution)/shard_map/ppermute | solution.py:283
  127.0 0.1 reshape.15
  127.1 0.1 reshape.18
  127.2 26.1 %all_to_all.11 = f32[16,1,256]{2,1,0:T(1,128)S(1)} all-to-all(f32[16,1,256]{2,1,0:T(1,128)S(1)} %reshape.18), channel_id=1, replica_groups=mesh['row'=32,'col'=16] {'col'}, dimensions={0} | all-to-all | bytes 32768 | tf_op jit(solution)/shard_map/all_to_all | solution.py:248
  153.3 0.5 broadcast.10
  153.8 0.7 reduce
  154.5 0.1 reshape.19
  154.6 0.6 reduce_sum.19
  155.2 0.8 fusion.4
  (29 shorter events, 0.5 us)
Async XLA Ops:
  0.6 57.5 %copy-start = (bf16[1,1,2,256,256]{4,3,2,1,0:T(8,128)(2,1)S(1)}, bf16[1,1,2,256,256]{4,3,2,1,0:T(8,128)(2,1)}, u32[]{:S(2)}) copy-start(bf16[1,1,2,256,256]{4,3,2,1,0:T(8,128)(2,1)} %param.11) | copy-start | bytes 786436
  0.6 22.0 %collective-permute-start = (f32[2,2,128,128]{3,2,1,0:T(8,128)}, f32[2,2,128,128]{3,2,1,0:T(8,128)S(1)}, u32[]{:S(2)}, u32[]{:S(2)}) collective-permute-start(f32[2,2,128,128]{3,2,1,0:T(8,128)} %own.1), channel_id=1, source_target_pairs={{0,16},{16,0},{32,48},{48,32},{64,80},{80,64},{96,112},{112,96},{1... | collective-permute-start | bytes 786440 | tf_op jit(solution)/shard_map/ppermute | solution.py:257
  22.6 7.8 %collective-permute-start.1 = (f32[2,2,128,128]{3,2,1,0:T(8,128)S(1)}, f32[2,2,128,128]{3,2,1,0:T(8,128)S(1)}, u32[]{:S(2)}, u32[]{:S(2)}) collective-permute-start(f32[2,2,128,128]{3,2,1,0:T(8,128)S(1)} %collective-permute-done.near), channel_id=1, source_target_pairs={{0,32},{32,64},{64,96},{96,128},{128,160},{160,192},{192,224},{224... | collective-permute-start | bytes 786440 | tf_op jit(solution)/shard_map/ppermute | solution.py:258
  26.5 0.7 copy-start.6
  30.5 25.8 %copy-start.3 = (bf16[256,256]{1,0:T(8,128)(2,1)S(1)}, bf16[256,256]{1,0:T(8,128)(2,1)}, u32[]{:S(2)}) copy-start(bf16[256,256]{1,0:T(8,128)(2,1)} %constant.36.clone) | copy-start | bytes 393220
  30.5 25.8 %copy-start.5 = (bf16[256,256]{1,0:T(8,128)(2,1)S(1)}, bf16[256,256]{1,0:T(8,128)(2,1)}, u32[]{:S(2)}) copy-start(bf16[256,256]{1,0:T(8,128)(2,1)} %param.10) | copy-start | bytes 393220
  32.4 31.1 %collective-permute-start.2 = (f32[3,2,2,128,128]{4,3,2,1,0:T(8,128)}, f32[3,2,2,128,128]{4,3,2,1,0:T(8,128)S(1)}, u32[]{:S(2)}, u32[]{:S(2)}) collective-permute-start(f32[3,2,2,128,128]{4,3,2,1,0:T(8,128)} %pad_maximum_fusion), channel_id=1, source_target_pairs={{0,1},{1,2},{2,3},{3,4},{4,5},{5,6},{6,7},{7,8},{8,9},{9,10},{10,1... | collective-permute-start | bytes 2359304 | tf_op jit(solution)/shard_map/ppermute | solution.py:260
  54.2 13.6 %collective-permute-start.3 = (f32[3,2,2,128,128]{4,3,2,1,0:T(8,128)}, f32[3,2,2,128,128]{4,3,2,1,0:T(8,128)}, u32[]{:S(2)}, u32[]{:S(2)}) collective-permute-start(f32[3,2,2,128,128]{4,3,2,1,0:T(8,128)} %pad_maximum_fusion), channel_id=1, source_target_pairs={{1,0},{2,1},{3,2},{4,3},{5,4},{6,5},{7,6},{8,7},{9,8},{10,9},{11,1... | collective-permute-start | bytes 2359304 | tf_op jit(solution)/shard_map/ppermute | solution.py:261
  57.4 0.7 copy-start.7
  57.4 0.9 copy-start.4
  58.3 9.5 %copy-start.1 = (f32[2,2,128,128]{3,2,1,0:T(8,128)S(1)}, f32[2,2,128,128]{3,2,1,0:T(8,128)}, u32[]{:S(2)}) copy-start(f32[2,2,128,128]{3,2,1,0:T(8,128)} %own.1) | copy-start | bytes 786436
  67.9 1.0 copy-start.2
  80.8 24.1 %collective-permute-start.4 = (f32[3,2,2,128,128]{4,3,2,1,0:T(8,128)S(1)}, f32[3,2,2,128,128]{4,3,2,1,0:T(8,128)S(1)}, u32[]{:S(2)}, u32[]{:S(2)}) collective-permute-start(f32[3,2,2,128,128]{4,3,2,1,0:T(8,128)S(1)} %get-tuple-element.12), channel_id=1, source_target_pairs={{0,1},{1,2},{2,3},{3,4},{4,5},{5,6},{6,7},{7,8},{8,9},{9,10},{10,1... | collective-permute-start | bytes 2359304 | tf_op jit(solution)/shard_map/ppermute | solution.py:278
  82.7 22.2 %collective-permute-start.5 = (f32[3,2,2,128,128]{4,3,2,1,0:T(8,128)S(1)}, f32[3,2,2,128,128]{4,3,2,1,0:T(8,128)S(1)}, u32[]{:S(2)}, u32[]{:S(2)}) collective-permute-start(f32[3,2,2,128,128]{4,3,2,1,0:T(8,128)S(1)} %get-tuple-element.13), channel_id=1, source_target_pairs={{1,0},{2,1},{3,2},{4,3},{5,4},{6,5},{7,6},{8,7},{9,8},{10,9},{11,1... | collective-permute-start | bytes 2359304 | tf_op jit(solution)/shard_map/ppermute | solution.py:277
  105.7 15.9 %collective-permute-start.6 = (f32[2,2,128,128]{3,2,1,0:T(8,128)}, f32[2,2,128,128]{3,2,1,0:T(8,128)S(1)}, u32[]{:S(2)}, u32[]{:S(2)}) collective-permute-start(f32[2,2,128,128]{3,2,1,0:T(8,128)} %bitcast_add_fusion), channel_id=1, source_target_pairs={{32,0},{64,32},{96,64},{128,96},{160,128},{192,160},{224,192},{256... | collective-permute-start | bytes 786440 | tf_op jit(solution)/shard_map/ppermute | solution.py:282
  107.0 19.9 %collective-permute-start.8 = (f32[2,8,256]{2,1,0:T(8,128)S(1)}, f32[2,8,256]{2,1,0:T(8,128)S(1)}, u32[]{:S(2)}, u32[]{:S(2)}) collective-permute-start(f32[2,8,256]{2,1,0:T(8,128)S(1)} %slice_select_fusion), channel_id=1, source_target_pairs={{0,16},{16,0},{32,48},{48,32},{64,80},{80,64},{96,112},{112,96},{1... | collective-permute-start | bytes 49160 | tf_op jit(solution)/shard_map/ppermute | solution.py:246
  121.6 33.6 %collective-permute-start.7 = (f32[2,2,128,128]{3,2,1,0:T(8,128)S(1)}, f32[2,2,128,128]{3,2,1,0:T(8,128)S(1)}, u32[]{:S(2)}, u32[]{:S(2)}) collective-permute-start(f32[2,2,128,128]{3,2,1,0:T(8,128)S(1)} %fusion.3), channel_id=1, source_target_pairs={{0,16},{16,0},{32,48},{48,32},{64,80},{80,64},{96,112},{112,96},{1... | collective-permute-start | bytes 786440 | tf_op jit(solution)/shard_map/ppermute | solution.py:283

commit v3 on v2

--- a/solution.py
+++ b/solution.py
@@ -139,50 +139,93 @@
     return jnp.where(kept, here, before).reshape(WIN + 8, value.shape[1])
 
 
-def work_kernel(place, weight, own, near, far, left, right, probe, propagator, intensity, tables,
-                out_own, out_near, out_far, out_left, out_right, out_probe, extended, total, arrived, left_sem):
+def pieces(place, field, middle, sibling, other):
     tops = (HALF, pl.multiple_of(place[4], HALF), pl.multiple_of(place[5], HALF))
-
-    def pieces(field, middle, before, after):
-        for k in range(3):
-            rows = pl.ds(tops[k], HALF)
-            yield middle[k], field.at[:, :, rows, HALF:2 * HALF]
-            yield before.at[k], field.at[:, :, rows, 0:HALF]
-            yield after.at[k], field.at[:, :, rows, 2 * HALF:3 * HALF]
-
-    loads = [
-        pltpu.make_async_copy(source, target, arrived.at[n])
-        for n, (source, target) in enumerate(pieces(extended, (own, near, far), left, right))
-    ]
+    for k in range(3):
+        rows = pl.ds(tops[k], HALF)
+        yield middle[k], field.at[:, rows, HALF:2 * HALF]
+        yield sibling[k], field.at[:, rows, pl.ds(pl.multiple_of(place[6], HALF), HALF)]
+        yield other[k], field.at[:, rows, pl.ds(pl.multiple_of(place[7], HALF), HALF)]
+
+
+def spot(place, slot):
+    row, col = (place[2 * slot], place[2 * slot + 1])
+    low = row % 8
+    return pl.multiple_of(row - low, 8), low, col
+
+
+def window(field, place, slot):
+    base, low, col = spot(place, slot)
+    strips = [field[part, pl.ds(base, WIN + 8), :] for part in range(2)]
+    return tuple(cut_rows(cut_lanes(strip, col), low) for strip in strips)
+
+
+def add_window(field, place, slot, term):
+    base, low, col = spot(place, slot)
+    for part in range(2):
+        field[part, pl.ds(base, WIN + 8), :] += put_lanes(put_rows(term[part], low), col)
+
+
+def assemble(place, field, layer, own, near, far, sibling, other, arrived):
+    middle = [tile.at[layer] for tile in (own, near, far)]
+    parts = pieces(place, field, middle, [sibling.at[k] for k in range(3)], [other.at[k] for k in range(3)])
+    return [pltpu.make_async_copy(a, b, arrived.at[n]) for n, (a, b) in enumerate(parts)]
+
+
+def front_kernel(place, own, near, far, sibling, other, probe, propagator, tables, out_wave, out_layer, field, arrived):
+    loads = assemble(place, field, 0, own, near, far, sibling, other, arrived)
     for load in loads:
         load.start()
-    total[...] = jnp.zeros(total.shape, F32)
     wave = (probe[0].astype(F32), probe[1].astype(F32))
     spread = (propagator[0], propagator[1])
     for load in loads:
         load.wait()
     for slot in range(2):
-        row, col = (place[2 * slot], place[2 * slot + 1])
-        low = row % 8
-        base = pl.multiple_of(row - low, 8)
-
-        def window(layer, part):
-            strip = extended[layer, part, pl.ds(base, WIN + 8), :]
-            return cut_rows(cut_lanes(strip, col), low)
-
-        layer0 = (window(0, 0), window(0, 1))
-        spectrum = forward(times(wave, layer0), tables)
+        layer = window(field, place, slot)
+        spectrum = forward(times(wave, layer), tables)
         entering = inverse(times(spectrum, spread), tables)
-        layer1 = (window(1, 0), window(1, 1))
-        spectrum = forward(times(entering, layer1), tables)
+        for part in range(2):
+            out_layer[slot, part] = layer[part]
+            out_wave[slot, part] = entering[part]
+
+
+def back_kernel(place, weight, own, near, far, sibling, other, waves, layers, probe, propagator, intensity, tables,
+                out_own, out_near, out_far, out_sibling, out_other, out_probe, field, total0, total1, kept, arrived, left_sem):
+    loads = assemble(place, field, 1, own, near, far, sibling, other, arrived)
+    for load in loads:
+        load.start()
+    totals = (total0, total1)
+
+    def stores(layer):
+        middle = [tile.at[layer] for tile in (out_own, out_near, out_far)]
+        sides = [[side.at[k, layer] for k in range(3)] for side in (out_sibling, out_other)]
+        parts = pieces(place, totals[layer], middle, *sides)
+        return [pltpu.make_async_copy(b, a, left_sem.at[layer, n]) for n, (a, b) in enumerate(parts)]
+
+    for total in totals:
+        total[...] = jnp.zeros(total.shape, F32)
+    spread = (propagator[0], propagator[1])
+    for load in loads:
+        load.wait()
+    for slot in range(2):
+        entering = (waves[slot, 0], waves[slot, 1])
+        layer = window(field, place, slot)
+        spectrum = forward(times(entering, layer), tables)
         power = spectrum[0] * spectrum[0] + spectrum[1] * spectrum[1]
         misfit = weight[slot] * (power - intensity[slot])
         adjoint = inverse((misfit * spectrum[0], misfit * spectrum[1]), tables)
-        term1 = conj_times(entering, adjoint)
-        spectrum = forward(conj_times(layer1, adjoint), tables)
+        add_window(total1, place, slot, conj_times(entering, adjoint))
+        upstream = conj_times(layer, adjoint)
+        for part in range(2):
+            kept[slot, part] = upstream[part]
+    for store in stores(1):
+        store.start()
+    wave = (probe[0].astype(F32), probe[1].astype(F32))
+    for slot in range(2):
+        spectrum = forward((kept[slot, 0], kept[slot, 1]), tables)
         adjoint = inverse(conj_times(spread, spectrum), tables)
-        term0 = conj_times(wave, adjoint)
-        upstream = conj_times(layer0, adjoint)
+        add_window(total0, place, slot, conj_times(wave, adjoint))
+        upstream = conj_times((layers[slot, 0], layers[slot, 1]), adjoint)
         blocks = out_probe.shape[0]
         for part in range(2):
             shared = upstream[part].reshape(blocks, WIN // blocks, WIN)
@@ -190,44 +233,66 @@
                 out_probe[:, part] = shared
             else:
                 out_probe[:, part] += shared
-
-        for layer, term in ((0, term0), (1, term1)):
-            for part in range(2):
-                total[layer, part, pl.ds(base, WIN + 8), :] += put_lanes(put_rows(term[part], low), col)
-    stores = [
-        pltpu.make_async_copy(source, target, left_sem.at[n])
-        for n, (target, source) in enumerate(pieces(total, (out_own, out_near, out_far), out_left, out_right))
-    ]
-    for store in stores:
+    for store in stores(0):
         store.start()
-    for store in stores:
-        store.wait()
-
-
-def work(place, weight, tiles, probe, propagator, intensity, tables, blocks):
-    vmem = pl.BlockSpec(memory_space=pltpu.VMEM)
-    smem = pl.BlockSpec(memory_space=pltpu.SMEM)
-    anywhere = pl.BlockSpec(memory_space=pl.ANY)
-    tile = jax.ShapeDtypeStruct((2, 2, HALF, HALF), F32)
-    triple = jax.ShapeDtypeStruct((3, 2, 2, HALF, HALF), F32)
-    term = jax.ShapeDtypeStruct((blocks, 2, WIN // blocks, WIN), F32)
+    for layer in range(2):
+        for store in stores(layer):
+            store.wait()
+
+
+VMEM = pl.BlockSpec(memory_space=pltpu.VMEM)
+SMEM = pl.BlockSpec(memory_space=pltpu.SMEM)
+ANYWHERE = pl.BlockSpec(memory_space=pl.ANY)
+
+
+def shaped(*shape):
+    return jax.ShapeDtypeStruct(shape, F32)
+
+
+def call(kernel, out_shape, in_specs, out_specs, scratch_shapes, flops):
     return pl.pallas_call(
-        work_kernel,
-        out_shape=[tile] * 3 + [triple] * 2 + [term],
-        in_specs=[smem, smem] + [anywhere] * 5 + [vmem] * 4,
-        out_specs=[anywhere] * 5 + [vmem],
-        scratch_shapes=[pltpu.VMEM((2, 2, 3 * HALF, 3 * HALF), F32)] * 2 + [pltpu.SemaphoreType.DMA((9,))] * 2,
-        compiler_params=pltpu.CompilerParams(vmem_limit_bytes=48 * 1024 * 1024),
-        cost_estimate=pl.CostEstimate(flops=10_000_000_000, bytes_accessed=8_000_000, transcendentals=0),
-    )(place, weight, *tiles, probe, propagator, intensity, tables)
-
-
-def pairs_up(count):
-    return [(i, i + 1) for i in range(count - 1)]
+        kernel,
+        out_shape=out_shape,
+        in_specs=in_specs,
+        out_specs=out_specs,
+        scratch_shapes=scratch_shapes,
+        compiler_params=pltpu.CompilerParams(vmem_limit_bytes=24 * 1024 * 1024),
+        cost_estimate=pl.CostEstimate(flops=flops, bytes_accessed=4_000_000, transcendentals=0),
+    )
+
+
+def front(place, tiles, probe, propagator, tables):
+    return call(
+        front_kernel,
+        [shaped(2, 2, WIN, WIN)] * 2,
+        [SMEM] + [ANYWHERE] * 5 + [VMEM] * 3,
+        [VMEM] * 2,
+        [pltpu.VMEM((2, 3 * HALF, 3 * HALF), F32), pltpu.SemaphoreType.DMA((9,))],
+        3_300_000_000,
+    )(place, *tiles, probe, propagator, tables)
+
+
+def back(place, weight, tiles, waves, layers, probe, propagator, intensity, tables, blocks):
+    return call(
+        back_kernel,
+        [shaped(2, 2, HALF, HALF)] * 3 + [shaped(3, 2, 2, HALF, HALF)] * 2 + [shaped(blocks, 2, WIN // blocks, WIN)],
+        [SMEM] * 2 + [ANYWHERE] * 5 + [VMEM] * 6,
+        [ANYWHERE] * 5 + [VMEM],
+        [pltpu.VMEM((2, 3 * HALF, 3 * HALF), F32)] * 3
+        + [pltpu.VMEM((2, 2, WIN, WIN), F32), pltpu.SemaphoreType.DMA((9,)), pltpu.SemaphoreType.DMA((2, 9))],
+        6_600_000_000,
+    )(place, weight, *tiles, waves, layers, probe, propagator, intensity, tables)
 
 
 def flipped(pairs):
     return [(j, i) for i, j in pairs]
+
+
+def sides(value):
+    cols = lax.axis_size("col")
+    inner = [(i, i + 1) for i in range(1, cols - 1, 2)]
+    other = lax.ppermute(value, "col", inner + flipped(inner))
+    return lax.ppermute(value, "col", [(i, i ^ 1) for i in range(cols)]), other
 
 
 def probe_rows(term):
@@ -236,16 +301,13 @@
     return lax.all_to_all(term, "row", 0, 0, tiled=True, axis_index_groups=groups)
 
 
-def probe_block(spread):
+def probe_block(pair):
     rows, cols = (lax.axis_size("row"), lax.axis_size("col"))
-    pair = jnp.sum(spread, axis=0)
-    size = pair.shape[1] // 2
-    upper = lax.axis_index("row") % 2 == 1
-    first, second = (pair[:, :size], pair[:, size:])
-    swap = [(i, i ^ 1) for i in range(rows)]
-    mine = jnp.where(upper, second, first) + lax.ppermute(jnp.where(upper, first, second), "row", swap)
-    mine = mine.reshape(2, size, cols, WIN // cols).transpose(2, 0, 1, 3)
-    return jnp.sum(lax.all_to_all(mine, "col", 0, 0, tiled=True), axis=0)
+    size, width = (WIN // rows, WIN // cols)
+    parts = pair.reshape(2, 2, size, cols, width).transpose(1, 3, 0, 2, 4).reshape(2 * cols, 2, size, width)
+    groups = [[(2 * k + half) * cols + c for half in range(2) for c in range(cols)] for k in range(rows // 2)]
+    gathered = lax.all_to_all(parts, ("row", "col"), 0, 0, tiled=True, axis_index_groups=groups)
+    return jnp.sum(gathered, axis=0)
 
 
 def per_device(object_slices, probe_wave, propagator_phase, intensity, centres, batch_order):
@@ -253,35 +315,39 @@
     row, col = (lax.axis_index("row"), lax.axis_index("col"))
     hops = [(i, i + 2) for i in range(0, rows - 2, 2)] + [(i + 2, i) for i in range(1, rows - 2, 2)]
     swap = [(i, i ^ 1) for i in range(rows)]
-    ups = pairs_up(lax.axis_size("col"))
     near = lax.ppermute(object_slices, "row", swap)
     far = lax.ppermute(near, "row", hops)
-    stack = jnp.stack([object_slices, near, far])
-    left = lax.ppermute(stack, "col", ups)
-    right = lax.ppermute(stack, "col", flipped(ups))
-    tiles = (object_slices, near, far, left, right)
+    stacks = lax.optimization_barrier([jnp.stack([object_slices[k], near[k], near[k]]) for k in range(2)])
+    sent = [lax.dynamic_update_slice(stacks[k], far[k][None], (2, 0, 0, 0)) for k in range(2)]
+    sides0, sides1 = (sides(sent[0]), sides(sent[1]))
 
     order = order_matrix()
     angles = dot(dot(order, propagator_phase).astype(BF16), order.T)
     propagator = jnp.stack([jnp.cos(angles), jnp.sin(angles)])
     middle = jnp.einsum("ab,sbc->sac", order, intensity[0, 0], preferred_element_type=F32).astype(BF16)
     measured = jnp.einsum("sac,dc->sad", middle, order, preferred_element_type=F32)
-    upper = row % 2
+    upper, odd = (row % 2, col % 2)
     place = jnp.concatenate([
         (centres[0, 0] - jnp.stack([row * HALF, col * HALF])).reshape(4),
-        jnp.stack([2 * HALF * (1 - upper), 2 * HALF * upper]),
+        2 * HALF * jnp.stack([1 - upper, upper, 1 - odd, odd]),
     ]).astype(jnp.int32)
     weight = (batch_order[0, 0] >= 0).astype(F32)
-    outs = work(place, weight, tiles, probe_wave, propagator, measured, half_tables(), rows // 2)
-    own, near, far, left, right, probe_term = outs
-    from_right = lax.ppermute(left, "col", flipped(ups))
-    from_left = lax.ppermute(right, "col", ups)
+    tables = half_tables()
+    tiles = (object_slices, near, far)
+    waves, layers = front(place, tiles + sides0, probe_wave, propagator, tables)
+    outs = back(place, weight, tiles + sides1, waves, layers, probe_wave, propagator, measured, tables, rows // 2)
+    own, near, far, to_sibling, to_other, probe_term = outs
+    cols = lax.axis_size("col")
+    inner = [(i, i + 1) for i in range(1, cols - 1, 2)]
+    other = lax.ppermute(to_other, "col", inner + flipped(inner))
+    sibling = lax.ppermute(to_sibling, "col", [(i, i ^ 1) for i in range(cols)])
     spread = probe_rows(probe_term)
-    from_left, from_right, spread = lax.optimization_barrier((from_left, from_right, spread))
-    far = far + from_left[2] + from_right[2]
-    near = near + from_left[1] + from_right[1] + lax.ppermute(far, "row", flipped(hops))
-    own = own + from_left[0] + from_right[0] + lax.ppermute(near, "row", swap)
-    return own, probe_block(spread)
+    sibling, other, spread = lax.optimization_barrier((sibling, other, spread))
+    far = lax.ppermute(far + sibling[2] + other[2], "row", flipped(hops))
+    far, pair = lax.optimization_barrier((far, jnp.sum(spread, axis=0)))
+    near = near + sibling[1] + other[1] + far
+    own = own + sibling[0] + other[0] + lax.ppermute(near, "row", swap)
+    return own, probe_block(pair)
 
 
 def solution(mesh):

time: 157 us -> 149 us (0.949)
  starting transfers between devices: 69.4 us -> 65.7 us
  waiting for transfers between devices: 17.9 us -> 14.8 us
  local copies, waits for them, and re-layouts: 3.44 us -> 5.22 us
    ppermute x1, waiting for transfers between devices: 5.58 us -> 1.74 us  [per_device(): near = lax.ppermute(object_slices, 'row', swap)]
    ppermute x7 -> x8, starting transfers between devices: 49.3 us -> 45.5 us  [the longest x2 21.8 us: sides(): other = lax.ppermute(value, 'col', inner + flipped(inner))]
    ppermute x7 -> x8, waiting for transfers between devices: 9.17 us -> 10 us  [the longest x1 8.26 us: per_device(): far = lax.ppermute(far + sibling[2] + other[2], 'row', flipped(hops))]
    pallas_call x1 -> x2, Pallas kernels: 11.9 us -> 11.8 us  [the longest x1 7.94 us: back(): call(back_kernel, [shaped(2, 2, HALF, HALF)] * 3 + [shaped(3, 2, 2, HALF,...]
  transfers between devices with their start and end apart: 9 -> 10, of which waited for: 4 -> 4; matrix products, arithmetic and copies ran while one was open for 3% -> 4% of each run, Pallas kernels for 0% -> 3%
where the time goes in v3:
time: 149 us
  starting transfers between devices  65.7 us (44%)
  blocking collectives  44.5 us (30%)
  waiting for transfers between devices  14.8 us (10%)
  Pallas kernels  11.8 us (8%)
  local copies, waits for them, and re-layouts  5.22 us (4%)
  other arithmetic  3.52 us (2%)
  matrix products  2.55 us (2%)
    all_to_all x1, blocking collectives, probe_block(): lax.all_to_all(parts, ('row', 'col'), 0, 0, tiled=True, axis_index_groups...  25.8 us
    ppermute x2, starting transfers between devices, sides(): other = lax.ppermute(value, 'col', inner + flipped(inner))  21.8 us
    all_to_all x1, blocking collectives, probe_rows(): lax.all_to_all(term, 'row', 0, 0, tiled=True, axis_index_groups=groups)  18.7 us
    ppermute x1, starting transfers between devices, per_device(): near = lax.ppermute(object_slices, 'row', swap)  16.4 us
    ppermute x1, starting transfers between devices, per_device(): own = own + sibling[0] + other[0] + lax.ppermute(near, 'row', swap)  11.7 us
    ppermute x1, waiting for transfers between devices, per_device(): far = lax.ppermute(far + sibling[2] + other[2], 'row', flipped(hops))  8.26 us
    pallas_call x1, Pallas kernels, back(): call(back_kernel, [shaped(2, 2, HALF, HALF)] * 3 + [shaped(3, 2, 2, HALF,...  7.94 us
    ppermute x2, starting transfers between devices, sides(): lax.ppermute(value, 'col', [(i, i ^ 1) for i in range(cols)])  6.26 us
  transfers between devices with their start and end apart: 10, of which 4 were waited for; matrix products, arithmetic and copies ran while one was open for 4% of the time, Pallas kernels for 3%

profile of v3, /device:TPU:1, one launch (start us, length us, event | category | flops | bytes accessed | tf_op | source)
XLA Modules:
  0.0 148.9 jit_solution(5783625975353357573)
XLA Ops:
  0.6 16.4 %collective-permute-start = (f32[2,2,128,128]{3,2,1,0:T(8,128)}, f32[2,2,128,128]{3,2,1,0:T(8,128)S(1)}, u32[]{:S(2)}, u32[]{:S(2)}) collective-permute-start(f32[2,2,128,128]{3,2,1,0:T(8,128)} %own.3), channel_id=1, source_target_pairs={{0,16},{16,0},{32,48},{48,32},{64,80},{80,64},{96,112},{112,96},{1... | collective-permute-start | bytes 786440 | tf_op jit(solution)/shard_map/ppermute | solution.py:318
  17.1 0.6 copy-done.7
  17.7 2.2 %cosine_bitcast_fusion = (f32[1,256,256]{2,1,0:T(8,128)S(1)}, f32[1,256,256]{2,1,0:T(8,128)S(1)}) fusion(bf16[256,256]{1,0:T(8,128)(2,1)} %constant.39.clone, bf16[256,256]{1,0:T(8,128)(2,1)} %param.10), kind=kOutput, calls=%fused_computation.18 | convolution fusion | flops 67174400 | bytes 786432 | tf_op jit(solution)/shard_map/dot_general | solution.py:47
  20.1 0.8 copy-done.1
  20.9 1.7 %collective-permute-done.near = f32[2,2,128,128]{3,2,1,0:T(8,128)S(1)} collective-permute-done((f32[2,2,128,128]{3,2,1,0:T(8,128)}, f32[2,2,128,128]{3,2,1,0:T(8,128)S(1)}, u32[]{:S(2)}, u32[]{:S(2)}) %collective-permute-start) | collective-permute-done | bytes 262176 | tf_op jit(solution)/shard_map/ppermute | solution.py:318
  22.6 3.8 %collective-permute-start.1 = (f32[2,2,128,128]{3,2,1,0:T(8,128)S(1)}, f32[2,2,128,128]{3,2,1,0:T(8,128)S(1)}, u32[]{:S(2)}, u32[]{:S(2)}) collective-permute-start(f32[2,2,128,128]{3,2,1,0:T(8,128)S(1)} %collective-permute-done.near), channel_id=1, source_target_pairs={{0,32},{32,64},{64,96},{96,128},{128,160},{160,192},{192,224},{224... | collective-permute-start | bytes 786440 | tf_op jit(solution)/shard_map/ppermute | solution.py:319
  26.4 1.0 pad_maximum_fusion.1
  27.4 3.0 %collective-permute-done.1.far = f32[2,2,128,128]{3,2,1,0:T(8,128)S(1)} collective-permute-done((f32[2,2,128,128]{3,2,1,0:T(8,128)S(1)}, f32[2,2,128,128]{3,2,1,0:T(8,128)S(1)}, u32[]{:S(2)}, u32[]{:S(2)}) %collective-permute-start.1) | collective-permute-done | bytes 262176 | tf_op jit(solution)/shard_map/ppermute | solution.py:319
  30.5 0.7 slice_dynamic-update-slice_fusion
  31.2 4.3 %collective-permute-start.4 = (f32[3,2,128,128]{3,2,1,0:T(8,128)}, f32[3,2,128,128]{3,2,1,0:T(8,128)S(1)}, u32[]{:S(2)}, u32[]{:S(2)}) collective-permute-start(f32[3,2,128,128]{3,2,1,0:T(8,128)} %get-tuple-element.34), channel_id=1, source_target_pairs={{0,1},{1,0},{2,3},{3,2},{4,5},{5,4},{6,7},{7,6},{8,9},{9,8},{10,11... | collective-permute-start | bytes 1179656 | tf_op jit(solution)/shard_map/ppermute | solution.py:295
  35.5 19.4 %collective-permute-start.5 = (f32[3,2,128,128]{3,2,1,0:T(8,128)}, f32[3,2,128,128]{3,2,1,0:T(8,128)S(1)}, u32[]{:S(2)}, u32[]{:S(2)}) collective-permute-start(f32[3,2,128,128]{3,2,1,0:T(8,128)} %get-tuple-element.34), channel_id=1, source_target_pairs={{1,2},{3,4},{5,6},{7,8},{9,10},{11,12},{13,14},{2,1},{4,3},{6,5},{... | collective-permute-start | bytes 1179656 | tf_op jit(solution)/shard_map/ppermute | solution.py:294
  55.1 0.6 copy-done.6
  55.8 0.4 fusion.1.intensity
  56.2 1.9 %collective-permute-start.2 = (f32[3,2,128,128]{3,2,1,0:T(8,128)}, f32[3,2,128,128]{3,2,1,0:T(8,128)S(1)}, u32[]{:S(2)}, u32[]{:S(2)}) collective-permute-start(f32[3,2,128,128]{3,2,1,0:T(8,128)} %get-tuple-element.35), channel_id=1, source_target_pairs={{0,1},{1,0},{2,3},{3,2},{4,5},{5,4},{6,7},{7,6},{8,9},{9,8},{10,11... | collective-permute-start | bytes 1179656 | tf_op jit(solution)/shard_map/ppermute | solution.py:295
  58.1 2.4 %collective-permute-start.3 = (f32[3,2,128,128]{3,2,1,0:T(8,128)}, f32[3,2,128,128]{3,2,1,0:T(8,128)S(1)}, u32[]{:S(2)}, u32[]{:S(2)}) collective-permute-start(f32[3,2,128,128]{3,2,1,0:T(8,128)} %get-tuple-element.35), channel_id=1, source_target_pairs={{1,2},{3,4},{5,6},{7,8},{9,10},{11,12},{13,14},{2,1},{4,3},{6,5},{... | collective-permute-start | bytes 1179656 | tf_op jit(solution)/shard_map/ppermute | solution.py:294
  60.6 1.2 copy-done.3
  61.9 3.8 %shard_map.95 = (f32[2,2,256,256]{3,2,1,0:T(8,128)S(1)}, f32[2,2,256,256]{3,2,1,0:T(8,128)S(1)}) custom-call(s32[8]{0:T(128)S(1)} %pad_add_fusion.1.place, f32[2,2,128,128]{3,2,1,0:T(8,128)S(1)} %copy-done.1, f32[2,2,128,128]{3,2,1,0:T(8,128)S(1)} %collective-permute-done.near, f32[2,2,128,128]{3,2,1,0:T(8,128)S(1)} %collective-permute-done.1.far, ...), custom_call_target="tpu_custom_call" | custom-call | flops 3300000000 | bytes 4000000 | tf_op jit(solution)/shard_map/pallas_call | solution.py:265
  65.7 1.7 %collective-permute-done.3.other = f32[3,2,128,128]{3,2,1,0:T(8,128)S(1)} collective-permute-done((f32[3,2,128,128]{3,2,1,0:T(8,128)}, f32[3,2,128,128]{3,2,1,0:T(8,128)S(1)}, u32[]{:S(2)}, u32[]{:S(2)}) %collective-permute-start.3) | collective-permute-done | bytes 393248 | tf_op jit(solution)/shard_map/ppermute | solution.py:294
  67.4 7.9 %shard_map.96 = (f32[2,2,128,128]{3,2,1,0:T(8,128)S(1)}, f32[2,2,128,128]{3,2,1,0:T(8,128)S(1)}, f32[2,2,128,128]{3,2,1,0:T(8,128)S(1)}, f32[3,2,2,128,128]{4,3,...) custom-call(s32[8]{0:T(128)S(1)} %pad_add_fusion.1.place, f32[2]{0:T(128)S(1)} %fusion.7.weight, ...), custom_call_target="tpu_custom_call" | custom-call | flops 6600000000 | bytes 4000000 | tf_op jit(solution)/shard_map/pallas_call | solution.py:276
  75.4 1.9 %collective-permute-start.6 = (f32[3,2,2,128,128]{4,3,2,1,0:T(8,128)S(1)}, f32[3,2,2,128,128]{4,3,2,1,0:T(8,128)S(1)}, u32[]{:S(2)}, u32[]{:S(2)}) collective-permute-start(f32[3,2,2,128,128]{4,3,2,1,0:T(8,128)S(1)} %get-tuple-element.22), channel_id=1, source_target_pairs={{0,1},{1,0},{2,3},{3,2},{4,5},{5,4},{6,7},{7,6},{8,9},{9,8},{10,11... | collective-permute-start | bytes 2359304 | tf_op jit(solution)/shard_map/ppermute | solution.py:343
  77.3 2.5 %collective-permute-start.7 = (f32[3,2,2,128,128]{4,3,2,1,0:T(8,128)S(1)}, f32[3,2,2,128,128]{4,3,2,1,0:T(8,128)S(1)}, u32[]{:S(2)}, u32[]{:S(2)}) collective-permute-start(f32[3,2,2,128,128]{4,3,2,1,0:T(8,128)S(1)} %get-tuple-element.23), channel_id=1, source_target_pairs={{1,2},{3,4},{5,6},{7,8},{9,10},{11,12},{13,14},{2,1},{4,3},{6,5},{... | collective-permute-start | bytes 2359304 | tf_op jit(solution)/shard_map/ppermute | solution.py:342
  79.8 18.7 %all_to_all.10 = f32[16,2,16,256]{3,2,1,0:T(8,128)S(1)} all-to-all(f32[16,2,16,256]{3,2,1,0:T(8,128)S(1)} %get-tuple-element.24), channel_id=1, replica_groups={{0,32,64,96,128,160,192,224,256,288,320,352,384,416,448,480},{16,48,80,..., dimensions={0} | all-to-all | bytes 1048576 | tf_op jit(solution)/shard_map/all_to_all | solution.py:301
  98.6 1.3 collective-permute-start.8
  100.0 8.3 %collective-permute-done.8 = f32[2,2,128,128]{3,2,1,0:T(8,128)S(1)} collective-permute-done((f32[2,2,128,128]{3,2,1,0:T(8,128)S(1)}, f32[2,2,128,128]{3,2,1,0:T(8,128)S(1)}, u32[]{:S(2)}, u32[]{:S(2)}) %collective-permute-start.8) | collective-permute-done | bytes 262176 | tf_op jit(solution)/shard_map/ppermute | solution.py:346
  108.3 11.7 %collective-permute-start.9 = (f32[2,2,128,128]{3,2,1,0:T(8,128)S(1)}, f32[2,2,128,128]{3,2,1,0:T(8,128)S(1)}, u32[]{:S(2)}, u32[]{:S(2)}) collective-permute-start(f32[2,2,128,128]{3,2,1,0:T(8,128)S(1)} %fusion.3), channel_id=1, source_target_pairs={{0,16},{16,0},{32,48},{48,32},{64,80},{80,64},{96,112},{112,96},{1... | collective-permute-start | bytes 786440 | tf_op jit(solution)/shard_map/ppermute | solution.py:349
  120.0 0.1 reshape.18
  120.2 0.1 reshape.22
  120.4 25.8 %all_to_all.11 = f32[32,1,256]{2,1,0:T(1,128)S(1)} all-to-all(f32[32,1,256]{2,1,0:T(1,128)S(1)} %reshape.22), channel_id=1, replica_groups={{0,1,2,3,4,5,6,7,8,9,10,11,12,13,14,15,16,17,18,19,20,21,22,23,24,25,26..., dimensions={0} | all-to-all | bytes 65536 | tf_op jit(solution)/shard_map/all_to_all | solution.py:309
  146.2 0.5 broadcast.16
  146.7 0.7 reduce
  147.5 0.6 reduce_sum.19
  148.2 0.8 fusion.4
  (34 shorter events, 0.9 us)
Async XLA Ops:
  0.6 55.2 %copy-start = (bf16[1,1,2,256,256]{4,3,2,1,0:T(8,128)(2,1)S(1)}, bf16[1,1,2,256,256]{4,3,2,1,0:T(8,128)(2,1)}, u32[]{:S(2)}) copy-start(bf16[1,1,2,256,256]{4,3,2,1,0:T(8,128)(2,1)} %param.11) | copy-start | bytes 786436
  0.6 22.0 %collective-permute-start = (f32[2,2,128,128]{3,2,1,0:T(8,128)}, f32[2,2,128,128]{3,2,1,0:T(8,128)S(1)}, u32[]{:S(2)}, u32[]{:S(2)}) collective-permute-start(f32[2,2,128,128]{3,2,1,0:T(8,128)} %own.3), channel_id=1, source_target_pairs={{0,16},{16,0},{32,48},{48,32},{64,80},{80,64},{96,112},{112,96},{1... | collective-permute-start | bytes 786440 | tf_op jit(solution)/shard_map/ppermute | solution.py:318
  17.1 0.7 copy-start.7
  19.9 1.0 copy-start.1
  22.6 7.8 %collective-permute-start.1 = (f32[2,2,128,128]{3,2,1,0:T(8,128)S(1)}, f32[2,2,128,128]{3,2,1,0:T(8,128)S(1)}, u32[]{:S(2)}, u32[]{:S(2)}) collective-permute-start(f32[2,2,128,128]{3,2,1,0:T(8,128)S(1)} %collective-permute-done.near), channel_id=1, source_target_pairs={{0,32},{32,64},{64,96},{96,128},{128,160},{160,192},{192,224},{224... | collective-permute-start | bytes 786440 | tf_op jit(solution)/shard_map/ppermute | solution.py:319
  30.5 25.4 %copy-start.5 = (bf16[256,256,1]{1,0,2:T(8,128)(2,1)S(1)}, bf16[256,256,1]{1,0,2:T(8,128)(2,1)}, u32[]{:S(2)}) copy-start(bf16[256,256,1]{1,0,2:T(8,128)(2,1)} %constant.44) | copy-start | bytes 393220
  31.2 29.4 %collective-permute-start.4 = (f32[3,2,128,128]{3,2,1,0:T(8,128)}, f32[3,2,128,128]{3,2,1,0:T(8,128)S(1)}, u32[]{:S(2)}, u32[]{:S(2)}) collective-permute-start(f32[3,2,128,128]{3,2,1,0:T(8,128)} %get-tuple-element.34), channel_id=1, source_target_pairs={{0,1},{1,0},{2,3},{3,2},{4,5},{5,4},{6,7},{7,6},{8,9},{9,8},{10,11... | collective-permute-start | bytes 1179656 | tf_op jit(solution)/shard_map/ppermute | solution.py:295
  35.5 25.1 %collective-permute-start.5 = (f32[3,2,128,128]{3,2,1,0:T(8,128)}, f32[3,2,128,128]{3,2,1,0:T(8,128)S(1)}, u32[]{:S(2)}, u32[]{:S(2)}) collective-permute-start(f32[3,2,128,128]{3,2,1,0:T(8,128)} %get-tuple-element.34), channel_id=1, source_target_pairs={{1,2},{3,4},{5,6},{7,8},{9,10},{11,12},{13,14},{2,1},{4,3},{6,5},{... | collective-permute-start | bytes 1179656 | tf_op jit(solution)/shard_map/ppermute | solution.py:294
  55.1 0.7 copy-start.6
  55.8 4.8 %copy-start.2 = (bf16[2,256,256]{2,1,0:T(8,128)(2,1)S(1)}, bf16[2,256,256]{2,1,0:T(8,128)(2,1)}, u32[]{:S(2)}) copy-start(bf16[2,256,256]{2,1,0:T(8,128)(2,1)} %probe.3) | copy-start | bytes 786436
  56.2 9.5 %collective-permute-start.2 = (f32[3,2,128,128]{3,2,1,0:T(8,128)}, f32[3,2,128,128]{3,2,1,0:T(8,128)S(1)}, u32[]{:S(2)}, u32[]{:S(2)}) collective-permute-start(f32[3,2,128,128]{3,2,1,0:T(8,128)} %get-tuple-element.35), channel_id=1, source_target_pairs={{0,1},{1,0},{2,3},{3,2},{4,5},{5,4},{6,7},{7,6},{8,9},{9,8},{10,11... | collective-permute-start | bytes 1179656 | tf_op jit(solution)/shard_map/ppermute | solution.py:295
  58.1 9.3 %collective-permute-start.3 = (f32[3,2,128,128]{3,2,1,0:T(8,128)}, f32[3,2,128,128]{3,2,1,0:T(8,128)S(1)}, u32[]{:S(2)}, u32[]{:S(2)}) collective-permute-start(f32[3,2,128,128]{3,2,1,0:T(8,128)} %get-tuple-element.35), channel_id=1, source_target_pairs={{1,2},{3,4},{5,6},{7,8},{9,10},{11,12},{13,14},{2,1},{4,3},{6,5},{... | collective-permute-start | bytes 1179656 | tf_op jit(solution)/shard_map/ppermute | solution.py:294
  60.6 1.2 copy-start.3
  61.9 5.6 %copy-start.4 = (bf16[4,2,256,256]{3,2,1,0:T(8,128)(2,1)S(1)}, bf16[4,2,256,256]{3,2,1,0:T(8,128)(2,1)}, u32[]{:S(2)}) copy-start(bf16[4,2,256,256]{3,2,1,0:T(8,128)(2,1)} %constant.40.clone.tables) | copy-start | bytes 3145732
  75.4 23.2 %collective-permute-start.6 = (f32[3,2,2,128,128]{4,3,2,1,0:T(8,128)S(1)}, f32[3,2,2,128,128]{4,3,2,1,0:T(8,128)S(1)}, u32[]{:S(2)}, u32[]{:S(2)}) collective-permute-start(f32[3,2,2,128,128]{4,3,2,1,0:T(8,128)S(1)} %get-tuple-element.22), channel_id=1, source_target_pairs={{0,1},{1,0},{2,3},{3,2},{4,5},{5,4},{6,7},{7,6},{8,9},{9,8},{10,11... | collective-permute-start | bytes 2359304 | tf_op jit(solution)/shard_map/ppermute | solution.py:343
  77.3 21.3 %collective-permute-start.7 = (f32[3,2,2,128,128]{4,3,2,1,0:T(8,128)S(1)}, f32[3,2,2,128,128]{4,3,2,1,0:T(8,128)S(1)}, u32[]{:S(2)}, u32[]{:S(2)}) collective-permute-start(f32[3,2,2,128,128]{4,3,2,1,0:T(8,128)S(1)} %get-tuple-element.23), channel_id=1, source_target_pairs={{1,2},{3,4},{5,6},{7,8},{9,10},{11,12},{13,14},{2,1},{4,3},{6,5},{... | collective-permute-start | bytes 2359304 | tf_op jit(solution)/shard_map/ppermute | solution.py:342
  98.6 9.6 %collective-permute-start.8 = (f32[2,2,128,128]{3,2,1,0:T(8,128)S(1)}, f32[2,2,128,128]{3,2,1,0:T(8,128)S(1)}, u32[]{:S(2)}, u32[]{:S(2)}) collective-permute-start(f32[2,2,128,128]{3,2,1,0:T(8,128)S(1)} %bitcast_add_fusion), channel_id=1, source_target_pairs={{32,0},{64,32},{96,64},{128,96},{160,128},{192,160},{224,192},{256... | collective-permute-start | bytes 786440 | tf_op jit(solution)/shard_map/ppermute | solution.py:346
  108.3 39.9 %collective-permute-start.9 = (f32[2,2,128,128]{3,2,1,0:T(8,128)S(1)}, f32[2,2,128,128]{3,2,1,0:T(8,128)S(1)}, u32[]{:S(2)}, u32[]{:S(2)}) collective-permute-start(f32[2,2,128,128]{3,2,1,0:T(8,128)S(1)} %fusion.3), channel_id=1, source_target_pairs={{0,16},{16,0},{32,48},{48,32},{64,80},{80,64},{96,112},{112,96},{1... | collective-permute-start | bytes 786440 | tf_op jit(solution)/shard_map/ppermute | solution.py:349

commit v4 on v3

--- a/solution.py
+++ b/solution.py
@@ -50,13 +50,17 @@
 def right_mul(value, table_ref, index):
     high, low = split(value)
     table = table_ref[index, 0]
-    return dot(high, table) + (dot(low, table) + dot(high, table_ref[index, 1]))
+    both = dot(join(high, low, 0), table)
+    size = value.shape[0]
+    return both[:size] + (both[size:] + dot(high, table_ref[index, 1]))
 
 
 def left_mul(table_ref, index, value):
     high, low = split(value)
     table = table_ref[index, 0]
-    return dot(table, high) + (dot(table, low) + dot(table_ref[index, 1], high))
+    both = dot(join(table, table_ref[index, 1], 0), high)
+    size = table.shape[0]
+    return both[:size] + (dot(table, low) + both[size:])
 
 
 def join(first, second, axis):
@@ -69,36 +73,49 @@
     return value[:, :HALF], value[:, HALF:]
 
 
-def forward_axis(field, tables, axis):
-    (re0, re1), (im0, im1) = (halves(field[0], axis), halves(field[1], axis))
-    even = join(re0 + re1, im0 + im1, axis)
-    odd = join(re0 - re1, im0 - im1, axis)
+def mul_all(values, tables, index, axis):
     if axis == 1:
-        even, odd = (right_mul(even, tables, 0), right_mul(odd, tables, 2))
-    else:
-        even, odd = (left_mul(tables, 1, even), left_mul(tables, 3, odd))
-    (re0, im0), (re1, im1) = (halves(even, axis), halves(odd, axis))
-    return (join(re0, re1, axis), join(im0, im1, axis))
-
-
-def inverse_axis(field, tables, axis):
-    (re0, re1), (im0, im1) = (halves(field[0], axis), halves(field[1], axis))
-    even = join(re0, im0, axis)
-    odd = join(re1, im1, axis)
-    if axis == 1:
-        even, odd = (right_mul(even, tables, 1), right_mul(odd, tables, 3))
-    else:
-        even, odd = (left_mul(tables, 0, even), left_mul(tables, 2, odd))
-    (re0, im0), (re1, im1) = (halves(even, axis), halves(odd, axis))
-    return (join(re0 + re1, re0 - re1, axis), join(im0 + im1, im0 - im1, axis))
-
-
-def forward(field, tables):
-    return forward_axis(forward_axis(field, tables, 1), tables, 0)
-
-
-def inverse(field, tables):
-    return inverse_axis(inverse_axis(field, tables, 0), tables, 1)
+        out = right_mul(jnp.concatenate(values, axis=0), tables, index)
+        return [out[n * WIN:(n + 1) * WIN] for n in range(len(values))]
+    return [left_mul(tables, index, value) for value in values]
+
+
+def forward_axis(fields, tables, axis):
+    evens, odds = ([], [])
+    for field in fields:
+        (re0, re1), (im0, im1) = (halves(field[0], axis), halves(field[1], axis))
+        evens.append(join(re0 + re1, im0 + im1, axis))
+        odds.append(join(re0 - re1, im0 - im1, axis))
+    evens = mul_all(evens, tables, 0 if axis == 1 else 1, axis)
+    odds = mul_all(odds, tables, 2 if axis == 1 else 3, axis)
+    outs = []
+    for even, odd in zip(evens, odds):
+        (re0, im0), (re1, im1) = (halves(even, axis), halves(odd, axis))
+        outs.append((join(re0, re1, axis), join(im0, im1, axis)))
+    return outs
+
+
+def inverse_axis(fields, tables, axis):
+    evens, odds = ([], [])
+    for field in fields:
+        (re0, re1), (im0, im1) = (halves(field[0], axis), halves(field[1], axis))
+        evens.append(join(re0, im0, axis))
+        odds.append(join(re1, im1, axis))
+    evens = mul_all(evens, tables, 1 if axis == 1 else 0, axis)
+    odds = mul_all(odds, tables, 3 if axis == 1 else 2, axis)
+    outs = []
+    for even, odd in zip(evens, odds):
+        (re0, im0), (re1, im1) = (halves(even, axis), halves(odd, axis))
+        outs.append((join(re0 + re1, re0 - re1, axis), join(im0 + im1, im0 - im1, axis)))
+    return outs
+
+
+def forward(fields, tables):
+    return forward_axis(forward_axis(fields, tables, 1), tables, 0)
+
+
+def inverse(fields, tables):
+    return inverse_axis(inverse_axis(fields, tables, 0), tables, 1)
 
 
 def times(left, right):
@@ -180,13 +197,13 @@
     spread = (propagator[0], propagator[1])
     for load in loads:
         load.wait()
+    layers = [window(field, place, slot) for slot in range(2)]
+    spectra = forward([times(wave, layer) for layer in layers], tables)
+    entering = inverse([times(spectrum, spread) for spectrum in spectra], tables)
     for slot in range(2):
-        layer = window(field, place, slot)
-        spectrum = forward(times(wave, layer), tables)
-        entering = inverse(times(spectrum, spread), tables)
         for part in range(2):
-            out_layer[slot, part] = layer[part]
-            out_wave[slot, part] = entering[part]
+            out_layer[slot, part] = layers[slot][part]
+            out_wave[slot, part] = entering[slot][part]
 
 
 def back_kernel(place, weight, own, near, far, sibling, other, waves, layers, probe, propagator, intensity, tables,
@@ -207,34 +224,33 @@
     spread = (propagator[0], propagator[1])
     for load in loads:
         load.wait()
-    for slot in range(2):
-        entering = (waves[slot, 0], waves[slot, 1])
-        layer = window(field, place, slot)
-        spectrum = forward(times(entering, layer), tables)
+    two = range(2)
+    spectra = forward([times((waves[slot, 0], waves[slot, 1]), window(field, place, slot)) for slot in two], tables)
+    fields = []
+    for slot in two:
+        spectrum = spectra[slot]
         power = spectrum[0] * spectrum[0] + spectrum[1] * spectrum[1]
         misfit = weight[slot] * (power - intensity[slot])
-        adjoint = inverse((misfit * spectrum[0], misfit * spectrum[1]), tables)
-        add_window(total1, place, slot, conj_times(entering, adjoint))
-        upstream = conj_times(layer, adjoint)
+        fields.append((misfit * spectrum[0], misfit * spectrum[1]))
+    adjoint = inverse(fields, tables)
+    for slot in two:
+        add_window(total1, place, slot, conj_times((waves[slot, 0], waves[slot, 1]), adjoint[slot]))
+        upstream = conj_times(window(field, place, slot), adjoint[slot])
         for part in range(2):
             kept[slot, part] = upstream[part]
     for store in stores(1):
         store.start()
     wave = (probe[0].astype(F32), probe[1].astype(F32))
-    for slot in range(2):
-        spectrum = forward((kept[slot, 0], kept[slot, 1]), tables)
-        adjoint = inverse(conj_times(spread, spectrum), tables)
-        add_window(total0, place, slot, conj_times(wave, adjoint))
-        upstream = conj_times((layers[slot, 0], layers[slot, 1]), adjoint)
-        blocks = out_probe.shape[0]
-        for part in range(2):
-            shared = upstream[part].reshape(blocks, WIN // blocks, WIN)
-            if slot == 0:
-                out_probe[:, part] = shared
-            else:
-                out_probe[:, part] += shared
+    spectra = forward([(kept[slot, 0], kept[slot, 1]) for slot in two], tables)
+    adjoint = inverse([conj_times(spread, spectrum) for spectrum in spectra], tables)
+    for slot in two:
+        add_window(total0, place, slot, conj_times(wave, adjoint[slot]))
     for store in stores(0):
         store.start()
+    upstream = [conj_times((layers[slot, 0], layers[slot, 1]), adjoint[slot]) for slot in two]
+    blocks = out_probe.shape[0]
+    for part in range(2):
+        out_probe[:, part] = (upstream[0][part] + upstream[1][part]).reshape(blocks, WIN // blocks, WIN)
     for layer in range(2):
         for store in stores(layer):
             store.wait()
@@ -301,13 +317,14 @@
     return lax.all_to_all(term, "row", 0, 0, tiled=True, axis_index_groups=groups)
 
 
-def probe_block(pair):
+def probe_block(pair, own):
     rows, cols = (lax.axis_size("row"), lax.axis_size("col"))
     size, width = (WIN // rows, WIN // cols)
-    parts = pair.reshape(2, 2, size, cols, width).transpose(1, 3, 0, 2, 4).reshape(2 * cols, 2, size, width)
+    parts = pair.reshape(2, 2, size, cols, width).transpose(1, 3, 0, 2, 4).reshape(2 * cols, 2, size * width)
     groups = [[(2 * k + half) * cols + c for half in range(2) for c in range(cols)] for k in range(rows // 2)]
     gathered = lax.all_to_all(parts, ("row", "col"), 0, 0, tiled=True, axis_index_groups=groups)
-    return jnp.sum(gathered, axis=0)
+    own, gathered = lax.optimization_barrier((own, gathered))
+    return own, jnp.sum(gathered, axis=0).reshape(2, size, width)
 
 
 def per_device(object_slices, probe_wave, propagator_phase, intensity, centres, batch_order):
@@ -342,12 +359,11 @@
     other = lax.ppermute(to_other, "col", inner + flipped(inner))
     sibling = lax.ppermute(to_sibling, "col", [(i, i ^ 1) for i in range(cols)])
     spread = probe_rows(probe_term)
-    sibling, other, spread = lax.optimization_barrier((sibling, other, spread))
     far = lax.ppermute(far + sibling[2] + other[2], "row", flipped(hops))
-    far, pair = lax.optimization_barrier((far, jnp.sum(spread, axis=0)))
+    pair = jnp.sum(spread, axis=0)
     near = near + sibling[1] + other[1] + far
     own = own + sibling[0] + other[0] + lax.ppermute(near, "row", swap)
-    return own, probe_block(pair)
+    return probe_block(pair, own)
 
 
 def solution(mesh):

time: 149 us -> 143 us (0.960)
  blocking collectives: 44.5 us -> 0 us
  starting transfers between devices: 65.7 us -> 89.6 us
  waiting for transfers between devices: 14.8 us -> 30.1 us
    all_to_all x2 -> x0, blocking collectives: 44.5 us -> none  [the longest x1 25.8 us: probe_block(): lax.all_to_all(parts, ('row', 'col'), 0, 0, tiled=True, axis_index_groups...]
    all_to_all x0 -> x2, starting transfers between devices: none -> 21.6 us  [the longest x1 12.1 us: probe_block(): lax.all_to_all(parts, ('row', 'col'), 0, 0, tiled=True, axis_index_groups...]
    all_to_all x0 -> x2, waiting for transfers between devices: none -> 14.5 us  [the longest x1 14.5 us: probe_block(): lax.all_to_all(parts, ('row', 'col'), 0, 0, tiled=True, axis_index_groups...]
    ppermute x1, waiting for transfers between devices: 0.01 us -> 9.97 us  [per_device(): other = lax.ppermute(to_other, 'col', inner + flipped(inner))]
    ppermute x1, waiting for transfers between devices: 8.26 us -> 0.01 us  [per_device(): far = lax.ppermute(far + sibling[2] + other[2], 'row', flipped(hops))]
    ppermute x2, starting transfers between devices: 6.26 us -> 3.84 us  [sides(): lax.ppermute(value, 'col', [(i, i ^ 1) for i in range(cols)])]
    ppermute x1, starting transfers between devices: 11.7 us -> 13.7 us  [per_device(): own = own + sibling[0] + other[0] + lax.ppermute(near, 'row', swap)]
    ppermute x2, starting transfers between devices: 21.8 us -> 23.8 us  [sides(): other = lax.ppermute(value, 'col', inner + flipped(inner))]
  transfers between devices with their start and end apart: 10 -> 12, of which waited for: 4 -> 5; matrix products, arithmetic and copies ran while one was open for 4% -> 4% of each run, Pallas kernels for 3% -> 2%
where the time goes in v4:
time: 143 us; the launch traced here: 142 us
  starting transfers between devices  89.6 us (63%)
  waiting for transfers between devices  30.1 us (21%)
  Pallas kernels  11.1 us (8%)
  local copies, waits for them, and re-layouts  5.84 us (4%)
  matrix products  2.55 us (2%)
  other arithmetic  2.19 us (2%)
    ppermute x2, starting transfers between devices, sides(): other = lax.ppermute(value, 'col', inner + flipped(inner))  23.8 us
    ppermute x1, starting transfers between devices, per_device(): near = lax.ppermute(object_slices, 'row', swap)  16.4 us
    all_to_all x1, waiting for transfers between devices, probe_block(): lax.all_to_all(parts, ('row', 'col'), 0, 0, tiled=True, axis_index_groups...  14.5 us
    ppermute x1, starting transfers between devices, per_device(): own = own + sibling[0] + other[0] + lax.ppermute(near, 'row', swap)  13.7 us
    all_to_all x1, starting transfers between devices, probe_block(): lax.all_to_all(parts, ('row', 'col'), 0, 0, tiled=True, axis_index_groups...  12.1 us
    ppermute x1, waiting for transfers between devices, per_device(): other = lax.ppermute(to_other, 'col', inner + flipped(inner))  9.97 us
    all_to_all x1, starting transfers between devices, probe_rows(): lax.all_to_all(term, 'row', 0, 0, tiled=True, axis_index_groups=groups)  9.5 us
    pallas_call x1, Pallas kernels, back(): call(back_kernel, [shaped(2, 2, HALF, HALF)] * 3 + [shaped(3, 2, 2, HALF,...  7.83 us
  transfers between devices with their start and end apart: 12, of which 5 were waited for; matrix products, arithmetic and copies ran while one was open for 4% of the time, Pallas kernels for 2%

profile of v4, /device:TPU:1, one launch (start us, length us, event | category | flops | bytes accessed | tf_op | source)
XLA Modules:
  0.0 142.3 jit_solution(5711880809737412179)
XLA Ops:
  0.6 16.4 %collective-permute-start = (f32[2,2,128,128]{3,2,1,0:T(8,128)}, f32[2,2,128,128]{3,2,1,0:T(8,128)S(1)}, u32[]{:S(2)}, u32[]{:S(2)}) collective-permute-start(f32[2,2,128,128]{3,2,1,0:T(8,128)} %own.3), channel_id=1, source_target_pairs={{0,16},{16,0},{32,48},{48,32},{64,80},{80,64},{96,112},{112,96},{1... | collective-permute-start | bytes 786440 | tf_op jit(solution)/shard_map/ppermute | solution.py:335
  17.1 0.6 copy-done.7
  17.7 2.2 %cosine_bitcast_fusion = (f32[1,256,256]{2,1,0:T(8,128)S(1)}, f32[1,256,256]{2,1,0:T(8,128)S(1)}) fusion(bf16[256,256]{1,0:T(8,128)(2,1)} %constant.39.clone, bf16[256,256]{1,0:T(8,128)(2,1)} %param.10), kind=kOutput, calls=%fused_computation.24 | convolution fusion | flops 67174400 | bytes 786432 | tf_op jit(solution)/shard_map/dot_general | solution.py:47
  20.1 0.8 copy-done.1
  20.9 1.7 %collective-permute-done.near = f32[2,2,128,128]{3,2,1,0:T(8,128)S(1)} collective-permute-done((f32[2,2,128,128]{3,2,1,0:T(8,128)}, f32[2,2,128,128]{3,2,1,0:T(8,128)S(1)}, u32[]{:S(2)}, u32[]{:S(2)}) %collective-permute-start) | collective-permute-done | bytes 262176 | tf_op jit(solution)/shard_map/ppermute | solution.py:335
  22.6 3.8 %collective-permute-start.1 = (f32[2,2,128,128]{3,2,1,0:T(8,128)S(1)}, f32[2,2,128,128]{3,2,1,0:T(8,128)S(1)}, u32[]{:S(2)}, u32[]{:S(2)}) collective-permute-start(f32[2,2,128,128]{3,2,1,0:T(8,128)S(1)} %collective-permute-done.near), channel_id=1, source_target_pairs={{0,32},{32,64},{64,96},{96,128},{128,160},{160,192},{192,224},{224... | collective-permute-start | bytes 786440 | tf_op jit(solution)/shard_map/ppermute | solution.py:336
  26.4 1.0 pad_maximum_fusion.1
  27.4 3.0 %collective-permute-done.1.far = f32[2,2,128,128]{3,2,1,0:T(8,128)S(1)} collective-permute-done((f32[2,2,128,128]{3,2,1,0:T(8,128)S(1)}, f32[2,2,128,128]{3,2,1,0:T(8,128)S(1)}, u32[]{:S(2)}, u32[]{:S(2)}) %collective-permute-start.1) | collective-permute-done | bytes 262176 | tf_op jit(solution)/shard_map/ppermute | solution.py:336
  30.5 0.7 slice_dynamic-update-slice_fusion
  31.2 21.8 %collective-permute-start.5 = (f32[3,2,128,128]{3,2,1,0:T(8,128)}, f32[3,2,128,128]{3,2,1,0:T(8,128)S(1)}, u32[]{:S(2)}, u32[]{:S(2)}) collective-permute-start(f32[3,2,128,128]{3,2,1,0:T(8,128)} %get-tuple-element.28), channel_id=1, source_target_pairs={{1,2},{3,4},{5,6},{7,8},{9,10},{11,12},{13,14},{2,1},{4,3},{6,5},{... | collective-permute-start | bytes 1179656 | tf_op jit(solution)/shard_map/ppermute | solution.py:310
  53.0 1.9 %collective-permute-start.4 = (f32[3,2,128,128]{3,2,1,0:T(8,128)}, f32[3,2,128,128]{3,2,1,0:T(8,128)S(1)}, u32[]{:S(2)}, u32[]{:S(2)}) collective-permute-start(f32[3,2,128,128]{3,2,1,0:T(8,128)} %get-tuple-element.28), channel_id=1, source_target_pairs={{0,1},{1,0},{2,3},{3,2},{4,5},{5,4},{6,7},{7,6},{8,9},{9,8},{10,11... | collective-permute-start | bytes 1179656 | tf_op jit(solution)/shard_map/ppermute | solution.py:311
  55.0 0.6 copy-done.6
  55.7 0.1 sub.18
  55.8 0.4 fusion.1.intensity
  56.2 1.9 %collective-permute-start.3 = (f32[3,2,128,128]{3,2,1,0:T(8,128)}, f32[3,2,128,128]{3,2,1,0:T(8,128)S(1)}, u32[]{:S(2)}, u32[]{:S(2)}) collective-permute-start(f32[3,2,128,128]{3,2,1,0:T(8,128)} %get-tuple-element.29), channel_id=1, source_target_pairs={{1,2},{3,4},{5,6},{7,8},{9,10},{11,12},{13,14},{2,1},{4,3},{6,5},{... | collective-permute-start | bytes 1179656 | tf_op jit(solution)/shard_map/ppermute | solution.py:310
  58.1 1.9 %collective-permute-start.2 = (f32[3,2,128,128]{3,2,1,0:T(8,128)}, f32[3,2,128,128]{3,2,1,0:T(8,128)S(1)}, u32[]{:S(2)}, u32[]{:S(2)}) collective-permute-start(f32[3,2,128,128]{3,2,1,0:T(8,128)} %get-tuple-element.29), channel_id=1, source_target_pairs={{0,1},{1,0},{2,3},{3,2},{4,5},{5,4},{6,7},{7,6},{8,9},{9,8},{10,11... | collective-permute-start | bytes 1179656 | tf_op jit(solution)/shard_map/ppermute | solution.py:311
  60.1 1.2 copy-done.3
  61.4 3.3 %shard_map.95 = (f32[2,2,256,256]{3,2,1,0:T(8,128)S(1)}, f32[2,2,256,256]{3,2,1,0:T(8,128)S(1)}) custom-call(s32[8]{0:T(128)S(1)} %pad_add_fusion.1.place, f32[2,2,128,128]{3,2,1,0:T(8,128)S(1)} %copy-done.1, f32[2,2,128,128]{3,2,1,0:T(8,128)S(1)} %collective-permute-done.near, f32[2,2,128,128]{3,2,1,0:T(8,128)S(1)} %collective-permute-done.1.far, ...), custom_call_target="tpu_custom_call" | custom-call | flops 3300000000 | bytes 4000000 | tf_op jit(solution)/shard_map/pallas_call | solution.py:281
  64.6 0.9 collective-permute-done.3.other
  65.5 7.8 %shard_map.96 = (f32[2,2,128,128]{3,2,1,0:T(8,128)S(1)}, f32[2,2,128,128]{3,2,1,0:T(8,128)S(1)}, f32[2,2,128,128]{3,2,1,0:T(8,128)S(1)}, f32[3,2,2,128,128]{4,3,...) custom-call(s32[8]{0:T(128)S(1)} %pad_add_fusion.1.place, f32[2]{0:T(128)S(1)} %fusion.13.weight, ...), custom_call_target="tpu_custom_call" | custom-call | flops 6600000000 | bytes 4000000 | tf_op jit(solution)/shard_map/pallas_call | solution.py:292
  73.3 1.9 %collective-permute-start.6 = (f32[3,2,2,128,128]{4,3,2,1,0:T(8,128)S(1)}, f32[3,2,2,128,128]{4,3,2,1,0:T(8,128)S(1)}, u32[]{:S(2)}, u32[]{:S(2)}) collective-permute-start(f32[3,2,2,128,128]{4,3,2,1,0:T(8,128)S(1)} %get-tuple-element.19), channel_id=1, source_target_pairs={{0,1},{1,0},{2,3},{3,2},{4,5},{5,4},{6,7},{7,6},{8,9},{9,8},{10,11... | collective-permute-start | bytes 2359304 | tf_op jit(solution)/shard_map/ppermute | solution.py:360
  75.3 3.3 %collective-permute-start.7 = (f32[3,2,2,128,128]{4,3,2,1,0:T(8,128)S(1)}, f32[3,2,2,128,128]{4,3,2,1,0:T(8,128)S(1)}, u32[]{:S(2)}, u32[]{:S(2)}) collective-permute-start(f32[3,2,2,128,128]{4,3,2,1,0:T(8,128)S(1)} %get-tuple-element.20), channel_id=1, source_target_pairs={{1,2},{3,4},{5,6},{7,8},{9,10},{11,12},{13,14},{2,1},{4,3},{6,5},{... | collective-permute-start | bytes 2359304 | tf_op jit(solution)/shard_map/ppermute | solution.py:359
  78.6 10.0 %collective-permute-done.7 = f32[3,2,2,128,128]{4,3,2,1,0:T(8,128)S(1)} collective-permute-done((f32[3,2,2,128,128]{4,3,2,1,0:T(8,128)S(1)}, f32[3,2,2,128,128]{4,3,2,1,0:T(8,128)S(1)}, u32[]{:S(2)}, u32[]{:S(2)}) %collective-permute-start.7) | collective-permute-done | bytes 786464 | tf_op jit(solution)/shard_map/ppermute | solution.py:359
  88.6 1.3 collective-permute-start.8
  89.9 9.5 %all-to-all-start = ((f32[16,2,16,256]{3,2,1,0:T(8,128)}), f32[16,2,16,256]{3,2,1,0:T(8,128)S(1)}, u32[]{:S(2)}, u32[]{:S(2)}) async-start(f32[16,2,16,256]{3,2,1,0:T(8,128)} %get-tuple-element.23), calls=%async_computation | async-start | bytes 1048576 | tf_op jit(solution)/shard_map/all_to_all | solution.py:317
  99.5 13.7 %collective-permute-start.9 = (f32[2,2,128,128]{3,2,1,0:T(8,128)S(1)}, f32[2,2,128,128]{3,2,1,0:T(8,128)S(1)}, u32[]{:S(2)}, u32[]{:S(2)}) collective-permute-start(f32[2,2,128,128]{3,2,1,0:T(8,128)S(1)} %fusion.6), channel_id=1, source_target_pairs={{0,16},{16,0},{32,48},{48,32},{64,80},{80,64},{96,112},{112,96},{1... | collective-permute-start | bytes 786440 | tf_op jit(solution)/shard_map/ppermute | solution.py:365
  113.3 0.1 reshape.21
  113.5 0.7 reshape.26
  114.2 12.1 %all-to-all-start.1 = ((f32[32,2,128]{2,1,0:T(2,128)}), f32[32,2,128]{2,1,0:T(2,128)S(1)}, u32[]{:S(2)}, u32[]{:S(2)}) async-start(f32[32,2,128]{2,1,0:T(2,128)} %reshape.26), calls=%async_computation.1 | async-start | bytes 65536 | tf_op jit(solution)/shard_map/all_to_all | solution.py:325
  126.4 0.8 fusion.9
  127.1 14.5 %all-to-all-done.1 = f32[32,2,128]{2,1,0:T(2,128)S(1)} async-done(((f32[32,2,128]{2,1,0:T(2,128)}), f32[32,2,128]{2,1,0:T(2,128)S(1)}, u32[]{:S(2)}, u32[]{:S(2)}) %all-to-all-start.1) | async-done | bytes 32800 | tf_op jit(solution)/shard_map/all_to_all | solution.py:325
  141.6 0.7 reshape.23
  (34 shorter events, 0.7 us)
Async XLA Ops:
  0.6 55.2 %copy-start = (bf16[1,1,2,256,256]{4,3,2,1,0:T(8,128)(2,1)S(1)}, bf16[1,1,2,256,256]{4,3,2,1,0:T(8,128)(2,1)}, u32[]{:S(2)}) copy-start(bf16[1,1,2,256,256]{4,3,2,1,0:T(8,128)(2,1)} %param.11) | copy-start | bytes 786436
  0.6 22.0 %collective-permute-start = (f32[2,2,128,128]{3,2,1,0:T(8,128)}, f32[2,2,128,128]{3,2,1,0:T(8,128)S(1)}, u32[]{:S(2)}, u32[]{:S(2)}) collective-permute-start(f32[2,2,128,128]{3,2,1,0:T(8,128)} %own.3), channel_id=1, source_target_pairs={{0,16},{16,0},{32,48},{48,32},{64,80},{80,64},{96,112},{112,96},{1... | collective-permute-start | bytes 786440 | tf_op jit(solution)/shard_map/ppermute | solution.py:335
  17.1 0.7 copy-start.7
  19.9 1.0 copy-start.1
  22.6 7.8 %collective-permute-start.1 = (f32[2,2,128,128]{3,2,1,0:T(8,128)S(1)}, f32[2,2,128,128]{3,2,1,0:T(8,128)S(1)}, u32[]{:S(2)}, u32[]{:S(2)}) collective-permute-start(f32[2,2,128,128]{3,2,1,0:T(8,128)S(1)} %collective-permute-done.near), channel_id=1, source_target_pairs={{0,32},{32,64},{64,96},{96,128},{128,160},{160,192},{192,224},{224... | collective-permute-start | bytes 786440 | tf_op jit(solution)/shard_map/ppermute | solution.py:336
  30.5 25.4 %copy-start.5 = (bf16[256,256,1]{1,0,2:T(8,128)(2,1)S(1)}, bf16[256,256,1]{1,0,2:T(8,128)(2,1)}, u32[]{:S(2)}) copy-start(bf16[256,256,1]{1,0,2:T(8,128)(2,1)} %constant.44) | copy-start | bytes 393220
  31.2 28.9 %collective-permute-start.5 = (f32[3,2,128,128]{3,2,1,0:T(8,128)}, f32[3,2,128,128]{3,2,1,0:T(8,128)S(1)}, u32[]{:S(2)}, u32[]{:S(2)}) collective-permute-start(f32[3,2,128,128]{3,2,1,0:T(8,128)} %get-tuple-element.28), channel_id=1, source_target_pairs={{1,2},{3,4},{5,6},{7,8},{9,10},{11,12},{13,14},{2,1},{4,3},{6,5},{... | collective-permute-start | bytes 1179656 | tf_op jit(solution)/shard_map/ppermute | solution.py:310
  53.0 7.1 %collective-permute-start.4 = (f32[3,2,128,128]{3,2,1,0:T(8,128)}, f32[3,2,128,128]{3,2,1,0:T(8,128)S(1)}, u32[]{:S(2)}, u32[]{:S(2)}) collective-permute-start(f32[3,2,128,128]{3,2,1,0:T(8,128)} %get-tuple-element.28), channel_id=1, source_target_pairs={{0,1},{1,0},{2,3},{3,2},{4,5},{5,4},{6,7},{7,6},{8,9},{9,8},{10,11... | collective-permute-start | bytes 1179656 | tf_op jit(solution)/shard_map/ppermute | solution.py:311
  55.0 0.7 copy-start.6
  55.8 4.3 %copy-start.2 = (bf16[2,256,256]{2,1,0:T(8,128)(2,1)S(1)}, bf16[2,256,256]{2,1,0:T(8,128)(2,1)}, u32[]{:S(2)}) copy-start(bf16[2,256,256]{2,1,0:T(8,128)(2,1)} %probe.3) | copy-start | bytes 786436
  56.2 9.3 %collective-permute-start.3 = (f32[3,2,128,128]{3,2,1,0:T(8,128)}, f32[3,2,128,128]{3,2,1,0:T(8,128)S(1)}, u32[]{:S(2)}, u32[]{:S(2)}) collective-permute-start(f32[3,2,128,128]{3,2,1,0:T(8,128)} %get-tuple-element.29), channel_id=1, source_target_pairs={{1,2},{3,4},{5,6},{7,8},{9,10},{11,12},{13,14},{2,1},{4,3},{6,5},{... | collective-permute-start | bytes 1179656 | tf_op jit(solution)/shard_map/ppermute | solution.py:310
  58.1 7.4 %collective-permute-start.2 = (f32[3,2,128,128]{3,2,1,0:T(8,128)}, f32[3,2,128,128]{3,2,1,0:T(8,128)S(1)}, u32[]{:S(2)}, u32[]{:S(2)}) collective-permute-start(f32[3,2,128,128]{3,2,1,0:T(8,128)} %get-tuple-element.29), channel_id=1, source_target_pairs={{0,1},{1,0},{2,3},{3,2},{4,5},{5,4},{6,7},{7,6},{8,9},{9,8},{10,11... | collective-permute-start | bytes 1179656 | tf_op jit(solution)/shard_map/ppermute | solution.py:311
  60.1 1.2 copy-start.3
  61.4 4.1 %copy-start.4 = (bf16[4,2,256,256]{3,2,1,0:T(8,128)(2,1)S(1)}, bf16[4,2,256,256]{3,2,1,0:T(8,128)(2,1)}, u32[]{:S(2)}) copy-start(bf16[4,2,256,256]{3,2,1,0:T(8,128)(2,1)} %constant.40.clone.tables) | copy-start | bytes 3145732
  73.3 5.3 %collective-permute-start.6 = (f32[3,2,2,128,128]{4,3,2,1,0:T(8,128)S(1)}, f32[3,2,2,128,128]{4,3,2,1,0:T(8,128)S(1)}, u32[]{:S(2)}, u32[]{:S(2)}) collective-permute-start(f32[3,2,2,128,128]{4,3,2,1,0:T(8,128)S(1)} %get-tuple-element.19), channel_id=1, source_target_pairs={{0,1},{1,0},{2,3},{3,2},{4,5},{5,4},{6,7},{7,6},{8,9},{9,8},{10,11... | collective-permute-start | bytes 2359304 | tf_op jit(solution)/shard_map/ppermute | solution.py:360
  75.3 13.3 %collective-permute-start.7 = (f32[3,2,2,128,128]{4,3,2,1,0:T(8,128)S(1)}, f32[3,2,2,128,128]{4,3,2,1,0:T(8,128)S(1)}, u32[]{:S(2)}, u32[]{:S(2)}) collective-permute-start(f32[3,2,2,128,128]{4,3,2,1,0:T(8,128)S(1)} %get-tuple-element.20), channel_id=1, source_target_pairs={{1,2},{3,4},{5,6},{7,8},{9,10},{11,12},{13,14},{2,1},{4,3},{6,5},{... | collective-permute-start | bytes 2359304 | tf_op jit(solution)/shard_map/ppermute | solution.py:359
  88.6 10.8 %collective-permute-start.8 = (f32[2,2,128,128]{3,2,1,0:T(8,128)S(1)}, f32[2,2,128,128]{3,2,1,0:T(8,128)S(1)}, u32[]{:S(2)}, u32[]{:S(2)}) collective-permute-start(f32[2,2,128,128]{3,2,1,0:T(8,128)S(1)} %fusion.3), channel_id=1, source_target_pairs={{32,0},{64,32},{96,64},{128,96},{160,128},{192,160},{224,192},{256... | collective-permute-start | bytes 786440 | tf_op jit(solution)/shard_map/ppermute | solution.py:362
  89.9 23.3 %all-to-all-start = ((f32[16,2,16,256]{3,2,1,0:T(8,128)}), f32[16,2,16,256]{3,2,1,0:T(8,128)S(1)}, u32[]{:S(2)}, u32[]{:S(2)}) async-start(f32[16,2,16,256]{3,2,1,0:T(8,128)} %get-tuple-element.23), calls=%async_computation | async-start | bytes 1048576 | tf_op jit(solution)/shard_map/all_to_all | solution.py:317
  99.5 26.8 %collective-permute-start.9 = (f32[2,2,128,128]{3,2,1,0:T(8,128)S(1)}, f32[2,2,128,128]{3,2,1,0:T(8,128)S(1)}, u32[]{:S(2)}, u32[]{:S(2)}) collective-permute-start(f32[2,2,128,128]{3,2,1,0:T(8,128)S(1)} %fusion.6), channel_id=1, source_target_pairs={{0,16},{16,0},{32,48},{48,32},{64,80},{80,64},{96,112},{112,96},{1... | collective-permute-start | bytes 786440 | tf_op jit(solution)/shard_map/ppermute | solution.py:365
  114.2 27.4 %all-to-all-start.1 = ((f32[32,2,128]{2,1,0:T(2,128)}), f32[32,2,128]{2,1,0:T(2,128)S(1)}, u32[]{:S(2)}, u32[]{:S(2)}) async-start(f32[32,2,128]{2,1,0:T(2,128)} %reshape.26), calls=%async_computation.1 | async-start | bytes 65536 | tf_op jit(solution)/shard_map/all_to_all | solution.py:325

commit v5 on v4

--- a/solution.py
+++ b/solution.py
@@ -277,6 +277,23 @@
     )
 
 
+def hold_kernel(stored, out, arrived):
+    load = pltpu.make_async_copy(stored, out, arrived)
+    load.start()
+    load.wait()
+
+
+def hold(tables):
+    return call(
+        hold_kernel,
+        jax.ShapeDtypeStruct(tables.shape, BF16),
+        [ANYWHERE],
+        VMEM,
+        [pltpu.SemaphoreType.DMA],
+        0,
+    )(tables)
+
+
 def front(place, tiles, probe, propagator, tables):
     return call(
         front_kernel,
@@ -333,11 +350,6 @@
     hops = [(i, i + 2) for i in range(0, rows - 2, 2)] + [(i + 2, i) for i in range(1, rows - 2, 2)]
     swap = [(i, i ^ 1) for i in range(rows)]
     near = lax.ppermute(object_slices, "row", swap)
-    far = lax.ppermute(near, "row", hops)
-    stacks = lax.optimization_barrier([jnp.stack([object_slices[k], near[k], near[k]]) for k in range(2)])
-    sent = [lax.dynamic_update_slice(stacks[k], far[k][None], (2, 0, 0, 0)) for k in range(2)]
-    sides0, sides1 = (sides(sent[0]), sides(sent[1]))
-
     order = order_matrix()
     angles = dot(dot(order, propagator_phase).astype(BF16), order.T)
     propagator = jnp.stack([jnp.cos(angles), jnp.sin(angles)])
@@ -349,8 +361,15 @@
         2 * HALF * jnp.stack([1 - upper, upper, 1 - odd, odd]),
     ]).astype(jnp.int32)
     weight = (batch_order[0, 0] >= 0).astype(F32)
-    tables = half_tables()
+    tables = hold(half_tables())
+    ready = (near, propagator, measured, place, weight, tables)
+    near, propagator, measured, place, weight, tables = lax.optimization_barrier(ready)
+    far = lax.ppermute(near, "row", hops)
     tiles = (object_slices, near, far)
+    stacks = lax.optimization_barrier([jnp.stack([object_slices[k], near[k], near[k]]) for k in range(2)])
+    sent = [lax.dynamic_update_slice(stacks[k], far[k][None], (2, 0, 0, 0)) for k in range(2)]
+    sides0, sides1 = (sides(sent[0]), sides(sent[1]))
+
     waves, layers = front(place, tiles + sides0, probe_wave, propagator, tables)
     outs = back(place, weight, tiles + sides1, waves, layers, probe_wave, propagator, measured, tables, rows // 2)
     own, near, far, to_sibling, to_other, probe_term = outs

time: 143 us -> 141 us (0.986)
  waiting for transfers between devices: 30.1 us -> 32.8 us
  local copies, waits for them, and re-layouts: 5.84 us -> 3.74 us
    unnamed x16 -> x18, local copies, waits for them, and re-layouts: 3.3 us -> 0.85 us
where the time goes in v5:
time: 141 us; the launch traced here: 140 us
  starting transfers between devices  88.3 us (63%)
  waiting for transfers between devices  32.8 us (23%)
  Pallas kernels  11 us (8%)
  local copies, waits for them, and re-layouts  3.74 us (3%)
  matrix products  1.52 us (1%)
    ppermute x2, starting transfers between devices, sides(): other = lax.ppermute(value, 'col', inner + flipped(inner))  23.9 us
    ppermute x1, starting transfers between devices, per_device(): near = lax.ppermute(object_slices, 'row', swap)  16.4 us
    all_to_all x1, waiting for transfers between devices, probe_block(): lax.all_to_all(parts, ('row', 'col'), 0, 0, tiled=True, axis_index_groups...  14.4 us
    ppermute x1, starting transfers between devices, per_device(): own = own + sibling[0] + other[0] + lax.ppermute(near, 'row', swap)  13.7 us
    all_to_all x1, starting transfers between devices, probe_block(): lax.all_to_all(parts, ('row', 'col'), 0, 0, tiled=True, axis_index_groups...  11.5 us
    ppermute x1, waiting for transfers between devices, per_device(): other = lax.ppermute(to_other, 'col', inner + flipped(inner))  10.9 us
    all_to_all x1, starting transfers between devices, probe_rows(): lax.all_to_all(term, 'row', 0, 0, tiled=True, axis_index_groups=groups)  9.51 us
    pallas_call x1, Pallas kernels, back(): call(back_kernel, [shaped(2, 2, HALF, HALF)] * 3 + [shaped(3, 2, 2, HALF,...  7.7 us
  transfers between devices with their start and end apart: 12, of which 5 were waited for; matrix products, arithmetic and copies ran while one was open for 4% of the time, Pallas kernels for 2%

profile of v5, /device:TPU:1, one launch (start us, length us, event | category | flops | bytes accessed | tf_op | source)
XLA Modules:
  0.0 139.5 jit_solution(12787732188471507777)
XLA Ops:
  0.6 16.4 %collective-permute-start = (f32[2,2,128,128]{3,2,1,0:T(8,128)}, f32[2,2,128,128]{3,2,1,0:T(8,128)S(1)}, u32[]{:S(2)}, u32[]{:S(2)}) collective-permute-start(f32[2,2,128,128]{3,2,1,0:T(8,128)} %own.3), channel_id=1, source_target_pairs={{0,16},{16,0},{32,48},{48,32},{64,80},{80,64},{96,112},{112,96},{1... | collective-permute-start | bytes 786440 | tf_op jit(solution)/shard_map/ppermute | solution.py:352
  17.1 1.0 fusion.14
  18.2 0.1 squeeze.26
  18.4 0.1 sub.18
  18.5 1.2 cosine_bitcast_fusion
  19.7 0.1 add_multiply_fusion
  19.8 0.1 shard_map.95.tables
  19.9 0.8 copy-done.5
  20.7 0.4 fusion.1.intensity
  21.1 1.5 %collective-permute-done.near = f32[2,2,128,128]{3,2,1,0:T(8,128)S(1)} collective-permute-done((f32[2,2,128,128]{3,2,1,0:T(8,128)}, f32[2,2,128,128]{3,2,1,0:T(8,128)S(1)}, u32[]{:S(2)}, u32[]{:S(2)}) %collective-permute-start) | collective-permute-done | bytes 262176 | tf_op jit(solution)/shard_map/ppermute | solution.py:352
  22.6 3.8 %collective-permute-start.1 = (f32[2,2,128,128]{3,2,1,0:T(8,128)S(1)}, f32[2,2,128,128]{3,2,1,0:T(8,128)S(1)}, u32[]{:S(2)}, u32[]{:S(2)}) collective-permute-start(f32[2,2,128,128]{3,2,1,0:T(8,128)S(1)} %collective-permute-done.near), channel_id=1, source_target_pairs={{0,32},{32,64},{64,96},{96,128},{128,160},{160,192},{192,224},{224... | collective-permute-start | bytes 786440 | tf_op jit(solution)/shard_map/ppermute | solution.py:367
  26.5 4.0 %collective-permute-done.1.far = f32[2,2,128,128]{3,2,1,0:T(8,128)S(1)} collective-permute-done((f32[2,2,128,128]{3,2,1,0:T(8,128)S(1)}, f32[2,2,128,128]{3,2,1,0:T(8,128)S(1)}, u32[]{:S(2)}, u32[]{:S(2)}) %collective-permute-start.1) | collective-permute-done | bytes 262176 | tf_op jit(solution)/shard_map/ppermute | solution.py:367
  30.5 22.0 %collective-permute-start.5 = (f32[3,2,128,128]{3,2,1,0:T(8,128)S(1)}, f32[3,2,128,128]{3,2,1,0:T(8,128)S(1)}, u32[]{:S(2)}, u32[]{:S(2)}) collective-permute-start(f32[3,2,128,128]{3,2,1,0:T(8,128)S(1)} %get-tuple-element.38), channel_id=1, source_target_pairs={{1,2},{3,4},{5,6},{7,8},{9,10},{11,12},{13,14},{2,1},{4,3},{6,5},{... | collective-permute-start | bytes 1179656 | tf_op jit(solution)/shard_map/ppermute | solution.py:327
  52.5 1.9 %collective-permute-start.4 = (f32[3,2,128,128]{3,2,1,0:T(8,128)S(1)}, f32[3,2,128,128]{3,2,1,0:T(8,128)S(1)}, u32[]{:S(2)}, u32[]{:S(2)}) collective-permute-start(f32[3,2,128,128]{3,2,1,0:T(8,128)S(1)} %get-tuple-element.38), channel_id=1, source_target_pairs={{0,1},{1,0},{2,3},{3,2},{4,5},{5,4},{6,7},{7,6},{8,9},{9,8},{10,11... | collective-permute-start | bytes 1179656 | tf_op jit(solution)/shard_map/ppermute | solution.py:328
  54.4 1.9 %collective-permute-start.3 = (f32[3,2,128,128]{3,2,1,0:T(8,128)S(1)}, f32[3,2,128,128]{3,2,1,0:T(8,128)S(1)}, u32[]{:S(2)}, u32[]{:S(2)}) collective-permute-start(f32[3,2,128,128]{3,2,1,0:T(8,128)S(1)} %get-tuple-element.39), channel_id=1, source_target_pairs={{1,2},{3,4},{5,6},{7,8},{9,10},{11,12},{13,14},{2,1},{4,3},{6,5},{... | collective-permute-start | bytes 1179656 | tf_op jit(solution)/shard_map/ppermute | solution.py:327
  56.3 1.9 %collective-permute-start.2 = (f32[3,2,128,128]{3,2,1,0:T(8,128)S(1)}, f32[3,2,128,128]{3,2,1,0:T(8,128)S(1)}, u32[]{:S(2)}, u32[]{:S(2)}) collective-permute-start(f32[3,2,128,128]{3,2,1,0:T(8,128)S(1)} %get-tuple-element.39), channel_id=1, source_target_pairs={{0,1},{1,0},{2,3},{3,2},{4,5},{5,4},{6,7},{7,6},{8,9},{9,8},{10,11... | collective-permute-start | bytes 1179656 | tf_op jit(solution)/shard_map/ppermute | solution.py:328
  58.3 3.2 %shard_map.96 = (f32[2,2,256,256]{3,2,1,0:T(8,128)S(1)}, f32[2,2,256,256]{3,2,1,0:T(8,128)S(1)}) custom-call(s32[8]{0:T(128)S(1)} %pad_add_fusion.1.place, f32[2,2,128,128]{3,2,1,0:T(8,128)S(1)} %copy-done.2, f32[2,2,128,128]{3,2,1,0:T(8,128)S(1)} %collective-permute-done.near, f32[2,2,128,128]{3,2,1,0:T(8,128)S(1)} %collective-permute-done.1.far, ...), custom_call_target="tpu_custom_call" | custom-call | flops 3300000000 | bytes 4000000 | tf_op jit(solution)/shard_map/pallas_call | solution.py:298
  61.5 2.0 %collective-permute-done.3.other = f32[3,2,128,128]{3,2,1,0:T(8,128)S(1)} collective-permute-done((f32[3,2,128,128]{3,2,1,0:T(8,128)S(1)}, f32[3,2,128,128]{3,2,1,0:T(8,128)S(1)}, u32[]{:S(2)}, u32[]{:S(2)}) %collective-permute-start.3) | collective-permute-done | bytes 393248 | tf_op jit(solution)/shard_map/ppermute | solution.py:327
  63.5 7.7 %shard_map.97 = (f32[2,2,128,128]{3,2,1,0:T(8,128)S(1)}, f32[2,2,128,128]{3,2,1,0:T(8,128)S(1)}, f32[2,2,128,128]{3,2,1,0:T(8,128)S(1)}, f32[3,2,2,128,128]{4,3,...) custom-call(s32[8]{0:T(128)S(1)} %pad_add_fusion.1.place, f32[2]{0:T(128)S(1)} %fusion.13.weight, ...), custom_call_target="tpu_custom_call" | custom-call | flops 6600000000 | bytes 4000000 | tf_op jit(solution)/shard_map/pallas_call | solution.py:309
  71.2 1.9 %collective-permute-start.6 = (f32[3,2,2,128,128]{4,3,2,1,0:T(8,128)S(1)}, f32[3,2,2,128,128]{4,3,2,1,0:T(8,128)S(1)}, u32[]{:S(2)}, u32[]{:S(2)}) collective-permute-start(f32[3,2,2,128,128]{4,3,2,1,0:T(8,128)S(1)} %get-tuple-element.31), channel_id=1, source_target_pairs={{0,1},{1,0},{2,3},{3,2},{4,5},{5,4},{6,7},{7,6},{8,9},{9,8},{10,11... | collective-permute-start | bytes 2359304 | tf_op jit(solution)/shard_map/ppermute | solution.py:379
  73.1 2.4 %collective-permute-start.7 = (f32[3,2,2,128,128]{4,3,2,1,0:T(8,128)S(1)}, f32[3,2,2,128,128]{4,3,2,1,0:T(8,128)S(1)}, u32[]{:S(2)}, u32[]{:S(2)}) collective-permute-start(f32[3,2,2,128,128]{4,3,2,1,0:T(8,128)S(1)} %get-tuple-element.32), channel_id=1, source_target_pairs={{1,2},{3,4},{5,6},{7,8},{9,10},{11,12},{13,14},{2,1},{4,3},{6,5},{... | collective-permute-start | bytes 2359304 | tf_op jit(solution)/shard_map/ppermute | solution.py:378
  75.6 10.9 %collective-permute-done.7 = f32[3,2,2,128,128]{4,3,2,1,0:T(8,128)S(1)} collective-permute-done((f32[3,2,2,128,128]{4,3,2,1,0:T(8,128)S(1)}, f32[3,2,2,128,128]{4,3,2,1,0:T(8,128)S(1)}, u32[]{:S(2)}, u32[]{:S(2)}) %collective-permute-start.7) | collective-permute-done | bytes 786464 | tf_op jit(solution)/shard_map/ppermute | solution.py:378
  86.5 1.3 collective-permute-start.8
  87.8 9.5 %all-to-all-start = ((f32[16,2,16,256]{3,2,1,0:T(8,128)}), f32[16,2,16,256]{3,2,1,0:T(8,128)S(1)}, u32[]{:S(2)}, u32[]{:S(2)}) async-start(f32[16,2,16,256]{3,2,1,0:T(8,128)} %get-tuple-element.35), calls=%async_computation | async-start | bytes 1048576 | tf_op jit(solution)/shard_map/all_to_all | solution.py:334
  97.4 13.7 %collective-permute-start.9 = (f32[2,2,128,128]{3,2,1,0:T(8,128)S(1)}, f32[2,2,128,128]{3,2,1,0:T(8,128)S(1)}, u32[]{:S(2)}, u32[]{:S(2)}) collective-permute-start(f32[2,2,128,128]{3,2,1,0:T(8,128)S(1)} %fusion.6), channel_id=1, source_target_pairs={{0,16},{16,0},{32,48},{48,32},{64,80},{80,64},{96,112},{112,96},{1... | collective-permute-start | bytes 786440 | tf_op jit(solution)/shard_map/ppermute | solution.py:384
  111.1 0.1 reshape.21
  111.3 0.1 copy.13
  111.4 0.8 reshape.26
  112.1 11.5 %all-to-all-start.1 = ((f32[32,2,128]{2,1,0:T(2,128)}), f32[32,2,128]{2,1,0:T(2,128)S(1)}, u32[]{:S(2)}, u32[]{:S(2)}) async-start(f32[32,2,128]{2,1,0:T(2,128)} %reshape.26), calls=%async_computation.1 | async-start | bytes 65536 | tf_op jit(solution)/shard_map/all_to_all | solution.py:342
  123.7 0.8 fusion.9
  124.4 14.4 %all-to-all-done.1 = f32[32,2,128]{2,1,0:T(2,128)S(1)} async-done(((f32[32,2,128]{2,1,0:T(2,128)}), f32[32,2,128]{2,1,0:T(2,128)S(1)}, u32[]{:S(2)}, u32[]{:S(2)}) %all-to-all-start.1) | async-done | bytes 32800 | tf_op jit(solution)/shard_map/all_to_all | solution.py:342
  138.9 0.7 reshape.23
  (37 shorter events, 0.5 us)
Async XLA Ops:
  0.6 19.3 %copy-start = (bf16[1,1,2,256,256]{4,3,2,1,0:T(8,128)(2,1)S(1)}, bf16[1,1,2,256,256]{4,3,2,1,0:T(8,128)(2,1)}, u32[]{:S(2)}) copy-start(bf16[1,1,2,256,256]{4,3,2,1,0:T(8,128)(2,1)} %param.11) | copy-start | bytes 786436
  0.6 22.0 %collective-permute-start = (f32[2,2,128,128]{3,2,1,0:T(8,128)}, f32[2,2,128,128]{3,2,1,0:T(8,128)S(1)}, u32[]{:S(2)}, u32[]{:S(2)}) collective-permute-start(f32[2,2,128,128]{3,2,1,0:T(8,128)} %own.3), channel_id=1, source_target_pairs={{0,16},{16,0},{32,48},{48,32},{64,80},{80,64},{96,112},{112,96},{1... | collective-permute-start | bytes 786440 | tf_op jit(solution)/shard_map/ppermute | solution.py:352
  17.1 1.1 copy-start.7
  17.1 1.2 copy-start.8
  17.1 1.4 copy-start.4
  17.1 1.3 copy-start.6
  18.2 1.7 %copy-start.1 = (bf16[4,2,256,256]{3,2,1,0:T(8,128)(2,1)S(1)}, bf16[4,2,256,256]{3,2,1,0:T(8,128)(2,1)}, u32[]{:S(2)}) copy-start(bf16[4,2,256,256]{3,2,1,0:T(8,128)(2,1)} %constant.40.clone.stored) | copy-start | bytes 3145732
  19.8 0.9 copy-start.5
  22.6 7.8 %collective-permute-start.1 = (f32[2,2,128,128]{3,2,1,0:T(8,128)S(1)}, f32[2,2,128,128]{3,2,1,0:T(8,128)S(1)}, u32[]{:S(2)}, u32[]{:S(2)}) collective-permute-start(f32[2,2,128,128]{3,2,1,0:T(8,128)S(1)} %collective-permute-done.near), channel_id=1, source_target_pairs={{0,32},{32,64},{64,96},{96,128},{128,160},{160,192},{192,224},{224... | collective-permute-start | bytes 786440 | tf_op jit(solution)/shard_map/ppermute | solution.py:367
  30.5 27.8 %copy-start.2 = (f32[2,2,128,128]{3,2,1,0:T(8,128)S(1)}, f32[2,2,128,128]{3,2,1,0:T(8,128)}, u32[]{:S(2)}) copy-start(f32[2,2,128,128]{3,2,1,0:T(8,128)} %own.3) | copy-start | bytes 786436
  30.5 27.8 %copy-start.3 = (bf16[2,256,256]{2,1,0:T(8,128)(2,1)S(1)}, bf16[2,256,256]{2,1,0:T(8,128)(2,1)}, u32[]{:S(2)}) copy-start(bf16[2,256,256]{2,1,0:T(8,128)(2,1)} %probe.3) | copy-start | bytes 786436
  30.5 27.8 %collective-permute-start.5 = (f32[3,2,128,128]{3,2,1,0:T(8,128)S(1)}, f32[3,2,128,128]{3,2,1,0:T(8,128)S(1)}, u32[]{:S(2)}, u32[]{:S(2)}) collective-permute-start(f32[3,2,128,128]{3,2,1,0:T(8,128)S(1)} %get-tuple-element.38), channel_id=1, source_target_pairs={{1,2},{3,4},{5,6},{7,8},{9,10},{11,12},{13,14},{2,1},{4,3},{6,5},{... | collective-permute-start | bytes 1179656 | tf_op jit(solution)/shard_map/ppermute | solution.py:327
  52.5 5.8 %collective-permute-start.4 = (f32[3,2,128,128]{3,2,1,0:T(8,128)S(1)}, f32[3,2,128,128]{3,2,1,0:T(8,128)S(1)}, u32[]{:S(2)}, u32[]{:S(2)}) collective-permute-start(f32[3,2,128,128]{3,2,1,0:T(8,128)S(1)} %get-tuple-element.38), channel_id=1, source_target_pairs={{0,1},{1,0},{2,3},{3,2},{4,5},{5,4},{6,7},{7,6},{8,9},{9,8},{10,11... | collective-permute-start | bytes 1179656 | tf_op jit(solution)/shard_map/ppermute | solution.py:328
  54.4 9.1 %collective-permute-start.3 = (f32[3,2,128,128]{3,2,1,0:T(8,128)S(1)}, f32[3,2,128,128]{3,2,1,0:T(8,128)S(1)}, u32[]{:S(2)}, u32[]{:S(2)}) collective-permute-start(f32[3,2,128,128]{3,2,1,0:T(8,128)S(1)} %get-tuple-element.39), channel_id=1, source_target_pairs={{1,2},{3,4},{5,6},{7,8},{9,10},{11,12},{13,14},{2,1},{4,3},{6,5},{... | collective-permute-start | bytes 1179656 | tf_op jit(solution)/shard_map/ppermute | solution.py:327
  56.3 7.2 %collective-permute-start.2 = (f32[3,2,128,128]{3,2,1,0:T(8,128)S(1)}, f32[3,2,128,128]{3,2,1,0:T(8,128)S(1)}, u32[]{:S(2)}, u32[]{:S(2)}) collective-permute-start(f32[3,2,128,128]{3,2,1,0:T(8,128)S(1)} %get-tuple-element.39), channel_id=1, source_target_pairs={{0,1},{1,0},{2,3},{3,2},{4,5},{5,4},{6,7},{7,6},{8,9},{9,8},{10,11... | collective-permute-start | bytes 1179656 | tf_op jit(solution)/shard_map/ppermute | solution.py:328
  71.2 4.4 %collective-permute-start.6 = (f32[3,2,2,128,128]{4,3,2,1,0:T(8,128)S(1)}, f32[3,2,2,128,128]{4,3,2,1,0:T(8,128)S(1)}, u32[]{:S(2)}, u32[]{:S(2)}) collective-permute-start(f32[3,2,2,128,128]{4,3,2,1,0:T(8,128)S(1)} %get-tuple-element.31), channel_id=1, source_target_pairs={{0,1},{1,0},{2,3},{3,2},{4,5},{5,4},{6,7},{7,6},{8,9},{9,8},{10,11... | collective-permute-start | bytes 2359304 | tf_op jit(solution)/shard_map/ppermute | solution.py:379
  73.1 13.3 %collective-permute-start.7 = (f32[3,2,2,128,128]{4,3,2,1,0:T(8,128)S(1)}, f32[3,2,2,128,128]{4,3,2,1,0:T(8,128)S(1)}, u32[]{:S(2)}, u32[]{:S(2)}) collective-permute-start(f32[3,2,2,128,128]{4,3,2,1,0:T(8,128)S(1)} %get-tuple-element.32), channel_id=1, source_target_pairs={{1,2},{3,4},{5,6},{7,8},{9,10},{11,12},{13,14},{2,1},{4,3},{6,5},{... | collective-permute-start | bytes 2359304 | tf_op jit(solution)/shard_map/ppermute | solution.py:378
  86.5 10.8 %collective-permute-start.8 = (f32[2,2,128,128]{3,2,1,0:T(8,128)S(1)}, f32[2,2,128,128]{3,2,1,0:T(8,128)S(1)}, u32[]{:S(2)}, u32[]{:S(2)}) collective-permute-start(f32[2,2,128,128]{3,2,1,0:T(8,128)S(1)} %fusion.3), channel_id=1, source_target_pairs={{32,0},{64,32},{96,64},{128,96},{160,128},{192,160},{224,192},{256... | collective-permute-start | bytes 786440 | tf_op jit(solution)/shard_map/ppermute | solution.py:381
  87.8 23.3 %all-to-all-start = ((f32[16,2,16,256]{3,2,1,0:T(8,128)}), f32[16,2,16,256]{3,2,1,0:T(8,128)S(1)}, u32[]{:S(2)}, u32[]{:S(2)}) async-start(f32[16,2,16,256]{3,2,1,0:T(8,128)} %get-tuple-element.35), calls=%async_computation | async-start | bytes 1048576 | tf_op jit(solution)/shard_map/all_to_all | solution.py:334
  97.4 26.3 %collective-permute-start.9 = (f32[2,2,128,128]{3,2,1,0:T(8,128)S(1)}, f32[2,2,128,128]{3,2,1,0:T(8,128)S(1)}, u32[]{:S(2)}, u32[]{:S(2)}) collective-permute-start(f32[2,2,128,128]{3,2,1,0:T(8,128)S(1)} %fusion.6), channel_id=1, source_target_pairs={{0,16},{16,0},{32,48},{48,32},{64,80},{80,64},{96,112},{112,96},{1... | collective-permute-start | bytes 786440 | tf_op jit(solution)/shard_map/ppermute | solution.py:384
  112.1 26.7 %all-to-all-start.1 = ((f32[32,2,128]{2,1,0:T(2,128)}), f32[32,2,128]{2,1,0:T(2,128)S(1)}, u32[]{:S(2)}, u32[]{:S(2)}) async-start(f32[32,2,128]{2,1,0:T(2,128)} %reshape.26), calls=%async_computation.1 | async-start | bytes 65536 | tf_op jit(solution)/shard_map/all_to_all | solution.py:342

commit v6 on v5

--- a/solution.py
+++ b/solution.py
@@ -207,7 +207,7 @@
 
 
 def back_kernel(place, weight, own, near, far, sibling, other, waves, layers, probe, propagator, intensity, tables,
-                out_own, out_near, out_far, out_sibling, out_other, out_probe, field, total0, total1, kept, arrived, left_sem):
+                out_own, out_near, out_far, out_sibling, out_other, out_last, out_probe, field, total0, total1, kept, arrived, left_sem):
     loads = assemble(place, field, 1, own, near, far, sibling, other, arrived)
     for load in loads:
         load.start()
@@ -215,8 +215,9 @@
 
     def stores(layer):
         middle = [tile.at[layer] for tile in (out_own, out_near, out_far)]
-        sides = [[side.at[k, layer] for k in range(3)] for side in (out_sibling, out_other)]
-        parts = pieces(place, totals[layer], middle, *sides)
+        beside = [out_sibling.at[k, layer] for k in range(3)]
+        beyond = [out_other.at[0, layer], out_other.at[1, layer], out_last.at[layer]]
+        parts = pieces(place, totals[layer], middle, beside, beyond)
         return [pltpu.make_async_copy(b, a, left_sem.at[layer, n]) for n, (a, b) in enumerate(parts)]
 
     for total in totals:
@@ -308,9 +309,11 @@
 def back(place, weight, tiles, waves, layers, probe, propagator, intensity, tables, blocks):
     return call(
         back_kernel,
-        [shaped(2, 2, HALF, HALF)] * 3 + [shaped(3, 2, 2, HALF, HALF)] * 2 + [shaped(blocks, 2, WIN // blocks, WIN)],
+        [shaped(2, 2, HALF, HALF)] * 3
+        + [shaped(3, 2, 2, HALF, HALF), shaped(2, 2, 2, HALF, HALF), shaped(2, 2, HALF, HALF)]
+        + [shaped(blocks, 2, WIN // blocks, WIN)],
         [SMEM] * 2 + [ANYWHERE] * 5 + [VMEM] * 6,
-        [ANYWHERE] * 5 + [VMEM],
+        [ANYWHERE] * 6 + [VMEM],
         [pltpu.VMEM((2, 3 * HALF, 3 * HALF), F32)] * 3
         + [pltpu.VMEM((2, 2, WIN, WIN), F32), pltpu.SemaphoreType.DMA((9,)), pltpu.SemaphoreType.DMA((2, 9))],
         6_600_000_000,
@@ -372,13 +375,14 @@
 
     waves, layers = front(place, tiles + sides0, probe_wave, propagator, tables)
     outs = back(place, weight, tiles + sides1, waves, layers, probe_wave, propagator, measured, tables, rows // 2)
-    own, near, far, to_sibling, to_other, probe_term = outs
+    own, near, far, to_sibling, to_other, to_last, probe_term = outs
     cols = lax.axis_size("col")
     inner = [(i, i + 1) for i in range(1, cols - 1, 2)]
+    last = lax.ppermute(to_last, "col", inner + flipped(inner))
     other = lax.ppermute(to_other, "col", inner + flipped(inner))
     sibling = lax.ppermute(to_sibling, "col", [(i, i ^ 1) for i in range(cols)])
     spread = probe_rows(probe_term)
-    far = lax.ppermute(far + sibling[2] + other[2], "row", flipped(hops))
+    far = lax.ppermute(far + sibling[2] + last, "row", flipped(hops))
     pair = jnp.sum(spread, axis=0)
     near = near + sibling[1] + other[1] + far
     own = own + sibling[0] + other[0] + lax.ppermute(near, "row", swap)

time: 141 us -> 137 us (0.972)
  waiting for transfers between devices: 32.8 us -> 26 us
  starting transfers between devices: 88.3 us -> 91.8 us
    ppermute x1, waiting for transfers between devices: 10.9 us -> 0.01 us  [per_device(): other = lax.ppermute(to_other, 'col', inner + flipped(inner))]
    ppermute x1, waiting for transfers between devices: 0.01 us -> 6.98 us  [per_device(): own = own + sibling[0] + other[0] + lax.ppermute(near, 'row', swap)]
    all_to_all x1, waiting for transfers between devices: 14.4 us -> 9.42 us  [probe_block(): lax.all_to_all(parts, ('row', 'col'), 0, 0, tiled=True, axis_index_groups...]
    ppermute x1 -> x2, starting transfers between devices: 1.29 us -> 3.7 us  [the longest x1 2.41 us: per_device(): last = lax.ppermute(to_last, 'col', inner + flipped(inner))]
    ppermute x1 -> x2, waiting for transfers between devices: 0.01 us -> 2.12 us  [the longest x1 2.11 us: per_device(): last = lax.ppermute(to_last, 'col', inner + flipped(inner))]
  transfers between devices with their start and end apart: 12 -> 13, of which waited for: 5 -> 6; matrix products, arithmetic and copies ran while one was open for 4% -> 4% of each run, Pallas kernels for 2% -> 2%
where the time goes in v6:
time: 137 us
  starting transfers between devices  91.8 us (67%)
  waiting for transfers between devices  26 us (19%)
  Pallas kernels  11.3 us (8%)
  local copies, waits for them, and re-layouts  3.72 us (3%)
  matrix products  1.52 us (1%)
    ppermute x2, starting transfers between devices, sides(): other = lax.ppermute(value, 'col', inner + flipped(inner))  23.9 us
    ppermute x1, starting transfers between devices, per_device(): near = lax.ppermute(object_slices, 'row', swap)  16.4 us
    ppermute x1, starting transfers between devices, per_device(): own = own + sibling[0] + other[0] + lax.ppermute(near, 'row', swap)  14 us
    all_to_all x1, starting transfers between devices, probe_block(): lax.all_to_all(parts, ('row', 'col'), 0, 0, tiled=True, axis_index_groups...  11.6 us
    all_to_all x1, starting transfers between devices, probe_rows(): lax.all_to_all(term, 'row', 0, 0, tiled=True, axis_index_groups=groups)  9.51 us
    all_to_all x1, waiting for transfers between devices, probe_block(): lax.all_to_all(parts, ('row', 'col'), 0, 0, tiled=True, axis_index_groups...  9.42 us
    pallas_call x1, Pallas kernels, back(): call(back_kernel, [shaped(2, 2, HALF, HALF)] * 3 + [shaped(3, 2, 2, HALF,...  7.98 us
    ppermute x1, waiting for transfers between devices, per_device(): own = own + sibling[0] + other[0] + lax.ppermute(near, 'row', swap)  6.98 us
  transfers between devices with their start and end apart: 13, of which 6 were waited for; matrix products, arithmetic and copies ran while one was open for 4% of the time, Pallas kernels for 2%

profile of v6, /device:TPU:1, one launch (start us, length us, event | category | flops | bytes accessed | tf_op | source)
XLA Modules:
  0.0 136.5 jit_solution(12469116408773457057)
XLA Ops:
  0.6 16.4 %collective-permute-start = (f32[2,2,128,128]{3,2,1,0:T(8,128)}, f32[2,2,128,128]{3,2,1,0:T(8,128)S(1)}, u32[]{:S(2)}, u32[]{:S(2)}) collective-permute-start(f32[2,2,128,128]{3,2,1,0:T(8,128)} %own.3), channel_id=1, source_target_pairs={{0,16},{16,0},{32,48},{48,32},{64,80},{80,64},{96,112},{112,96},{1... | collective-permute-start | bytes 786440 | tf_op jit(solution)/shard_map/ppermute | solution.py:355
  17.1 1.0 fusion.14
  18.4 0.1 sub.18
  18.5 1.2 cosine_bitcast_fusion
  19.8 0.1 shard_map.95.tables
  19.9 0.8 copy-done.5
  20.7 0.4 fusion.1.intensity
  21.1 1.5 %collective-permute-done.near = f32[2,2,128,128]{3,2,1,0:T(8,128)S(1)} collective-permute-done((f32[2,2,128,128]{3,2,1,0:T(8,128)}, f32[2,2,128,128]{3,2,1,0:T(8,128)S(1)}, u32[]{:S(2)}, u32[]{:S(2)}) %collective-permute-start) | collective-permute-done | bytes 262176 | tf_op jit(solution)/shard_map/ppermute | solution.py:355
  22.6 3.8 %collective-permute-start.1 = (f32[2,2,128,128]{3,2,1,0:T(8,128)S(1)}, f32[2,2,128,128]{3,2,1,0:T(8,128)S(1)}, u32[]{:S(2)}, u32[]{:S(2)}) collective-permute-start(f32[2,2,128,128]{3,2,1,0:T(8,128)S(1)} %collective-permute-done.near), channel_id=1, source_target_pairs={{0,32},{32,64},{64,96},{96,128},{128,160},{160,192},{192,224},{224... | collective-permute-start | bytes 786440 | tf_op jit(solution)/shard_map/ppermute | solution.py:370
  26.5 4.0 %collective-permute-done.1.far = f32[2,2,128,128]{3,2,1,0:T(8,128)S(1)} collective-permute-done((f32[2,2,128,128]{3,2,1,0:T(8,128)S(1)}, f32[2,2,128,128]{3,2,1,0:T(8,128)S(1)}, u32[]{:S(2)}, u32[]{:S(2)}) %collective-permute-start.1) | collective-permute-done | bytes 262176 | tf_op jit(solution)/shard_map/ppermute | solution.py:370
  30.5 22.0 %collective-permute-start.5 = (f32[3,2,128,128]{3,2,1,0:T(8,128)S(1)}, f32[3,2,128,128]{3,2,1,0:T(8,128)S(1)}, u32[]{:S(2)}, u32[]{:S(2)}) collective-permute-start(f32[3,2,128,128]{3,2,1,0:T(8,128)S(1)} %get-tuple-element.40), channel_id=1, source_target_pairs={{1,2},{3,4},{5,6},{7,8},{9,10},{11,12},{13,14},{2,1},{4,3},{6,5},{... | collective-permute-start | bytes 1179656 | tf_op jit(solution)/shard_map/ppermute | solution.py:330
  52.5 1.9 %collective-permute-start.4 = (f32[3,2,128,128]{3,2,1,0:T(8,128)S(1)}, f32[3,2,128,128]{3,2,1,0:T(8,128)S(1)}, u32[]{:S(2)}, u32[]{:S(2)}) collective-permute-start(f32[3,2,128,128]{3,2,1,0:T(8,128)S(1)} %get-tuple-element.40), channel_id=1, source_target_pairs={{0,1},{1,0},{2,3},{3,2},{4,5},{5,4},{6,7},{7,6},{8,9},{9,8},{10,11... | collective-permute-start | bytes 1179656 | tf_op jit(solution)/shard_map/ppermute | solution.py:331
  54.4 1.9 %collective-permute-start.3 = (f32[3,2,128,128]{3,2,1,0:T(8,128)S(1)}, f32[3,2,128,128]{3,2,1,0:T(8,128)S(1)}, u32[]{:S(2)}, u32[]{:S(2)}) collective-permute-start(f32[3,2,128,128]{3,2,1,0:T(8,128)S(1)} %get-tuple-element.41), channel_id=1, source_target_pairs={{1,2},{3,4},{5,6},{7,8},{9,10},{11,12},{13,14},{2,1},{4,3},{6,5},{... | collective-permute-start | bytes 1179656 | tf_op jit(solution)/shard_map/ppermute | solution.py:330
  56.3 1.9 %collective-permute-start.2 = (f32[3,2,128,128]{3,2,1,0:T(8,128)S(1)}, f32[3,2,128,128]{3,2,1,0:T(8,128)S(1)}, u32[]{:S(2)}, u32[]{:S(2)}) collective-permute-start(f32[3,2,128,128]{3,2,1,0:T(8,128)S(1)} %get-tuple-element.41), channel_id=1, source_target_pairs={{0,1},{1,0},{2,3},{3,2},{4,5},{5,4},{6,7},{7,6},{8,9},{9,8},{10,11... | collective-permute-start | bytes 1179656 | tf_op jit(solution)/shard_map/ppermute | solution.py:331
  58.3 3.2 %shard_map.96 = (f32[2,2,256,256]{3,2,1,0:T(8,128)S(1)}, f32[2,2,256,256]{3,2,1,0:T(8,128)S(1)}) custom-call(s32[8]{0:T(128)S(1)} %pad_add_fusion.1.place, f32[2,2,128,128]{3,2,1,0:T(8,128)S(1)} %copy-done.2, f32[2,2,128,128]{3,2,1,0:T(8,128)S(1)} %collective-permute-done.near, f32[2,2,128,128]{3,2,1,0:T(8,128)S(1)} %collective-permute-done.1.far, ...), custom_call_target="tpu_custom_call" | custom-call | flops 3300000000 | bytes 4000000 | tf_op jit(solution)/shard_map/pallas_call | solution.py:299
  61.5 2.0 %collective-permute-done.3.other = f32[3,2,128,128]{3,2,1,0:T(8,128)S(1)} collective-permute-done((f32[3,2,128,128]{3,2,1,0:T(8,128)S(1)}, f32[3,2,128,128]{3,2,1,0:T(8,128)S(1)}, u32[]{:S(2)}, u32[]{:S(2)}) %collective-permute-start.3) | collective-permute-done | bytes 393248 | tf_op jit(solution)/shard_map/ppermute | solution.py:330
  63.5 8.0 %shard_map.97 = (f32[2,2,128,128]{3,2,1,0:T(8,128)S(1)}, f32[2,2,128,128]{3,2,1,0:T(8,128)S(1)}, f32[2,2,128,128]{3,2,1,0:T(8,128)S(1)}, f32[3,2,2,128,128]{4,3,...) custom-call(s32[8]{0:T(128)S(1)} %pad_add_fusion.1.place, ...), custom_call_target="tpu_custom_call" | custom-call | flops 6600000000 | bytes 4000000 | tf_op jit(solution)/shard_map/pallas_call | solution.py:310
  71.5 1.9 %collective-permute-start.6 = (f32[3,2,2,128,128]{4,3,2,1,0:T(8,128)S(1)}, f32[3,2,2,128,128]{4,3,2,1,0:T(8,128)S(1)}, u32[]{:S(2)}, u32[]{:S(2)}) collective-permute-start(f32[3,2,2,128,128]{4,3,2,1,0:T(8,128)S(1)} %get-tuple-element.32), channel_id=1, source_target_pairs={{0,1},{1,0},{2,3},{3,2},{4,5},{5,4},{6,7},{7,6},{8,9},{9,8},{10,11... | collective-permute-start | bytes 2359304 | tf_op jit(solution)/shard_map/ppermute | solution.py:383
  73.4 2.4 %collective-permute-start.8 = (f32[2,2,128,128]{3,2,1,0:T(8,128)S(1)}, f32[2,2,128,128]{3,2,1,0:T(8,128)S(1)}, u32[]{:S(2)}, u32[]{:S(2)}) collective-permute-start(f32[2,2,128,128]{3,2,1,0:T(8,128)S(1)} %get-tuple-element.36), channel_id=1, source_target_pairs={{1,2},{3,4},{5,6},{7,8},{9,10},{11,12},{13,14},{2,1},{4,3},{6,5},{... | collective-permute-start | bytes 786440 | tf_op jit(solution)/shard_map/ppermute | solution.py:381
  75.8 3.1 %collective-permute-start.7 = (f32[2,2,2,128,128]{4,3,2,1,0:T(8,128)}, f32[2,2,2,128,128]{4,3,2,1,0:T(8,128)S(1)}, u32[]{:S(2)}, u32[]{:S(2)}) collective-permute-start(f32[2,2,2,128,128]{4,3,2,1,0:T(8,128)} %get-tuple-element.33), channel_id=1, source_target_pairs={{1,2},{3,4},{5,6},{7,8},{9,10},{11,12},{13,14},{2,1},{4,3},{6,5},{... | collective-permute-start | bytes 1572872 | tf_op jit(solution)/shard_map/ppermute | solution.py:382
  79.0 2.1 %collective-permute-done.8 = f32[2,2,128,128]{3,2,1,0:T(8,128)S(1)} collective-permute-done((f32[2,2,128,128]{3,2,1,0:T(8,128)S(1)}, f32[2,2,128,128]{3,2,1,0:T(8,128)S(1)}, u32[]{:S(2)}, u32[]{:S(2)}) %collective-permute-start.8) | collective-permute-done | bytes 262176 | tf_op jit(solution)/shard_map/ppermute | solution.py:381
  81.2 1.3 collective-permute-start.9
  82.5 9.5 %all-to-all-start = ((f32[16,2,16,256]{3,2,1,0:T(8,128)}), f32[16,2,16,256]{3,2,1,0:T(8,128)S(1)}, u32[]{:S(2)}, u32[]{:S(2)}) async-start(f32[16,2,16,256]{3,2,1,0:T(8,128)} %get-tuple-element.37), calls=%async_computation | async-start | bytes 1048576 | tf_op jit(solution)/shard_map/all_to_all | solution.py:337
  92.1 14.0 %collective-permute-start.10 = (f32[2,2,128,128]{3,2,1,0:T(8,128)S(1)}, f32[2,2,128,128]{3,2,1,0:T(8,128)S(1)}, u32[]{:S(2)}, u32[]{:S(2)}) collective-permute-start(f32[2,2,128,128]{3,2,1,0:T(8,128)S(1)} %fusion.6), channel_id=1, source_target_pairs={{0,16},{16,0},{32,48},{48,32},{64,80},{80,64},{96,112},{112,96},{1... | collective-permute-start | bytes 786440 | tf_op jit(solution)/shard_map/ppermute | solution.py:388
  106.1 0.1 reshape.21
  106.2 0.1 copy.13
  106.3 0.7 reshape.26
  107.1 11.6 %all-to-all-start.1 = ((f32[32,2,128]{2,1,0:T(2,128)}), f32[32,2,128]{2,1,0:T(2,128)S(1)}, u32[]{:S(2)}, u32[]{:S(2)}) async-start(f32[32,2,128]{2,1,0:T(2,128)} %reshape.26), calls=%async_computation.1 | async-start | bytes 65536 | tf_op jit(solution)/shard_map/all_to_all | solution.py:345
  118.7 7.0 %collective-permute-done.10 = f32[2,2,128,128]{3,2,1,0:T(8,128)S(1)} collective-permute-done((f32[2,2,128,128]{3,2,1,0:T(8,128)S(1)}, f32[2,2,128,128]{3,2,1,0:T(8,128)S(1)}, u32[]{:S(2)}, u32[]{:S(2)}) %collective-permute-start.10) | collective-permute-done | bytes 262176 | tf_op jit(solution)/shard_map/ppermute | solution.py:388
  125.6 0.8 fusion.9
  126.4 9.4 %all-to-all-done.1 = f32[32,2,128]{2,1,0:T(2,128)S(1)} async-done(((f32[32,2,128]{2,1,0:T(2,128)}), f32[32,2,128]{2,1,0:T(2,128)S(1)}, u32[]{:S(2)}, u32[]{:S(2)}) %all-to-all-start.1) | async-done | bytes 32800 | tf_op jit(solution)/shard_map/all_to_all | solution.py:345
  135.9 0.7 reshape.23
  (39 shorter events, 0.7 us)
Async XLA Ops:
  0.6 19.3 %copy-start = (bf16[1,1,2,256,256]{4,3,2,1,0:T(8,128)(2,1)S(1)}, bf16[1,1,2,256,256]{4,3,2,1,0:T(8,128)(2,1)}, u32[]{:S(2)}) copy-start(bf16[1,1,2,256,256]{4,3,2,1,0:T(8,128)(2,1)} %param.11) | copy-start | bytes 786436
  0.6 22.0 %collective-permute-start = (f32[2,2,128,128]{3,2,1,0:T(8,128)}, f32[2,2,128,128]{3,2,1,0:T(8,128)S(1)}, u32[]{:S(2)}, u32[]{:S(2)}) collective-permute-start(f32[2,2,128,128]{3,2,1,0:T(8,128)} %own.3), channel_id=1, source_target_pairs={{0,16},{16,0},{32,48},{48,32},{64,80},{80,64},{96,112},{112,96},{1... | collective-permute-start | bytes 786440 | tf_op jit(solution)/shard_map/ppermute | solution.py:355
  17.1 1.1 copy-start.7
  17.1 1.2 copy-start.8
  17.1 1.4 copy-start.4
  17.1 1.3 copy-start.6
  18.2 1.7 %copy-start.1 = (bf16[4,2,256,256]{3,2,1,0:T(8,128)(2,1)S(1)}, bf16[4,2,256,256]{3,2,1,0:T(8,128)(2,1)}, u32[]{:S(2)}) copy-start(bf16[4,2,256,256]{3,2,1,0:T(8,128)(2,1)} %constant.40.clone.stored) | copy-start | bytes 3145732
  19.8 0.9 copy-start.5
  22.6 7.8 %collective-permute-start.1 = (f32[2,2,128,128]{3,2,1,0:T(8,128)S(1)}, f32[2,2,128,128]{3,2,1,0:T(8,128)S(1)}, u32[]{:S(2)}, u32[]{:S(2)}) collective-permute-start(f32[2,2,128,128]{3,2,1,0:T(8,128)S(1)} %collective-permute-done.near), channel_id=1, source_target_pairs={{0,32},{32,64},{64,96},{96,128},{128,160},{160,192},{192,224},{224... | collective-permute-start | bytes 786440 | tf_op jit(solution)/shard_map/ppermute | solution.py:370
  30.5 27.8 %copy-start.2 = (f32[2,2,128,128]{3,2,1,0:T(8,128)S(1)}, f32[2,2,128,128]{3,2,1,0:T(8,128)}, u32[]{:S(2)}) copy-start(f32[2,2,128,128]{3,2,1,0:T(8,128)} %own.3) | copy-start | bytes 786436
  30.5 27.8 %copy-start.3 = (bf16[2,256,256]{2,1,0:T(8,128)(2,1)S(1)}, bf16[2,256,256]{2,1,0:T(8,128)(2,1)}, u32[]{:S(2)}) copy-start(bf16[2,256,256]{2,1,0:T(8,128)(2,1)} %probe.3) | copy-start | bytes 786436
  30.5 27.8 %collective-permute-start.5 = (f32[3,2,128,128]{3,2,1,0:T(8,128)S(1)}, f32[3,2,128,128]{3,2,1,0:T(8,128)S(1)}, u32[]{:S(2)}, u32[]{:S(2)}) collective-permute-start(f32[3,2,128,128]{3,2,1,0:T(8,128)S(1)} %get-tuple-element.40), channel_id=1, source_target_pairs={{1,2},{3,4},{5,6},{7,8},{9,10},{11,12},{13,14},{2,1},{4,3},{6,5},{... | collective-permute-start | bytes 1179656 | tf_op jit(solution)/shard_map/ppermute | solution.py:330
  52.5 5.8 %collective-permute-start.4 = (f32[3,2,128,128]{3,2,1,0:T(8,128)S(1)}, f32[3,2,128,128]{3,2,1,0:T(8,128)S(1)}, u32[]{:S(2)}, u32[]{:S(2)}) collective-permute-start(f32[3,2,128,128]{3,2,1,0:T(8,128)S(1)} %get-tuple-element.40), channel_id=1, source_target_pairs={{0,1},{1,0},{2,3},{3,2},{4,5},{5,4},{6,7},{7,6},{8,9},{9,8},{10,11... | collective-permute-start | bytes 1179656 | tf_op jit(solution)/shard_map/ppermute | solution.py:331
  54.4 9.1 %collective-permute-start.3 = (f32[3,2,128,128]{3,2,1,0:T(8,128)S(1)}, f32[3,2,128,128]{3,2,1,0:T(8,128)S(1)}, u32[]{:S(2)}, u32[]{:S(2)}) collective-permute-start(f32[3,2,128,128]{3,2,1,0:T(8,128)S(1)} %get-tuple-element.41), channel_id=1, source_target_pairs={{1,2},{3,4},{5,6},{7,8},{9,10},{11,12},{13,14},{2,1},{4,3},{6,5},{... | collective-permute-start | bytes 1179656 | tf_op jit(solution)/shard_map/ppermute | solution.py:330
  56.3 7.2 %collective-permute-start.2 = (f32[3,2,128,128]{3,2,1,0:T(8,128)S(1)}, f32[3,2,128,128]{3,2,1,0:T(8,128)S(1)}, u32[]{:S(2)}, u32[]{:S(2)}) collective-permute-start(f32[3,2,128,128]{3,2,1,0:T(8,128)S(1)} %get-tuple-element.41), channel_id=1, source_target_pairs={{0,1},{1,0},{2,3},{3,2},{4,5},{5,4},{6,7},{7,6},{8,9},{9,8},{10,11... | collective-permute-start | bytes 1179656 | tf_op jit(solution)/shard_map/ppermute | solution.py:331
  71.5 9.6 %collective-permute-start.6 = (f32[3,2,2,128,128]{4,3,2,1,0:T(8,128)S(1)}, f32[3,2,2,128,128]{4,3,2,1,0:T(8,128)S(1)}, u32[]{:S(2)}, u32[]{:S(2)}) collective-permute-start(f32[3,2,2,128,128]{4,3,2,1,0:T(8,128)S(1)} %get-tuple-element.32), channel_id=1, source_target_pairs={{0,1},{1,0},{2,3},{3,2},{4,5},{5,4},{6,7},{7,6},{8,9},{9,8},{10,11... | collective-permute-start | bytes 2359304 | tf_op jit(solution)/shard_map/ppermute | solution.py:383
  73.4 7.7 %collective-permute-start.8 = (f32[2,2,128,128]{3,2,1,0:T(8,128)S(1)}, f32[2,2,128,128]{3,2,1,0:T(8,128)S(1)}, u32[]{:S(2)}, u32[]{:S(2)}) collective-permute-start(f32[2,2,128,128]{3,2,1,0:T(8,128)S(1)} %get-tuple-element.36), channel_id=1, source_target_pairs={{1,2},{3,4},{5,6},{7,8},{9,10},{11,12},{13,14},{2,1},{4,3},{6,5},{... | collective-permute-start | bytes 786440 | tf_op jit(solution)/shard_map/ppermute | solution.py:381
  75.8 16.2 %collective-permute-start.7 = (f32[2,2,2,128,128]{4,3,2,1,0:T(8,128)}, f32[2,2,2,128,128]{4,3,2,1,0:T(8,128)S(1)}, u32[]{:S(2)}, u32[]{:S(2)}) collective-permute-start(f32[2,2,2,128,128]{4,3,2,1,0:T(8,128)} %get-tuple-element.33), channel_id=1, source_target_pairs={{1,2},{3,4},{5,6},{7,8},{9,10},{11,12},{13,14},{2,1},{4,3},{6,5},{... | collective-permute-start | bytes 1572872 | tf_op jit(solution)/shard_map/ppermute | solution.py:382
  81.2 10.8 %collective-permute-start.9 = (f32[2,2,128,128]{3,2,1,0:T(8,128)S(1)}, f32[2,2,128,128]{3,2,1,0:T(8,128)S(1)}, u32[]{:S(2)}, u32[]{:S(2)}) collective-permute-start(f32[2,2,128,128]{3,2,1,0:T(8,128)S(1)} %fusion.4), channel_id=1, source_target_pairs={{32,0},{64,32},{96,64},{128,96},{160,128},{192,160},{224,192},{256... | collective-permute-start | bytes 786440 | tf_op jit(solution)/shard_map/ppermute | solution.py:385
  82.5 23.6 %all-to-all-start = ((f32[16,2,16,256]{3,2,1,0:T(8,128)}), f32[16,2,16,256]{3,2,1,0:T(8,128)S(1)}, u32[]{:S(2)}, u32[]{:S(2)}) async-start(f32[16,2,16,256]{3,2,1,0:T(8,128)} %get-tuple-element.37), calls=%async_computation | async-start | bytes 1048576 | tf_op jit(solution)/shard_map/all_to_all | solution.py:337
  92.1 33.6 %collective-permute-start.10 = (f32[2,2,128,128]{3,2,1,0:T(8,128)S(1)}, f32[2,2,128,128]{3,2,1,0:T(8,128)S(1)}, u32[]{:S(2)}, u32[]{:S(2)}) collective-permute-start(f32[2,2,128,128]{3,2,1,0:T(8,128)S(1)} %fusion.6), channel_id=1, source_target_pairs={{0,16},{16,0},{32,48},{48,32},{64,80},{80,64},{96,112},{112,96},{1... | collective-permute-start | bytes 786440 | tf_op jit(solution)/shard_map/ppermute | solution.py:388
  107.1 28.7 %all-to-all-start.1 = ((f32[32,2,128]{2,1,0:T(2,128)}), f32[32,2,128]{2,1,0:T(2,128)S(1)}, u32[]{:S(2)}, u32[]{:S(2)}) async-start(f32[32,2,128]{2,1,0:T(2,128)} %reshape.26), calls=%async_computation.1 | async-start | bytes 65536 | tf_op jit(solution)/shard_map/all_to_all | solution.py:345

commit v7 on v6

--- a/solution.py
+++ b/solution.py
@@ -77,7 +77,8 @@
     if axis == 1:
         out = right_mul(jnp.concatenate(values, axis=0), tables, index)
         return [out[n * WIN:(n + 1) * WIN] for n in range(len(values))]
-    return [left_mul(tables, index, value) for value in values]
+    out = left_mul(tables, index, jnp.concatenate(values, axis=1))
+    return [out[:, n * WIN:(n + 1) * WIN] for n in range(len(values))]
 
 
 def forward_axis(fields, tables, axis):

time: 137 us -> 137 us (level)
  no operation moved by 1% of the time
where the time goes in v7:
time: 137 us
  starting transfers between devices  91.4 us (67%)
  waiting for transfers between devices  26.3 us (19%)
  Pallas kernels  11.3 us (8%)
  local copies, waits for them, and re-layouts  3.72 us (3%)
  matrix products  1.52 us (1%)
    ppermute x2, starting transfers between devices, sides(): other = lax.ppermute(value, 'col', inner + flipped(inner))  23.9 us
    ppermute x1, starting transfers between devices, per_device(): near = lax.ppermute(object_slices, 'row', swap)  16.4 us
    ppermute x1, starting transfers between devices, per_device(): own = own + sibling[0] + other[0] + lax.ppermute(near, 'row', swap)  14 us
    all_to_all x1, starting transfers between devices, probe_block(): lax.all_to_all(parts, ('row', 'col'), 0, 0, tiled=True, axis_index_groups...  11.5 us
    all_to_all x1, waiting for transfers between devices, probe_block(): lax.all_to_all(parts, ('row', 'col'), 0, 0, tiled=True, axis_index_groups...  9.42 us
    all_to_all x1, starting transfers between devices, probe_rows(): lax.all_to_all(term, 'row', 0, 0, tiled=True, axis_index_groups=groups)  9.17 us
    pallas_call x1, Pallas kernels, back(): call(back_kernel, [shaped(2, 2, HALF, HALF)] * 3 + [shaped(3, 2, 2, HALF,...  8.04 us
    ppermute x1, waiting for transfers between devices, per_device(): own = own + sibling[0] + other[0] + lax.ppermute(near, 'row', swap)  6.97 us
  transfers between devices with their start and end apart: 13, of which 6 were waited for; matrix products, arithmetic and copies ran while one was open for 4% of the time, Pallas kernels for 2%

profile of v7, /device:TPU:1, one launch (start us, length us, event | category | flops | bytes accessed | tf_op | source)
XLA Modules:
  0.0 136.5 jit_solution(1542180987583639388)
XLA Ops:
  0.6 16.4 %collective-permute-start = (f32[2,2,128,128]{3,2,1,0:T(8,128)}, f32[2,2,128,128]{3,2,1,0:T(8,128)S(1)}, u32[]{:S(2)}, u32[]{:S(2)}) collective-permute-start(f32[2,2,128,128]{3,2,1,0:T(8,128)} %own.3), channel_id=1, source_target_pairs={{0,16},{16,0},{32,48},{48,32},{64,80},{80,64},{96,112},{112,96},{1... | collective-permute-start | bytes 786440 | tf_op jit(solution)/shard_map/ppermute | solution.py:356
  17.1 1.0 fusion.14
  18.4 0.1 sub.18
  18.5 1.2 cosine_bitcast_fusion
  19.8 0.1 shard_map.95.tables
  19.9 0.8 copy-done.5
  20.7 0.4 fusion.1.intensity
  21.1 1.5 %collective-permute-done.near = f32[2,2,128,128]{3,2,1,0:T(8,128)S(1)} collective-permute-done((f32[2,2,128,128]{3,2,1,0:T(8,128)}, f32[2,2,128,128]{3,2,1,0:T(8,128)S(1)}, u32[]{:S(2)}, u32[]{:S(2)}) %collective-permute-start) | collective-permute-done | bytes 262176 | tf_op jit(solution)/shard_map/ppermute | solution.py:356
  22.6 3.8 %collective-permute-start.1 = (f32[2,2,128,128]{3,2,1,0:T(8,128)S(1)}, f32[2,2,128,128]{3,2,1,0:T(8,128)S(1)}, u32[]{:S(2)}, u32[]{:S(2)}) collective-permute-start(f32[2,2,128,128]{3,2,1,0:T(8,128)S(1)} %collective-permute-done.near), channel_id=1, source_target_pairs={{0,32},{32,64},{64,96},{96,128},{128,160},{160,192},{192,224},{224... | collective-permute-start | bytes 786440 | tf_op jit(solution)/shard_map/ppermute | solution.py:371
  26.5 4.0 %collective-permute-done.1.far = f32[2,2,128,128]{3,2,1,0:T(8,128)S(1)} collective-permute-done((f32[2,2,128,128]{3,2,1,0:T(8,128)S(1)}, f32[2,2,128,128]{3,2,1,0:T(8,128)S(1)}, u32[]{:S(2)}, u32[]{:S(2)}) %collective-permute-start.1) | collective-permute-done | bytes 262176 | tf_op jit(solution)/shard_map/ppermute | solution.py:371
  30.5 22.0 %collective-permute-start.5 = (f32[3,2,128,128]{3,2,1,0:T(8,128)S(1)}, f32[3,2,128,128]{3,2,1,0:T(8,128)S(1)}, u32[]{:S(2)}, u32[]{:S(2)}) collective-permute-start(f32[3,2,128,128]{3,2,1,0:T(8,128)S(1)} %get-tuple-element.40), channel_id=1, source_target_pairs={{1,2},{3,4},{5,6},{7,8},{9,10},{11,12},{13,14},{2,1},{4,3},{6,5},{... | collective-permute-start | bytes 1179656 | tf_op jit(solution)/shard_map/ppermute | solution.py:331
  52.5 1.9 %collective-permute-start.4 = (f32[3,2,128,128]{3,2,1,0:T(8,128)S(1)}, f32[3,2,128,128]{3,2,1,0:T(8,128)S(1)}, u32[]{:S(2)}, u32[]{:S(2)}) collective-permute-start(f32[3,2,128,128]{3,2,1,0:T(8,128)S(1)} %get-tuple-element.40), channel_id=1, source_target_pairs={{0,1},{1,0},{2,3},{3,2},{4,5},{5,4},{6,7},{7,6},{8,9},{9,8},{10,11... | collective-permute-start | bytes 1179656 | tf_op jit(solution)/shard_map/ppermute | solution.py:332
  54.4 1.9 %collective-permute-start.3 = (f32[3,2,128,128]{3,2,1,0:T(8,128)S(1)}, f32[3,2,128,128]{3,2,1,0:T(8,128)S(1)}, u32[]{:S(2)}, u32[]{:S(2)}) collective-permute-start(f32[3,2,128,128]{3,2,1,0:T(8,128)S(1)} %get-tuple-element.41), channel_id=1, source_target_pairs={{1,2},{3,4},{5,6},{7,8},{9,10},{11,12},{13,14},{2,1},{4,3},{6,5},{... | collective-permute-start | bytes 1179656 | tf_op jit(solution)/shard_map/ppermute | solution.py:331
  56.3 1.9 %collective-permute-start.2 = (f32[3,2,128,128]{3,2,1,0:T(8,128)S(1)}, f32[3,2,128,128]{3,2,1,0:T(8,128)S(1)}, u32[]{:S(2)}, u32[]{:S(2)}) collective-permute-start(f32[3,2,128,128]{3,2,1,0:T(8,128)S(1)} %get-tuple-element.41), channel_id=1, source_target_pairs={{0,1},{1,0},{2,3},{3,2},{4,5},{5,4},{6,7},{7,6},{8,9},{9,8},{10,11... | collective-permute-start | bytes 1179656 | tf_op jit(solution)/shard_map/ppermute | solution.py:332
  58.3 3.2 %shard_map.96 = (f32[2,2,256,256]{3,2,1,0:T(8,128)S(1)}, f32[2,2,256,256]{3,2,1,0:T(8,128)S(1)}) custom-call(s32[8]{0:T(128)S(1)} %pad_add_fusion.1.place, f32[2,2,128,128]{3,2,1,0:T(8,128)S(1)} %copy-done.2, f32[2,2,128,128]{3,2,1,0:T(8,128)S(1)} %collective-permute-done.near, f32[2,2,128,128]{3,2,1,0:T(8,128)S(1)} %collective-permute-done.1.far, ...), custom_call_target="tpu_custom_call" | custom-call | flops 3300000000 | bytes 4000000 | tf_op jit(solution)/shard_map/pallas_call | solution.py:300
  61.5 2.0 %collective-permute-done.3.other = f32[3,2,128,128]{3,2,1,0:T(8,128)S(1)} collective-permute-done((f32[3,2,128,128]{3,2,1,0:T(8,128)S(1)}, f32[3,2,128,128]{3,2,1,0:T(8,128)S(1)}, u32[]{:S(2)}, u32[]{:S(2)}) %collective-permute-start.3) | collective-permute-done | bytes 393248 | tf_op jit(solution)/shard_map/ppermute | solution.py:331
  63.5 8.0 %shard_map.97 = (f32[2,2,128,128]{3,2,1,0:T(8,128)S(1)}, f32[2,2,128,128]{3,2,1,0:T(8,128)S(1)}, f32[2,2,128,128]{3,2,1,0:T(8,128)S(1)}, f32[3,2,2,128,128]{4,3,...) custom-call(s32[8]{0:T(128)S(1)} %pad_add_fusion.1.place, ...), custom_call_target="tpu_custom_call" | custom-call | flops 6600000000 | bytes 4000000 | tf_op jit(solution)/shard_map/pallas_call | solution.py:311
  71.6 1.9 %collective-permute-start.6 = (f32[3,2,2,128,128]{4,3,2,1,0:T(8,128)S(1)}, f32[3,2,2,128,128]{4,3,2,1,0:T(8,128)S(1)}, u32[]{:S(2)}, u32[]{:S(2)}) collective-permute-start(f32[3,2,2,128,128]{4,3,2,1,0:T(8,128)S(1)} %get-tuple-element.32), channel_id=1, source_target_pairs={{0,1},{1,0},{2,3},{3,2},{4,5},{5,4},{6,7},{7,6},{8,9},{9,8},{10,11... | collective-permute-start | bytes 2359304 | tf_op jit(solution)/shard_map/ppermute | solution.py:384
  73.5 2.4 %collective-permute-start.8 = (f32[2,2,128,128]{3,2,1,0:T(8,128)S(1)}, f32[2,2,128,128]{3,2,1,0:T(8,128)S(1)}, u32[]{:S(2)}, u32[]{:S(2)}) collective-permute-start(f32[2,2,128,128]{3,2,1,0:T(8,128)S(1)} %get-tuple-element.36), channel_id=1, source_target_pairs={{1,2},{3,4},{5,6},{7,8},{9,10},{11,12},{13,14},{2,1},{4,3},{6,5},{... | collective-permute-start | bytes 786440 | tf_op jit(solution)/shard_map/ppermute | solution.py:382
  75.9 3.2 %collective-permute-start.7 = (f32[2,2,2,128,128]{4,3,2,1,0:T(8,128)}, f32[2,2,2,128,128]{4,3,2,1,0:T(8,128)S(1)}, u32[]{:S(2)}, u32[]{:S(2)}) collective-permute-start(f32[2,2,2,128,128]{4,3,2,1,0:T(8,128)} %get-tuple-element.33), channel_id=1, source_target_pairs={{1,2},{3,4},{5,6},{7,8},{9,10},{11,12},{13,14},{2,1},{4,3},{6,5},{... | collective-permute-start | bytes 1572872 | tf_op jit(solution)/shard_map/ppermute | solution.py:383
  79.1 2.4 %collective-permute-done.8 = f32[2,2,128,128]{3,2,1,0:T(8,128)S(1)} collective-permute-done((f32[2,2,128,128]{3,2,1,0:T(8,128)S(1)}, f32[2,2,128,128]{3,2,1,0:T(8,128)S(1)}, u32[]{:S(2)}, u32[]{:S(2)}) %collective-permute-start.8) | collective-permute-done | bytes 262176 | tf_op jit(solution)/shard_map/ppermute | solution.py:382
  81.5 1.3 collective-permute-start.9
  82.8 9.2 %all-to-all-start = ((f32[16,2,16,256]{3,2,1,0:T(8,128)}), f32[16,2,16,256]{3,2,1,0:T(8,128)S(1)}, u32[]{:S(2)}, u32[]{:S(2)}) async-start(f32[16,2,16,256]{3,2,1,0:T(8,128)} %get-tuple-element.37), calls=%async_computation | async-start | bytes 1048576 | tf_op jit(solution)/shard_map/all_to_all | solution.py:338
  92.1 14.0 %collective-permute-start.10 = (f32[2,2,128,128]{3,2,1,0:T(8,128)S(1)}, f32[2,2,128,128]{3,2,1,0:T(8,128)S(1)}, u32[]{:S(2)}, u32[]{:S(2)}) collective-permute-start(f32[2,2,128,128]{3,2,1,0:T(8,128)S(1)} %fusion.6), channel_id=1, source_target_pairs={{0,16},{16,0},{32,48},{48,32},{64,80},{80,64},{96,112},{112,96},{1... | collective-permute-start | bytes 786440 | tf_op jit(solution)/shard_map/ppermute | solution.py:389
  106.2 0.1 reshape.21
  106.3 0.1 copy.13
  106.4 0.7 reshape.26
  107.1 11.5 %all-to-all-start.1 = ((f32[32,2,128]{2,1,0:T(2,128)}), f32[32,2,128]{2,1,0:T(2,128)S(1)}, u32[]{:S(2)}, u32[]{:S(2)}) async-start(f32[32,2,128]{2,1,0:T(2,128)} %reshape.26), calls=%async_computation.1 | async-start | bytes 65536 | tf_op jit(solution)/shard_map/all_to_all | solution.py:346
  118.6 7.0 %collective-permute-done.10 = f32[2,2,128,128]{3,2,1,0:T(8,128)S(1)} collective-permute-done((f32[2,2,128,128]{3,2,1,0:T(8,128)S(1)}, f32[2,2,128,128]{3,2,1,0:T(8,128)S(1)}, u32[]{:S(2)}, u32[]{:S(2)}) %collective-permute-start.10) | collective-permute-done | bytes 262176 | tf_op jit(solution)/shard_map/ppermute | solution.py:389
  125.6 0.8 fusion.9
  126.4 9.4 %all-to-all-done.1 = f32[32,2,128]{2,1,0:T(2,128)S(1)} async-done(((f32[32,2,128]{2,1,0:T(2,128)}), f32[32,2,128]{2,1,0:T(2,128)S(1)}, u32[]{:S(2)}, u32[]{:S(2)}) %all-to-all-start.1) | async-done | bytes 32800 | tf_op jit(solution)/shard_map/all_to_all | solution.py:346
  135.8 0.7 reshape.23
  (39 shorter events, 0.7 us)
Async XLA Ops:
  0.6 19.3 %copy-start = (bf16[1,1,2,256,256]{4,3,2,1,0:T(8,128)(2,1)S(1)}, bf16[1,1,2,256,256]{4,3,2,1,0:T(8,128)(2,1)}, u32[]{:S(2)}) copy-start(bf16[1,1,2,256,256]{4,3,2,1,0:T(8,128)(2,1)} %param.11) | copy-start | bytes 786436
  0.6 22.0 %collective-permute-start = (f32[2,2,128,128]{3,2,1,0:T(8,128)}, f32[2,2,128,128]{3,2,1,0:T(8,128)S(1)}, u32[]{:S(2)}, u32[]{:S(2)}) collective-permute-start(f32[2,2,128,128]{3,2,1,0:T(8,128)} %own.3), channel_id=1, source_target_pairs={{0,16},{16,0},{32,48},{48,32},{64,80},{80,64},{96,112},{112,96},{1... | collective-permute-start | bytes 786440 | tf_op jit(solution)/shard_map/ppermute | solution.py:356
  17.1 1.1 copy-start.7
  17.1 1.2 copy-start.8
  17.1 1.4 copy-start.4
  17.1 1.3 copy-start.6
  18.2 1.7 %copy-start.1 = (bf16[4,2,256,256]{3,2,1,0:T(8,128)(2,1)S(1)}, bf16[4,2,256,256]{3,2,1,0:T(8,128)(2,1)}, u32[]{:S(2)}) copy-start(bf16[4,2,256,256]{3,2,1,0:T(8,128)(2,1)} %constant.40.clone.stored) | copy-start | bytes 3145732
  19.8 0.9 copy-start.5
  22.6 7.8 %collective-permute-start.1 = (f32[2,2,128,128]{3,2,1,0:T(8,128)S(1)}, f32[2,2,128,128]{3,2,1,0:T(8,128)S(1)}, u32[]{:S(2)}, u32[]{:S(2)}) collective-permute-start(f32[2,2,128,128]{3,2,1,0:T(8,128)S(1)} %collective-permute-done.near), channel_id=1, source_target_pairs={{0,32},{32,64},{64,96},{96,128},{128,160},{160,192},{192,224},{224... | collective-permute-start | bytes 786440 | tf_op jit(solution)/shard_map/ppermute | solution.py:371
  30.5 27.8 %copy-start.2 = (f32[2,2,128,128]{3,2,1,0:T(8,128)S(1)}, f32[2,2,128,128]{3,2,1,0:T(8,128)}, u32[]{:S(2)}) copy-start(f32[2,2,128,128]{3,2,1,0:T(8,128)} %own.3) | copy-start | bytes 786436
  30.5 27.8 %copy-start.3 = (bf16[2,256,256]{2,1,0:T(8,128)(2,1)S(1)}, bf16[2,256,256]{2,1,0:T(8,128)(2,1)}, u32[]{:S(2)}) copy-start(bf16[2,256,256]{2,1,0:T(8,128)(2,1)} %probe.3) | copy-start | bytes 786436
  30.5 27.8 %collective-permute-start.5 = (f32[3,2,128,128]{3,2,1,0:T(8,128)S(1)}, f32[3,2,128,128]{3,2,1,0:T(8,128)S(1)}, u32[]{:S(2)}, u32[]{:S(2)}) collective-permute-start(f32[3,2,128,128]{3,2,1,0:T(8,128)S(1)} %get-tuple-element.40), channel_id=1, source_target_pairs={{1,2},{3,4},{5,6},{7,8},{9,10},{11,12},{13,14},{2,1},{4,3},{6,5},{... | collective-permute-start | bytes 1179656 | tf_op jit(solution)/shard_map/ppermute | solution.py:331
  52.5 5.8 %collective-permute-start.4 = (f32[3,2,128,128]{3,2,1,0:T(8,128)S(1)}, f32[3,2,128,128]{3,2,1,0:T(8,128)S(1)}, u32[]{:S(2)}, u32[]{:S(2)}) collective-permute-start(f32[3,2,128,128]{3,2,1,0:T(8,128)S(1)} %get-tuple-element.40), channel_id=1, source_target_pairs={{0,1},{1,0},{2,3},{3,2},{4,5},{5,4},{6,7},{7,6},{8,9},{9,8},{10,11... | collective-permute-start | bytes 1179656 | tf_op jit(solution)/shard_map/ppermute | solution.py:332
  54.4 9.1 %collective-permute-start.3 = (f32[3,2,128,128]{3,2,1,0:T(8,128)S(1)}, f32[3,2,128,128]{3,2,1,0:T(8,128)S(1)}, u32[]{:S(2)}, u32[]{:S(2)}) collective-permute-start(f32[3,2,128,128]{3,2,1,0:T(8,128)S(1)} %get-tuple-element.41), channel_id=1, source_target_pairs={{1,2},{3,4},{5,6},{7,8},{9,10},{11,12},{13,14},{2,1},{4,3},{6,5},{... | collective-permute-start | bytes 1179656 | tf_op jit(solution)/shard_map/ppermute | solution.py:331
  56.3 7.2 %collective-permute-start.2 = (f32[3,2,128,128]{3,2,1,0:T(8,128)S(1)}, f32[3,2,128,128]{3,2,1,0:T(8,128)S(1)}, u32[]{:S(2)}, u32[]{:S(2)}) collective-permute-start(f32[3,2,128,128]{3,2,1,0:T(8,128)S(1)} %get-tuple-element.41), channel_id=1, source_target_pairs={{0,1},{1,0},{2,3},{3,2},{4,5},{5,4},{6,7},{7,6},{8,9},{9,8},{10,11... | collective-permute-start | bytes 1179656 | tf_op jit(solution)/shard_map/ppermute | solution.py:332
  71.6 9.9 %collective-permute-start.6 = (f32[3,2,2,128,128]{4,3,2,1,0:T(8,128)S(1)}, f32[3,2,2,128,128]{4,3,2,1,0:T(8,128)S(1)}, u32[]{:S(2)}, u32[]{:S(2)}) collective-permute-start(f32[3,2,2,128,128]{4,3,2,1,0:T(8,128)S(1)} %get-tuple-element.32), channel_id=1, source_target_pairs={{0,1},{1,0},{2,3},{3,2},{4,5},{5,4},{6,7},{7,6},{8,9},{9,8},{10,11... | collective-permute-start | bytes 2359304 | tf_op jit(solution)/shard_map/ppermute | solution.py:384
  73.5 8.0 %collective-permute-start.8 = (f32[2,2,128,128]{3,2,1,0:T(8,128)S(1)}, f32[2,2,128,128]{3,2,1,0:T(8,128)S(1)}, u32[]{:S(2)}, u32[]{:S(2)}) collective-permute-start(f32[2,2,128,128]{3,2,1,0:T(8,128)S(1)} %get-tuple-element.36), channel_id=1, source_target_pairs={{1,2},{3,4},{5,6},{7,8},{9,10},{11,12},{13,14},{2,1},{4,3},{6,5},{... | collective-permute-start | bytes 786440 | tf_op jit(solution)/shard_map/ppermute | solution.py:382
  75.9 16.1 %collective-permute-start.7 = (f32[2,2,2,128,128]{4,3,2,1,0:T(8,128)}, f32[2,2,2,128,128]{4,3,2,1,0:T(8,128)S(1)}, u32[]{:S(2)}, u32[]{:S(2)}) collective-permute-start(f32[2,2,2,128,128]{4,3,2,1,0:T(8,128)} %get-tuple-element.33), channel_id=1, source_target_pairs={{1,2},{3,4},{5,6},{7,8},{9,10},{11,12},{13,14},{2,1},{4,3},{6,5},{... | collective-permute-start | bytes 1572872 | tf_op jit(solution)/shard_map/ppermute | solution.py:383
  81.5 10.5 %collective-permute-start.9 = (f32[2,2,128,128]{3,2,1,0:T(8,128)S(1)}, f32[2,2,128,128]{3,2,1,0:T(8,128)S(1)}, u32[]{:S(2)}, u32[]{:S(2)}) collective-permute-start(f32[2,2,128,128]{3,2,1,0:T(8,128)S(1)} %fusion.4), channel_id=1, source_target_pairs={{32,0},{64,32},{96,64},{128,96},{160,128},{192,160},{224,192},{256... | collective-permute-start | bytes 786440 | tf_op jit(solution)/shard_map/ppermute | solution.py:386
  82.8 23.3 %all-to-all-start = ((f32[16,2,16,256]{3,2,1,0:T(8,128)}), f32[16,2,16,256]{3,2,1,0:T(8,128)S(1)}, u32[]{:S(2)}, u32[]{:S(2)}) async-start(f32[16,2,16,256]{3,2,1,0:T(8,128)} %get-tuple-element.37), calls=%async_computation | async-start | bytes 1048576 | tf_op jit(solution)/shard_map/all_to_all | solution.py:338
  92.1 33.5 %collective-permute-start.10 = (f32[2,2,128,128]{3,2,1,0:T(8,128)S(1)}, f32[2,2,128,128]{3,2,1,0:T(8,128)S(1)}, u32[]{:S(2)}, u32[]{:S(2)}) collective-permute-start(f32[2,2,128,128]{3,2,1,0:T(8,128)S(1)} %fusion.6), channel_id=1, source_target_pairs={{0,16},{16,0},{32,48},{48,32},{64,80},{80,64},{96,112},{112,96},{1... | collective-permute-start | bytes 786440 | tf_op jit(solution)/shard_map/ppermute | solution.py:389
  107.1 28.7 %all-to-all-start.1 = ((f32[32,2,128]{2,1,0:T(2,128)}), f32[32,2,128]{2,1,0:T(2,128)S(1)}, u32[]{:S(2)}, u32[]{:S(2)}) async-start(f32[32,2,128]{2,1,0:T(2,128)} %reshape.26), calls=%async_computation.1 | async-start | bytes 65536 | tf_op jit(solution)/shard_map/all_to_all | solution.py:346

commit v8 on v7

--- a/solution.py
+++ b/solution.py
@@ -208,7 +208,7 @@
 
 
 def back_kernel(place, weight, own, near, far, sibling, other, waves, layers, probe, propagator, intensity, tables,
-                out_own, out_near, out_far, out_sibling, out_other, out_last, out_probe, field, total0, total1, kept, arrived, left_sem):
+                out_own, out_near, out_far, out_sibling, out_other, out_last, out_probe, field, total0, total1, arrived, left_sem):
     loads = assemble(place, field, 1, own, near, far, sibling, other, arrived)
     for load in loads:
         load.start()
@@ -237,13 +237,11 @@
     adjoint = inverse(fields, tables)
     for slot in two:
         add_window(total1, place, slot, conj_times((waves[slot, 0], waves[slot, 1]), adjoint[slot]))
-        upstream = conj_times(window(field, place, slot), adjoint[slot])
-        for part in range(2):
-            kept[slot, part] = upstream[part]
+    upstream = [conj_times(window(field, place, slot), adjoint[slot]) for slot in two]
     for store in stores(1):
         store.start()
     wave = (probe[0].astype(F32), probe[1].astype(F32))
-    spectra = forward([(kept[slot, 0], kept[slot, 1]) for slot in two], tables)
+    spectra = forward(upstream, tables)
     adjoint = inverse([conj_times(spread, spectrum) for spectrum in spectra], tables)
     for slot in two:
         add_window(total0, place, slot, conj_times(wave, adjoint[slot]))
@@ -316,7 +314,7 @@
         [SMEM] * 2 + [ANYWHERE] * 5 + [VMEM] * 6,
         [ANYWHERE] * 6 + [VMEM],
         [pltpu.VMEM((2, 3 * HALF, 3 * HALF), F32)] * 3
-        + [pltpu.VMEM((2, 2, WIN, WIN), F32), pltpu.SemaphoreType.DMA((9,)), pltpu.SemaphoreType.DMA((2, 9))],
+        + [pltpu.SemaphoreType.DMA((9,)), pltpu.SemaphoreType.DMA((2, 9))],
         6_600_000_000,
     )(place, weight, *tiles, waves, layers, probe, propagator, intensity, tables)
 

time: 137 us -> 137 us (level)
  no operation moved by 1% of the time
where the time goes in v8:
time: 137 us
  starting transfers between devices  91.1 us (66%)
  waiting for transfers between devices  26.7 us (19%)
  Pallas kernels  11.3 us (8%)
  local copies, waits for them, and re-layouts  3.72 us (3%)
  matrix products  1.52 us (1%)
    ppermute x2, starting transfers between devices, sides(): other = lax.ppermute(value, 'col', inner + flipped(inner))  23.9 us
    ppermute x1, starting transfers between devices, per_device(): near = lax.ppermute(object_slices, 'row', swap)  16.4 us
    ppermute x1, starting transfers between devices, per_device(): own = own + sibling[0] + other[0] + lax.ppermute(near, 'row', swap)  14 us
    all_to_all x1, starting transfers between devices, probe_block(): lax.all_to_all(parts, ('row', 'col'), 0, 0, tiled=True, axis_index_groups...  11.1 us
    all_to_all x1, waiting for transfers between devices, probe_block(): lax.all_to_all(parts, ('row', 'col'), 0, 0, tiled=True, axis_index_groups...  9.41 us
    all_to_all x1, starting transfers between devices, probe_rows(): lax.all_to_all(term, 'row', 0, 0, tiled=True, axis_index_groups=groups)  9.17 us
    pallas_call x1, Pallas kernels, back(): call(back_kernel, [shaped(2, 2, HALF, HALF)] * 3 + [shaped(3, 2, 2, HALF,...  8.05 us
    ppermute x1, waiting for transfers between devices, per_device(): own = own + sibling[0] + other[0] + lax.ppermute(near, 'row', swap)  7.35 us
  transfers between devices with their start and end apart: 13, of which 6 were waited for; matrix products, arithmetic and copies ran while one was open for 4% of the time, Pallas kernels for 2%

profile of v8, /device:TPU:1, one launch (start us, length us, event | category | flops | bytes accessed | tf_op | source)
XLA Modules:
  0.0 136.6 jit_solution(16225809922778342518)
XLA Ops:
  0.6 16.4 %collective-permute-start = (f32[2,2,128,128]{3,2,1,0:T(8,128)}, f32[2,2,128,128]{3,2,1,0:T(8,128)S(1)}, u32[]{:S(2)}, u32[]{:S(2)}) collective-permute-start(f32[2,2,128,128]{3,2,1,0:T(8,128)} %own.3), channel_id=1, source_target_pairs={{0,16},{16,0},{32,48},{48,32},{64,80},{80,64},{96,112},{112,96},{1... | collective-permute-start | bytes 786440 | tf_op jit(solution)/shard_map/ppermute | solution.py:354
  17.1 1.0 fusion.14
  18.4 0.1 sub.18
  18.5 1.2 cosine_bitcast_fusion
  19.8 0.1 shard_map.95.tables
  19.9 0.8 copy-done.5
  20.7 0.4 fusion.1.intensity
  21.1 1.5 %collective-permute-done.near = f32[2,2,128,128]{3,2,1,0:T(8,128)S(1)} collective-permute-done((f32[2,2,128,128]{3,2,1,0:T(8,128)}, f32[2,2,128,128]{3,2,1,0:T(8,128)S(1)}, u32[]{:S(2)}, u32[]{:S(2)}) %collective-permute-start) | collective-permute-done | bytes 262176 | tf_op jit(solution)/shard_map/ppermute | solution.py:354
  22.6 3.8 %collective-permute-start.1 = (f32[2,2,128,128]{3,2,1,0:T(8,128)S(1)}, f32[2,2,128,128]{3,2,1,0:T(8,128)S(1)}, u32[]{:S(2)}, u32[]{:S(2)}) collective-permute-start(f32[2,2,128,128]{3,2,1,0:T(8,128)S(1)} %collective-permute-done.near), channel_id=1, source_target_pairs={{0,32},{32,64},{64,96},{96,128},{128,160},{160,192},{192,224},{224... | collective-permute-start | bytes 786440 | tf_op jit(solution)/shard_map/ppermute | solution.py:369
  26.5 4.0 %collective-permute-done.1.far = f32[2,2,128,128]{3,2,1,0:T(8,128)S(1)} collective-permute-done((f32[2,2,128,128]{3,2,1,0:T(8,128)S(1)}, f32[2,2,128,128]{3,2,1,0:T(8,128)S(1)}, u32[]{:S(2)}, u32[]{:S(2)}) %collective-permute-start.1) | collective-permute-done | bytes 262176 | tf_op jit(solution)/shard_map/ppermute | solution.py:369
  30.5 22.0 %collective-permute-start.5 = (f32[3,2,128,128]{3,2,1,0:T(8,128)S(1)}, f32[3,2,128,128]{3,2,1,0:T(8,128)S(1)}, u32[]{:S(2)}, u32[]{:S(2)}) collective-permute-start(f32[3,2,128,128]{3,2,1,0:T(8,128)S(1)} %get-tuple-element.40), channel_id=1, source_target_pairs={{1,2},{3,4},{5,6},{7,8},{9,10},{11,12},{13,14},{2,1},{4,3},{6,5},{... | collective-permute-start | bytes 1179656 | tf_op jit(solution)/shard_map/ppermute | solution.py:329
  52.5 1.9 %collective-permute-start.4 = (f32[3,2,128,128]{3,2,1,0:T(8,128)S(1)}, f32[3,2,128,128]{3,2,1,0:T(8,128)S(1)}, u32[]{:S(2)}, u32[]{:S(2)}) collective-permute-start(f32[3,2,128,128]{3,2,1,0:T(8,128)S(1)} %get-tuple-element.40), channel_id=1, source_target_pairs={{0,1},{1,0},{2,3},{3,2},{4,5},{5,4},{6,7},{7,6},{8,9},{9,8},{10,11... | collective-permute-start | bytes 1179656 | tf_op jit(solution)/shard_map/ppermute | solution.py:330
  54.4 1.9 %collective-permute-start.3 = (f32[3,2,128,128]{3,2,1,0:T(8,128)S(1)}, f32[3,2,128,128]{3,2,1,0:T(8,128)S(1)}, u32[]{:S(2)}, u32[]{:S(2)}) collective-permute-start(f32[3,2,128,128]{3,2,1,0:T(8,128)S(1)} %get-tuple-element.41), channel_id=1, source_target_pairs={{1,2},{3,4},{5,6},{7,8},{9,10},{11,12},{13,14},{2,1},{4,3},{6,5},{... | collective-permute-start | bytes 1179656 | tf_op jit(solution)/shard_map/ppermute | solution.py:329
  56.3 1.9 %collective-permute-start.2 = (f32[3,2,128,128]{3,2,1,0:T(8,128)S(1)}, f32[3,2,128,128]{3,2,1,0:T(8,128)S(1)}, u32[]{:S(2)}, u32[]{:S(2)}) collective-permute-start(f32[3,2,128,128]{3,2,1,0:T(8,128)S(1)} %get-tuple-element.41), channel_id=1, source_target_pairs={{0,1},{1,0},{2,3},{3,2},{4,5},{5,4},{6,7},{7,6},{8,9},{9,8},{10,11... | collective-permute-start | bytes 1179656 | tf_op jit(solution)/shard_map/ppermute | solution.py:330
  58.3 3.2 %shard_map.96 = (f32[2,2,256,256]{3,2,1,0:T(8,128)S(1)}, f32[2,2,256,256]{3,2,1,0:T(8,128)S(1)}) custom-call(s32[8]{0:T(128)S(1)} %pad_add_fusion.1.place, f32[2,2,128,128]{3,2,1,0:T(8,128)S(1)} %copy-done.2, f32[2,2,128,128]{3,2,1,0:T(8,128)S(1)} %collective-permute-done.near, f32[2,2,128,128]{3,2,1,0:T(8,128)S(1)} %collective-permute-done.1.far, ...), custom_call_target="tpu_custom_call" | custom-call | flops 3300000000 | bytes 4000000 | tf_op jit(solution)/shard_map/pallas_call | solution.py:298
  61.5 2.0 %collective-permute-done.3.other = f32[3,2,128,128]{3,2,1,0:T(8,128)S(1)} collective-permute-done((f32[3,2,128,128]{3,2,1,0:T(8,128)S(1)}, f32[3,2,128,128]{3,2,1,0:T(8,128)S(1)}, u32[]{:S(2)}, u32[]{:S(2)}) %collective-permute-start.3) | collective-permute-done | bytes 393248 | tf_op jit(solution)/shard_map/ppermute | solution.py:329
  63.5 8.0 %shard_map.97 = (f32[2,2,128,128]{3,2,1,0:T(8,128)S(1)}, f32[2,2,128,128]{3,2,1,0:T(8,128)S(1)}, f32[2,2,128,128]{3,2,1,0:T(8,128)S(1)}, f32[3,2,2,128,128]{4,3,...) custom-call(s32[8]{0:T(128)S(1)} %pad_add_fusion.1.place, ...), custom_call_target="tpu_custom_call" | custom-call | flops 6600000000 | bytes 4000000 | tf_op jit(solution)/shard_map/pallas_call | solution.py:309
  71.6 1.9 %collective-permute-start.6 = (f32[3,2,2,128,128]{4,3,2,1,0:T(8,128)S(1)}, f32[3,2,2,128,128]{4,3,2,1,0:T(8,128)S(1)}, u32[]{:S(2)}, u32[]{:S(2)}) collective-permute-start(f32[3,2,2,128,128]{4,3,2,1,0:T(8,128)S(1)} %get-tuple-element.32), channel_id=1, source_target_pairs={{0,1},{1,0},{2,3},{3,2},{4,5},{5,4},{6,7},{7,6},{8,9},{9,8},{10,11... | collective-permute-start | bytes 2359304 | tf_op jit(solution)/shard_map/ppermute | solution.py:382
  73.5 2.4 %collective-permute-start.8 = (f32[2,2,128,128]{3,2,1,0:T(8,128)S(1)}, f32[2,2,128,128]{3,2,1,0:T(8,128)S(1)}, u32[]{:S(2)}, u32[]{:S(2)}) collective-permute-start(f32[2,2,128,128]{3,2,1,0:T(8,128)S(1)} %get-tuple-element.36), channel_id=1, source_target_pairs={{1,2},{3,4},{5,6},{7,8},{9,10},{11,12},{13,14},{2,1},{4,3},{6,5},{... | collective-permute-start | bytes 786440 | tf_op jit(solution)/shard_map/ppermute | solution.py:380
  75.9 3.1 %collective-permute-start.7 = (f32[2,2,2,128,128]{4,3,2,1,0:T(8,128)}, f32[2,2,2,128,128]{4,3,2,1,0:T(8,128)S(1)}, u32[]{:S(2)}, u32[]{:S(2)}) collective-permute-start(f32[2,2,2,128,128]{4,3,2,1,0:T(8,128)} %get-tuple-element.33), channel_id=1, source_target_pairs={{1,2},{3,4},{5,6},{7,8},{9,10},{11,12},{13,14},{2,1},{4,3},{6,5},{... | collective-permute-start | bytes 1572872 | tf_op jit(solution)/shard_map/ppermute | solution.py:381
  79.1 2.4 %collective-permute-done.8 = f32[2,2,128,128]{3,2,1,0:T(8,128)S(1)} collective-permute-done((f32[2,2,128,128]{3,2,1,0:T(8,128)S(1)}, f32[2,2,128,128]{3,2,1,0:T(8,128)S(1)}, u32[]{:S(2)}, u32[]{:S(2)}) %collective-permute-start.8) | collective-permute-done | bytes 262176 | tf_op jit(solution)/shard_map/ppermute | solution.py:380
  81.5 1.3 collective-permute-start.9
  82.8 9.2 %all-to-all-start = ((f32[16,2,16,256]{3,2,1,0:T(8,128)}), f32[16,2,16,256]{3,2,1,0:T(8,128)S(1)}, u32[]{:S(2)}, u32[]{:S(2)}) async-start(f32[16,2,16,256]{3,2,1,0:T(8,128)} %get-tuple-element.37), calls=%async_computation | async-start | bytes 1048576 | tf_op jit(solution)/shard_map/all_to_all | solution.py:336
  92.1 14.0 %collective-permute-start.10 = (f32[2,2,128,128]{3,2,1,0:T(8,128)S(1)}, f32[2,2,128,128]{3,2,1,0:T(8,128)S(1)}, u32[]{:S(2)}, u32[]{:S(2)}) collective-permute-start(f32[2,2,128,128]{3,2,1,0:T(8,128)S(1)} %fusion.6), channel_id=1, source_target_pairs={{0,16},{16,0},{32,48},{48,32},{64,80},{80,64},{96,112},{112,96},{1... | collective-permute-start | bytes 786440 | tf_op jit(solution)/shard_map/ppermute | solution.py:387
  106.2 0.1 reshape.21
  106.3 0.1 copy.13
  106.4 0.7 reshape.26
  107.2 11.1 %all-to-all-start.1 = ((f32[32,2,128]{2,1,0:T(2,128)}), f32[32,2,128]{2,1,0:T(2,128)S(1)}, u32[]{:S(2)}, u32[]{:S(2)}) async-start(f32[32,2,128]{2,1,0:T(2,128)} %reshape.26), calls=%async_computation.1 | async-start | bytes 65536 | tf_op jit(solution)/shard_map/all_to_all | solution.py:344
  118.3 7.3 %collective-permute-done.10 = f32[2,2,128,128]{3,2,1,0:T(8,128)S(1)} collective-permute-done((f32[2,2,128,128]{3,2,1,0:T(8,128)S(1)}, f32[2,2,128,128]{3,2,1,0:T(8,128)S(1)}, u32[]{:S(2)}, u32[]{:S(2)}) %collective-permute-start.10) | collective-permute-done | bytes 262176 | tf_op jit(solution)/shard_map/ppermute | solution.py:387
  125.7 0.8 fusion.9
  126.4 9.4 %all-to-all-done.1 = f32[32,2,128]{2,1,0:T(2,128)S(1)} async-done(((f32[32,2,128]{2,1,0:T(2,128)}), f32[32,2,128]{2,1,0:T(2,128)S(1)}, u32[]{:S(2)}, u32[]{:S(2)}) %all-to-all-start.1) | async-done | bytes 32800 | tf_op jit(solution)/shard_map/all_to_all | solution.py:344
  135.9 0.7 reshape.23
  (39 shorter events, 0.7 us)
Async XLA Ops:
  0.6 19.3 %copy-start = (bf16[1,1,2,256,256]{4,3,2,1,0:T(8,128)(2,1)S(1)}, bf16[1,1,2,256,256]{4,3,2,1,0:T(8,128)(2,1)}, u32[]{:S(2)}) copy-start(bf16[1,1,2,256,256]{4,3,2,1,0:T(8,128)(2,1)} %param.11) | copy-start | bytes 786436
  0.6 22.0 %collective-permute-start = (f32[2,2,128,128]{3,2,1,0:T(8,128)}, f32[2,2,128,128]{3,2,1,0:T(8,128)S(1)}, u32[]{:S(2)}, u32[]{:S(2)}) collective-permute-start(f32[2,2,128,128]{3,2,1,0:T(8,128)} %own.3), channel_id=1, source_target_pairs={{0,16},{16,0},{32,48},{48,32},{64,80},{80,64},{96,112},{112,96},{1... | collective-permute-start | bytes 786440 | tf_op jit(solution)/shard_map/ppermute | solution.py:354
  17.1 1.1 copy-start.7
  17.1 1.2 copy-start.8
  17.1 1.4 copy-start.4
  17.1 1.3 copy-start.6
  18.2 1.7 %copy-start.1 = (bf16[4,2,256,256]{3,2,1,0:T(8,128)(2,1)S(1)}, bf16[4,2,256,256]{3,2,1,0:T(8,128)(2,1)}, u32[]{:S(2)}) copy-start(bf16[4,2,256,256]{3,2,1,0:T(8,128)(2,1)} %constant.40.clone.stored) | copy-start | bytes 3145732
  19.8 0.9 copy-start.5
  22.6 7.8 %collective-permute-start.1 = (f32[2,2,128,128]{3,2,1,0:T(8,128)S(1)}, f32[2,2,128,128]{3,2,1,0:T(8,128)S(1)}, u32[]{:S(2)}, u32[]{:S(2)}) collective-permute-start(f32[2,2,128,128]{3,2,1,0:T(8,128)S(1)} %collective-permute-done.near), channel_id=1, source_target_pairs={{0,32},{32,64},{64,96},{96,128},{128,160},{160,192},{192,224},{224... | collective-permute-start | bytes 786440 | tf_op jit(solution)/shard_map/ppermute | solution.py:369
  30.5 27.8 %copy-start.2 = (f32[2,2,128,128]{3,2,1,0:T(8,128)S(1)}, f32[2,2,128,128]{3,2,1,0:T(8,128)}, u32[]{:S(2)}) copy-start(f32[2,2,128,128]{3,2,1,0:T(8,128)} %own.3) | copy-start | bytes 786436
  30.5 27.8 %copy-start.3 = (bf16[2,256,256]{2,1,0:T(8,128)(2,1)S(1)}, bf16[2,256,256]{2,1,0:T(8,128)(2,1)}, u32[]{:S(2)}) copy-start(bf16[2,256,256]{2,1,0:T(8,128)(2,1)} %probe.3) | copy-start | bytes 786436
  30.5 27.8 %collective-permute-start.5 = (f32[3,2,128,128]{3,2,1,0:T(8,128)S(1)}, f32[3,2,128,128]{3,2,1,0:T(8,128)S(1)}, u32[]{:S(2)}, u32[]{:S(2)}) collective-permute-start(f32[3,2,128,128]{3,2,1,0:T(8,128)S(1)} %get-tuple-element.40), channel_id=1, source_target_pairs={{1,2},{3,4},{5,6},{7,8},{9,10},{11,12},{13,14},{2,1},{4,3},{6,5},{... | collective-permute-start | bytes 1179656 | tf_op jit(solution)/shard_map/ppermute | solution.py:329
  52.5 5.8 %collective-permute-start.4 = (f32[3,2,128,128]{3,2,1,0:T(8,128)S(1)}, f32[3,2,128,128]{3,2,1,0:T(8,128)S(1)}, u32[]{:S(2)}, u32[]{:S(2)}) collective-permute-start(f32[3,2,128,128]{3,2,1,0:T(8,128)S(1)} %get-tuple-element.40), channel_id=1, source_target_pairs={{0,1},{1,0},{2,3},{3,2},{4,5},{5,4},{6,7},{7,6},{8,9},{9,8},{10,11... | collective-permute-start | bytes 1179656 | tf_op jit(solution)/shard_map/ppermute | solution.py:330
  54.4 9.1 %collective-permute-start.3 = (f32[3,2,128,128]{3,2,1,0:T(8,128)S(1)}, f32[3,2,128,128]{3,2,1,0:T(8,128)S(1)}, u32[]{:S(2)}, u32[]{:S(2)}) collective-permute-start(f32[3,2,128,128]{3,2,1,0:T(8,128)S(1)} %get-tuple-element.41), channel_id=1, source_target_pairs={{1,2},{3,4},{5,6},{7,8},{9,10},{11,12},{13,14},{2,1},{4,3},{6,5},{... | collective-permute-start | bytes 1179656 | tf_op jit(solution)/shard_map/ppermute | solution.py:329
  56.3 7.2 %collective-permute-start.2 = (f32[3,2,128,128]{3,2,1,0:T(8,128)S(1)}, f32[3,2,128,128]{3,2,1,0:T(8,128)S(1)}, u32[]{:S(2)}, u32[]{:S(2)}) collective-permute-start(f32[3,2,128,128]{3,2,1,0:T(8,128)S(1)} %get-tuple-element.41), channel_id=1, source_target_pairs={{0,1},{1,0},{2,3},{3,2},{4,5},{5,4},{6,7},{7,6},{8,9},{9,8},{10,11... | collective-permute-start | bytes 1179656 | tf_op jit(solution)/shard_map/ppermute | solution.py:330
  71.6 9.9 %collective-permute-start.6 = (f32[3,2,2,128,128]{4,3,2,1,0:T(8,128)S(1)}, f32[3,2,2,128,128]{4,3,2,1,0:T(8,128)S(1)}, u32[]{:S(2)}, u32[]{:S(2)}) collective-permute-start(f32[3,2,2,128,128]{4,3,2,1,0:T(8,128)S(1)} %get-tuple-element.32), channel_id=1, source_target_pairs={{0,1},{1,0},{2,3},{3,2},{4,5},{5,4},{6,7},{7,6},{8,9},{9,8},{10,11... | collective-permute-start | bytes 2359304 | tf_op jit(solution)/shard_map/ppermute | solution.py:382
  73.5 8.0 %collective-permute-start.8 = (f32[2,2,128,128]{3,2,1,0:T(8,128)S(1)}, f32[2,2,128,128]{3,2,1,0:T(8,128)S(1)}, u32[]{:S(2)}, u32[]{:S(2)}) collective-permute-start(f32[2,2,128,128]{3,2,1,0:T(8,128)S(1)} %get-tuple-element.36), channel_id=1, source_target_pairs={{1,2},{3,4},{5,6},{7,8},{9,10},{11,12},{13,14},{2,1},{4,3},{6,5},{... | collective-permute-start | bytes 786440 | tf_op jit(solution)/shard_map/ppermute | solution.py:380
  75.9 16.1 %collective-permute-start.7 = (f32[2,2,2,128,128]{4,3,2,1,0:T(8,128)}, f32[2,2,2,128,128]{4,3,2,1,0:T(8,128)S(1)}, u32[]{:S(2)}, u32[]{:S(2)}) collective-permute-start(f32[2,2,2,128,128]{4,3,2,1,0:T(8,128)} %get-tuple-element.33), channel_id=1, source_target_pairs={{1,2},{3,4},{5,6},{7,8},{9,10},{11,12},{13,14},{2,1},{4,3},{6,5},{... | collective-permute-start | bytes 1572872 | tf_op jit(solution)/shard_map/ppermute | solution.py:381
  81.5 10.5 %collective-permute-start.9 = (f32[2,2,128,128]{3,2,1,0:T(8,128)S(1)}, f32[2,2,128,128]{3,2,1,0:T(8,128)S(1)}, u32[]{:S(2)}, u32[]{:S(2)}) collective-permute-start(f32[2,2,128,128]{3,2,1,0:T(8,128)S(1)} %fusion.4), channel_id=1, source_target_pairs={{32,0},{64,32},{96,64},{128,96},{160,128},{192,160},{224,192},{256... | collective-permute-start | bytes 786440 | tf_op jit(solution)/shard_map/ppermute | solution.py:384
  82.8 23.3 %all-to-all-start = ((f32[16,2,16,256]{3,2,1,0:T(8,128)}), f32[16,2,16,256]{3,2,1,0:T(8,128)S(1)}, u32[]{:S(2)}, u32[]{:S(2)}) async-start(f32[16,2,16,256]{3,2,1,0:T(8,128)} %get-tuple-element.37), calls=%async_computation | async-start | bytes 1048576 | tf_op jit(solution)/shard_map/all_to_all | solution.py:336
  92.1 33.6 %collective-permute-start.10 = (f32[2,2,128,128]{3,2,1,0:T(8,128)S(1)}, f32[2,2,128,128]{3,2,1,0:T(8,128)S(1)}, u32[]{:S(2)}, u32[]{:S(2)}) collective-permute-start(f32[2,2,128,128]{3,2,1,0:T(8,128)S(1)} %fusion.6), channel_id=1, source_target_pairs={{0,16},{16,0},{32,48},{48,32},{64,80},{80,64},{96,112},{112,96},{1... | collective-permute-start | bytes 786440 | tf_op jit(solution)/shard_map/ppermute | solution.py:387
  107.2 28.7 %all-to-all-start.1 = ((f32[32,2,128]{2,1,0:T(2,128)}), f32[32,2,128]{2,1,0:T(2,128)S(1)}, u32[]{:S(2)}, u32[]{:S(2)}) async-start(f32[32,2,128]{2,1,0:T(2,128)} %reshape.26), calls=%async_computation.1 | async-start | bytes 65536 | tf_op jit(solution)/shard_map/all_to_all | solution.py:344
